TPU v7x, 256 devices: a whole 4x4x8 slice. The times are simulated.
256 devices in a mesh: gx: 16 (over x, z_hi, core), gy: 16 (over z_lo, y).
Axes of the slice: x: 4, y: 4, z: 8 (z_hi: 2, z_lo: 4; z = z_hi * 4 + z_lo), core: 2. Of those that a mesh axis runs over, the one named last changes fastest.
Arguments:
- volume: bfloat16 [4, 256, 256, 128], P(None, 'gx', 'gy'), may hold values from -6 to 6
- w_first: bfloat16 [27, 128, 128], replicated, may hold values from -0.109375 to 0.109375
- w_down: bfloat16 [1024, 256], replicated, may hold values from -0.1875 to 0.1875
- w_middle: bfloat16 [27, 256, 256], replicated, may hold values from -0.078125 to 0.078125
- w_up: bfloat16 [256, 1024], replicated, may hold values from -0.375 to 0.375
- w_last: bfloat16 [27, 256, 128], replicated, may hold values from -0.078125 to 0.078125
- cotangent: bfloat16 [4, 256, 256, 128], P(None, 'gx', 'gy'), may hold values from -6 to 6
Outputs:
- logits: bfloat16 [4, 256, 256, 128], P(None, 'gx', 'gy')
- grad_volume: bfloat16 [4, 256, 256, 128], P(None, 'gx', 'gy')
- grad_last: float32 [27, 32768], P(None, ('gx', 'gy'))
All inputs are finite; a program needn't handle non-finite values.
Results may differ from a plain program's by a relative error of at most 0.008.
Values may be sent and summed in bfloat16 or wider, within the bound.
No kernel may reach another device: no remote copies, remote signals or barrier semaphores. Data moves between devices by JAX's collectives and lax.ppermute only.
A program may use at most 128 MiB of HBM per device.

v0:
```python
import math

import jax
import jax.numpy as jnp
from jax import lax
from jax.sharding import PartitionSpec as P


def with_halo(x, sides, width):
    for axis, dim in sides:
        peers, length = (lax.axis_size(axis), x.shape[dim])
        up = [(i, (i + 1) % peers) for i in range(peers - 1)]
        down = [(j, i) for i, j in up]
        last = lax.slice_in_dim(x, length - width, length, axis=dim)
        leading = lax.slice_in_dim(x, 0, width, axis=dim)
        before = lax.ppermute(last, axis, up)
        after = lax.ppermute(leading, axis, down)
        x = jnp.concatenate([before, x, after], axis=dim)
    return x


def fine_rims(field):
    return with_halo(field, (("gx", 1), ("gy", 2)), 1)


def coarse_rims(field):
    return with_halo(field, (("gx", 1), ("gy", 2)), 1)


def patch_matrix(extended):
    depth_here = extended.shape[0]
    rows_here = extended.shape[1] - 2
    cols_here = extended.shape[2] - 2
    padded = jnp.pad(extended, ((1, 1), (0, 0), (0, 0), (0, 0)))
    pieces = []
    for depth_off in range(3):
        for row_off in range(3):
            for col_off in range(3):
                pieces.append(
                    padded[
                        depth_off : depth_off + depth_here,
                        row_off : row_off + rows_here,
                        col_off : col_off + cols_here,
                    ]
                )
    stacked = jnp.concatenate(pieces, axis=-1)
    return stacked.reshape(depth_here * rows_here * cols_here, stacked.shape[-1])


def apply_taps(matrix, weight):
    return jnp.dot(matrix, weight.reshape(-1, weight.shape[2]), preferred_element_type=jnp.float32)


def flipped(weight):
    return jnp.transpose(weight[::-1], (0, 2, 1))


def to_blocks(field):
    extent = field.shape
    moved = field.reshape(extent[0] // 2, 2, extent[1] // 2, 2, extent[2] // 2, 2, extent[3])
    moved = moved.transpose(0, 2, 4, 1, 3, 5, 6)
    return moved.reshape(extent[0] // 2, extent[1] // 2, extent[2] // 2, 8 * extent[3])


def from_blocks(blocked, channels):
    extent = blocked.shape
    moved = blocked.reshape(extent[0], extent[1], extent[2], 2, 2, 2, channels)
    moved = moved.transpose(0, 3, 1, 4, 2, 5, 6)
    return moved.reshape(2 * extent[0], 2 * extent[1], 2 * extent[2], channels)


def silu_slope(pre_act):
    sigma = jax.nn.sigmoid(pre_act)
    return sigma * (1.0 + pre_act * (1.0 - sigma))


def on_device(volume, w_first, w_down, w_middle, w_up, w_last, cotangent):
    depth_here, rows_here, cols_here, width_one = volume.shape
    width_two = w_middle.shape[1]
    fine_dims = (depth_here, rows_here, cols_here)
    coarse_dims = (depth_here // 2, rows_here // 2, cols_here // 2)
    pre_first = apply_taps(patch_matrix(fine_rims(volume)), w_first).reshape(
        fine_dims + (width_one,)
    )
    skip_out = jax.nn.silu(pre_first).astype(jnp.bfloat16)
    pre_coarse = jnp.dot(
        to_blocks(skip_out).reshape(-1, 8 * width_one), w_down, preferred_element_type=jnp.float32
    )
    coarse = jax.nn.silu(pre_coarse).astype(jnp.bfloat16)
    pre_middle = apply_taps(
        patch_matrix(coarse_rims(coarse.reshape(coarse_dims + (width_two,)))), w_middle
    )
    middle = jax.nn.silu(pre_middle).astype(jnp.bfloat16)
    up_flat = jnp.dot(middle, w_up, preferred_element_type=jnp.float32)
    pre_up = from_blocks(up_flat.reshape(coarse_dims + (8 * width_one,)), width_one)
    upward = jax.nn.silu(pre_up).astype(jnp.bfloat16)
    joined_ext = with_halo(jnp.concatenate([skip_out, upward], axis=-1), (("gx", 1), ("gy", 2)), 1)
    joined_matrix = patch_matrix(joined_ext)
    logits = (
        apply_taps(joined_matrix, w_last).astype(jnp.bfloat16).reshape(fine_dims + (width_one,))
    )
    grad_term = lax.dot_general(
        joined_matrix,
        cotangent.reshape(-1, width_one),
        (((0,), (0,)), ((), ())),
        preferred_element_type=jnp.float32,
    )
    grad_term = grad_term.reshape(27, -1)
    count_gx = lax.axis_size("gx")
    count_gy = lax.axis_size("gy")
    grad_scale = 1.0 / math.sqrt(depth_here * rows_here * cols_here * count_gx * count_gy)
    summed = lax.psum_scatter(grad_term, ("gx", "gy"), scatter_dimension=1, tiled=True)
    grad_last = summed * grad_scale
    cot_ext = with_halo(cotangent, (("gx", 1), ("gy", 2)), 1)
    grad_joined = (
        apply_taps(patch_matrix(cot_ext), flipped(w_last))
        .astype(jnp.bfloat16)
        .reshape(fine_dims + (2 * width_one,))
    )
    grad_up = (grad_joined[..., width_one:].astype(jnp.float32) * silu_slope(pre_up)).astype(
        jnp.bfloat16
    )
    middle_back = jnp.dot(
        to_blocks(grad_up).reshape(-1, 8 * width_one), w_up.T, preferred_element_type=jnp.float32
    )
    grad_middle = (middle_back * silu_slope(pre_middle)).astype(jnp.bfloat16)
    coarse_back = apply_taps(
        patch_matrix(coarse_rims(grad_middle.reshape(coarse_dims + (width_two,)))),
        flipped(w_middle),
    )
    grad_coarse = (coarse_back * silu_slope(pre_coarse)).astype(jnp.bfloat16)
    down_flat = jnp.dot(grad_coarse, w_down.T, preferred_element_type=jnp.float32)
    grad_down = from_blocks(down_flat.reshape(coarse_dims + (8 * width_one,)), width_one)
    grad_first = (
        (grad_joined[..., :width_one].astype(jnp.float32) + grad_down) * silu_slope(pre_first)
    ).astype(jnp.bfloat16)
    grad_volume = (
        apply_taps(patch_matrix(fine_rims(grad_first)), flipped(w_first))
        .astype(jnp.bfloat16)
        .reshape(fine_dims + (width_one,))
    )
    return (logits, grad_volume, grad_last)


def solution(mesh):
    return jax.shard_map(
        on_device,
        mesh=mesh,
        in_specs=(P(None, "gx", "gy", None), P(), P(), P(), P(), P(), P(None, "gx", "gy", None)),
        out_specs=(P(None, "gx", "gy", None), P(None, "gx", "gy", None), P(None, ("gx", "gy"))),
        check_vma=False,
    )
```

profile of v0, /device:TPU:32, one launch (start us, length us, event | category | flops | bytes accessed | tf_op | source)
XLA Modules:
  0.0 1460.2 jit_solution(5151939340454270479)
XLA Ops:
  11.8 9.1 collective-permute-start
  26.3 2.9 collective-permute-done.13
  29.2 3.5 collective-permute-start.14
  32.7 4.5 collective-permute-start.15
  39.3 6.0 collective-permute-start.3
  55.5 7.2 collective-permute-start.4
  66.1 3.0 collective-permute-done.5
  71.0 6.2 collective-permute-start.7
  81.1 7.1 collective-permute-start.16
  90.8 5.7 copy.16
  96.6 4.1 rev.10
  102.7 6.0 collective-permute-start.19
  112.2 3.6 fusion.11
  117.5 4.2 collective-permute-start.20
  123.0 9.0 collective-permute-start.8
  133.4 3.2 collective-permute-start.22
  136.6 5.1 collective-permute-start.23
  143.8 6.0 collective-permute-start.11
  157.9 5.0 copy-done.11
  162.9 5.8 convolution_bitcast_fusion
  168.7 5.0 reshape.144
  193.0 5.7 convolution_convert_fusion.2
  198.8 4.5 convolution_convert_fusion.1
  203.3 1248.8 %reduce-scatter.2.cloned.1.call-done = f32[27,128]{1,0:T(8,128)} async-done(((f32[27,32768]{1,0:T(8,128)}), f32[27,128]{1,0:T(8,128)}) %reduce-scatter.2.cloned.1.call-update) | async-done | bytes 13840 | tf_op jit(solution)/shard_map/reduce_scatter | solution.py:112
  (275 shorter events, 73.3 us)
Async XLA Ops:
  7.2 1444.9 %reduce-scatter.2.cloned.1.call-start = ((), (), s32[]{:S(2)}) async-start(), calls=%async_computation.1 | async-start | bytes 4210688 | tf_op jit(solution)/shard_map/reduce_scatter | solution.py:112
  8.1 18.2 %collective-permute-start.12 = (bf16[4,1,16,128]{3,2,1,0:T(8,128)(2,1)S(1)}, bf16[4,1,16,128]{3,2,1,0:T(8,128)(2,1)S(1)}, u32[]{:S(2)}, u32[]{:S(2)}) collective-permute-start(bf16[4,1,16,128]{3,2,1,0:T(8,128)(2,1)S(1)} %get-tuple-element.58), channel_id=1, source_target_pairs={{0,16},{16,32},{32,48},{48,64},{64,80},{80,96},{96,112},{112,128},... | collective-permute-start | bytes 49160 | tf_op jit(solution)/shard_map/ppermute | solution.py:16
  10.5 26.7 %collective-permute-start.1 = (bf16[4,1,16,128]{3,2,1,0:T(8,128)(2,1)S(1)}, bf16[4,1,16,128]{3,2,1,0:T(8,128)(2,1)S(1)}, u32[]{:S(2)}, u32[]{:S(2)}) collective-permute-start(bf16[4,1,16,128]{3,2,1,0:T(8,128)(2,1)S(1)} %get-tuple-element.59), channel_id=1, source_target_pairs={{16,0},{32,16},{48,32},{64,48},{80,64},{96,80},{112,96},{128,112},... | collective-permute-start | bytes 49160 | tf_op jit(solution)/shard_map/ppermute | solution.py:17
  11.8 25.4 %collective-permute-start = (bf16[4,1,16,128]{3,2,1,0:T(8,128)(2,1)S(1)}, bf16[4,1,16,128]{3,2,1,0:T(8,128)(2,1)S(1)}, u32[]{:S(2)}, u32[]{:S(2)}) collective-permute-start(bf16[4,1,16,128]{3,2,1,0:T(8,128)(2,1)S(1)} %get-tuple-element.60), channel_id=1, source_target_pairs={{0,16},{16,32},{32,48},{48,64},{64,80},{80,96},{96,112},{112,128},... | collective-permute-start | bytes 49160 | tf_op jit(solution)/shard_map/ppermute | solution.py:16
  20.9 8.2 collective-permute-start.13
  29.2 16.1 %collective-permute-start.14 = (bf16[4,18,1,128]{3,2,1,0:T(2,128)(2,1)S(1)}, bf16[4,18,1,128]{3,2,1,0:T(2,128)(2,1)S(1)}, u32[]{:S(2)}, u32[]{:S(2)}) collective-permute-start(bf16[4,18,1,128]{3,2,1,0:T(2,128)(2,1)S(1)} %get-tuple-element.51), channel_id=1, source_target_pairs={{0,1},{1,2},{2,3},{3,4},{4,5},{5,6},{6,7},{7,8},{8,9},{9,10},{10,1... | collective-permute-start | bytes 55304 | tf_op jit(solution)/shard_map/ppermute | solution.py:16
  32.7 12.6 collective-permute-start.15
  37.4 11.4 collective-permute-start.2
  39.3 9.5 collective-permute-start.3
  55.5 10.6 collective-permute-start.4
  69.1 8.2 collective-permute-start.6
  71.0 7.5 collective-permute-start.7
  81.1 19.7 %collective-permute-start.16 = (bf16[2,1,8,256]{3,2,1,0:T(8,128)(2,1)S(1)}, bf16[2,1,8,256]{3,2,1,0:T(8,128)(2,1)S(1)}, u32[]{:S(2)}, u32[]{:S(2)}) collective-permute-start(bf16[2,1,8,256]{3,2,1,0:T(8,128)(2,1)S(1)} %get-tuple-element.83), channel_id=1, source_target_pairs={{0,16},{16,32},{32,48},{48,64},{64,80},{80,96},{96,112},{112,128},... | collective-permute-start | bytes 24584 | tf_op jit(solution)/shard_map/ppermute | solution.py:16
  88.2 12.6 collective-permute-start.17
  100.8 8.0 collective-permute-start.18
  102.7 7.5 collective-permute-start.19
  117.5 15.9 %collective-permute-start.20 = (bf16[4,1,16,128]{3,2,1,0:T(8,128)(2,1)S(1)}, bf16[4,1,16,128]{3,2,1,0:T(8,128)(2,1)S(1)}, u32[]{:S(2)}, u32[]{:S(2)}) collective-permute-start(bf16[4,1,16,128]{3,2,1,0:T(8,128)(2,1)S(1)} %get-tuple-element.55), channel_id=1, source_target_pairs={{0,16},{16,32},{32,48},{48,64},{64,80},{80,96},{96,112},{112,128},... | collective-permute-start | bytes 49160 | tf_op jit(solution)/shard_map/ppermute | solution.py:16
  121.7 11.7 collective-permute-start.21
  123.0 18.7 %collective-permute-start.8 = (bf16[4,1,16,256]{3,2,1,0:T(8,128)(2,1)S(1)}, bf16[4,1,16,256]{3,2,1,0:T(8,128)(2,1)S(1)}, u32[]{:S(2)}, u32[]{:S(2)}) collective-permute-start(bf16[4,1,16,256]{3,2,1,0:T(8,128)(2,1)S(1)} %get-tuple-element.9), channel_id=1, source_target_pairs={{0,16},{16,32},{32,48},{48,64},{64,80},{80,96},{96,112},{112,128},... | collective-permute-start | bytes 98312 | tf_op jit(solution)/shard_map/ppermute | solution.py:16
  132.0 9.7 collective-permute-start.9
  133.4 16.4 %collective-permute-start.22 = (bf16[4,18,1,128]{3,2,1,0:T(2,128)(2,1)S(1)}, bf16[4,18,1,128]{3,2,1,0:T(2,128)(2,1)S(1)}, u32[]{:S(2)}, u32[]{:S(2)}) collective-permute-start(bf16[4,18,1,128]{3,2,1,0:T(2,128)(2,1)S(1)} %get-tuple-element.49), channel_id=1, source_target_pairs={{0,1},{1,2},{2,3},{3,4},{4,5},{5,6},{6,7},{7,8},{8,9},{9,10},{10,1... | collective-permute-start | bytes 55304 | tf_op jit(solution)/shard_map/ppermute | solution.py:16
  136.6 13.2 collective-permute-start.23
  141.9 10.7 collective-permute-start.10
  143.8 8.8 collective-permute-start.11
  (14 other events, 1448.6 us)
Sparse Core Ops, SparseCore 0:
  173.8 1278.1 reduce-scatter.1
where the time goes:
time: 1470 us; the launch traced here: 1460 us
  waiting for transfers between devices  1260 us (86%)
  starting transfers between devices  94.3 us (6%)
  local copies, waits for them, and re-layouts  56.9 us (4%)
  matrix products  26 us (2%)
  between operations  15.7 us (1%)
    reduce_scatter x1, waiting for transfers between devices, on_device(): lax.psum_scatter(grad_term, ('gx', 'gy'), scatter_dimension=1, tiled=True)  1250 us
    ppermute x12, starting transfers between devices, with_halo(): before = lax.ppermute(last, axis, up)  52.6 us
    unnamed x170, local copies, waits for them, and re-layouts  42.3 us
    ppermute x12, starting transfers between devices, with_halo(): after = lax.ppermute(leading, axis, down)  41.6 us
  transfers between devices with their start and end apart: 25, of which 5 were waited for; matrix products, arithmetic and copies ran while one was open for 4% of the time, Pallas kernels for 0%

commit v1 on v0

v1 whole, which is shorter than its diff:
```python
import math

import jax
import jax.numpy as jnp
from jax import lax
from jax.sharding import PartitionSpec as P

AXES = ("gx", "gy")
BF = jnp.bfloat16
F32 = jnp.float32


def swap_pairs(axis, offset):
    count = lax.axis_size(axis)
    pairs = []
    for low in range(offset, count - 1, 2):
        pairs += [(low, low + 1), (low + 1, low)]
    return pairs


def exchange(fields, widths, axis, dim):
    even = lax.rem(lax.axis_index(axis), 2) == 0
    firsts, lasts = [], []
    for field, width in zip(fields, widths):
        length = field.shape[dim]
        firsts.append(lax.slice_in_dim(field, 0, width, axis=dim))
        lasts.append(lax.slice_in_dim(field, length - width, length, axis=dim))
    lanes = 128

    def flat(strips):
        return jnp.concatenate([s.reshape(-1, lanes) for s in strips], axis=0)

    head, tail = flat(firsts), flat(lasts)
    far = lax.ppermute(jnp.where(even, head, tail), axis, swap_pairs(axis, 1))
    near = lax.ppermute(jnp.where(even, tail, head), axis, swap_pairs(axis, 0))
    before = jnp.where(even, far, near)
    after = jnp.where(even, near, far)
    grown, start = [], 0
    for field, strip in zip(fields, firsts):
        rows = strip.size // lanes
        grown.append(
            jnp.concatenate(
                [
                    before[start : start + rows].reshape(strip.shape),
                    field,
                    after[start : start + rows].reshape(strip.shape),
                ],
                axis=dim,
            )
        )
        start += rows
    return grown


def with_halos(fields, widths):
    fields = exchange(fields, widths, "gx", 1)
    return exchange(fields, widths, "gy", 2)


def inside(halo, extent):
    rows, cols = extent
    gx, gy = lax.axis_index("gx"), lax.axis_index("gy")
    row = gx * rows - halo + jnp.arange(rows + 2 * halo)
    col = gy * cols - halo + jnp.arange(cols + 2 * halo)
    row_in = (row >= 0) & (row < rows * lax.axis_size("gx"))
    col_in = (col >= 0) & (col < cols * lax.axis_size("gy"))
    return (row_in[:, None] & col_in[None, :])[None, :, :, None]


def patches(extended, mirrored=False):
    depth, rows, cols = extended.shape[0], extended.shape[1] - 2, extended.shape[2] - 2
    padded = jnp.pad(extended, ((1, 1), (0, 0), (0, 0), (0, 0)))
    pieces = []
    for z in range(3):
        for y in range(3):
            for x in range(3):
                pieces.append(padded[z : z + depth, y : y + rows, x : x + cols])
    if mirrored:
        pieces = pieces[::-1]
    stacked = jnp.concatenate(pieces, axis=-1)
    return stacked.reshape(depth * rows * cols, stacked.shape[-1])


def dot(a, b):
    return jnp.dot(a, b, preferred_element_type=F32)


def flat_weight(weight):
    return weight.reshape(-1, weight.shape[2])


def turned(weight):
    return flat_weight(jnp.transpose(weight, (0, 2, 1)))


def to_blocks(field):
    z, y, x, c = field.shape
    moved = field.reshape(z // 2, 2, y // 2, 2, x // 2, 2, c).transpose(0, 2, 4, 1, 3, 5, 6)
    return moved.reshape(z // 2 * (y // 2) * (x // 2), 8 * c)


def from_blocks(blocked, dims, channels):
    z, y, x = dims
    moved = blocked.reshape(z, y, x, 2, 2, 2, channels).transpose(0, 3, 1, 4, 2, 5, 6)
    return moved.reshape(2 * z, 2 * y, 2 * x, channels)


def silu(a):
    return a * jax.nn.sigmoid(a)


def slope(a):
    s = jax.nn.sigmoid(a)
    return s * (1.0 + a * (1.0 - s))


def crop(field, by):
    return field[:, by:-by, by:-by]


PARTS = (4, 2, 2, 4, 4)


def groups_over(dims):
    table = {}
    for rank in range(math.prod(PARTS)):
        place, rest = [], rank
        for size in PARTS[::-1]:
            place.insert(0, rest % size)
            rest //= size
        table.setdefault(tuple(p for d, p in enumerate(place) if d not in dims), []).append(rank)
    return list(table.values())


def core_swap(array):
    count = lax.axis_size("gx")
    return lax.ppermute(array, "gx", [(i, i ^ 1) for i in range(count)])


def reduce_entries(term):
    width = term.shape[1]
    core = lax.rem(lax.axis_index("gx"), 2)
    split = term.astype(BF).reshape(8, 2, 16, width)
    theirs = lax.dynamic_index_in_dim(split, 1 - core, 1, keepdims=False)
    mine = lax.dynamic_index_in_dim(split, core, 1, keepdims=False)
    got = core_swap(theirs)
    pair = mine.astype(F32) + got.astype(F32)
    pair = pair.reshape(4, 2, 4, 4, width).transpose(0, 3, 1, 2, 4).astype(BF)
    pair = pair.reshape(16, 8 * width)
    pair = lax.all_to_all(pair, AXES, 0, 0, axis_index_groups=groups_over((0, 4)), tiled=True)
    plane = pair.astype(F32).sum(0).reshape(8, width)
    plane = lax.all_to_all(plane, AXES, 0, 0, axis_index_groups=groups_over((1, 3)), tiled=True)
    return plane.sum(0)


def on_device(volume, w_first, w_down, w_middle, w_up, w_last, cotangent):
    depth, rows, cols, one = volume.shape
    two = w_middle.shape[1]
    coarse_dims = (depth // 2, rows // 2, cols // 2)

    volume_ext, cot_ext = with_halos([volume, cotangent], (3, 1))

    pre_first = dot(patches(volume_ext), flat_weight(w_first))
    pre_first = pre_first.reshape(depth, rows + 4, cols + 4, one)
    skip = jnp.where(inside(2, (rows, cols)), silu(pre_first), 0.0).astype(BF)
    pre_coarse = dot(to_blocks(skip), w_down)
    coarse = silu(pre_coarse).astype(BF)
    coarse = coarse.reshape(coarse_dims[0], coarse_dims[1] + 2, coarse_dims[2] + 2, two)
    pre_middle = dot(patches(coarse), flat_weight(w_middle))
    middle = silu(pre_middle).astype(BF)
    pre_up = from_blocks(dot(middle, w_up), coarse_dims, one)
    upward = silu(pre_up).astype(BF)

    joined = jnp.concatenate([crop(skip, 2), upward], axis=-1)
    cot_patches = patches(cot_ext, mirrored=True)
    term = lax.dot_general(
        joined.reshape(-1, 2 * one),
        cot_patches,
        (((0,), (0,)), ((), ())),
        preferred_element_type=F32,
    )

    grad_joined = dot(cot_patches, turned(w_last)).astype(BF)
    grad_joined = grad_joined.reshape(depth, rows, cols, 2 * one)
    grad_up = (grad_joined[..., one:].astype(F32) * slope(pre_up)).astype(BF)
    grad_middle = (dot(to_blocks(grad_up), w_up.T) * slope(pre_middle)).astype(BF)
    grad_middle = grad_middle.reshape(coarse_dims + (two,))

    fine = jnp.concatenate([upward, grad_joined[..., :one]], axis=-1)
    fine_ext, middle_ext = with_halos([fine, grad_middle], (1, 2))

    total = reduce_entries(term)
    scale = 1.0 / math.sqrt(
        depth * rows * cols * lax.axis_size("gx") * lax.axis_size("gy")
    )
    grad_last = (total * scale).reshape(27, one)

    joined_ext = jnp.concatenate([crop(skip, 1), fine_ext[..., :one]], axis=-1)
    logits = dot(patches(joined_ext), flat_weight(w_last)).astype(BF)
    logits = logits.reshape(depth, rows, cols, one)

    coarse_back = dot(patches(middle_ext, mirrored=True), turned(w_middle))
    grad_coarse = (coarse_back * slope(pre_coarse)).astype(BF)
    around = (coarse_dims[0], coarse_dims[1] + 2, coarse_dims[2] + 2)
    grad_down = crop(from_blocks(dot(grad_coarse, w_down.T), around, one), 1)
    grad_first = (fine_ext[..., one:].astype(F32) + grad_down) * slope(crop(pre_first, 1))
    grad_first = jnp.where(inside(1, (rows, cols)), grad_first, 0.0).astype(BF)
    grad_volume = dot(patches(grad_first, mirrored=True), turned(w_first)).astype(BF)
    grad_volume = grad_volume.reshape(depth, rows, cols, one)
    return logits, grad_volume, grad_last


def solution(mesh):
    field = P(None, "gx", "gy", None)
    return jax.shard_map(
        on_device,
        mesh=mesh,
        in_specs=(field, P(), P(), P(), P(), P(), field),
        out_specs=(field, field, P(None, AXES)),
        check_vma=False,
    )
```

time: 1470 us -> 193 us (0.13)
  the two profiles are of different devices: /device:TPU:32 before, /device:TPU:8 now
where the time goes in v1:
time: 193 us; the launch traced here: 189 us
  local copies, waits for them, and re-layouts  75.4 us (39%)
  matrix products  39.6 us (21%)
  starting transfers between devices  38.6 us (20%)
  other arithmetic  22.5 us (12%)
  waiting for transfers between devices  10.2 us (5%)
  between operations  2.76 us (1%)
    unnamed x180, local copies, waits for them, and re-layouts  51.6 us
    dot_general x9, matrix products, dot(): return jnp.dot(a, b, preferred_element_type=F32)  34.5 us
    ppermute x4, starting transfers between devices, exchange(): near = lax.ppermute(jnp.where(even, tail, head), axis, swap_pairs(axis, 0))  16.8 us
    all_to_all x1, starting transfers between devices, reduce_entries(): lax.all_to_all(pair, AXES, 0, 0, axis_index_groups=groups_over((0, 4)), t...  9.78 us
    ppermute x4, starting transfers between devices, exchange(): far = lax.ppermute(jnp.where(even, head, tail), axis, swap_pairs(axis, 1))  8.64 us
    all_to_all x1, other arithmetic, reduce_entries(): lax.all_to_all(pair, AXES, 0, 0, axis_index_groups=groups_over((0, 4)), t...  6 us
    reshape x1, local copies, waits for them, and re-layouts, patches(): return stacked.reshape(depth * rows * cols, stacked.shape[-1])  5.85 us
    dot_general x1, matrix products, on_device(): lax.dot_general(joined.reshape(-1, 2 * one), cot_patches, (((0,), (0,)),...  5.1 us
  transfers between devices with their start and end apart: 11, of which 4 were waited for; matrix products, arithmetic and copies ran while one was open for 44% of the time, Pallas kernels for 0%

profile of v1, /device:TPU:8, one launch (start us, length us, event | category | flops | bytes accessed | tf_op | source)
XLA Modules:
  0.0 189.1 jit_solution(13353196604090652657)
XLA Ops:
  3.1 8.6 %collective-permute-start.1 = (bf16[256,128]{1,0:T(8,128)(2,1)S(1)}, bf16[256,128]{1,0:T(8,128)(2,1)S(1)}, u32[]{:S(2)}, u32[]{:S(2)}) collective-permute-start(bf16[256,128]{1,0:T(8,128)(2,1)S(1)} %get-tuple-element.26), channel_id=1, source_target_pairs={{0,16},{16,0},{32,48},{48,32},{64,80},{80,64},{96,112},{112,96},{1... | collective-permute-start | bytes 196616 | tf_op jit(solution)/shard_map/ppermute | solution.py:35
  15.1 3.5 %collective-permute-start.2 = (bf16[336,128]{1,0:T(8,128)(2,1)S(1)}, bf16[336,128]{1,0:T(8,128)(2,1)S(1)}, u32[]{:S(2)}, u32[]{:S(2)}) collective-permute-start(bf16[336,128]{1,0:T(8,128)(2,1)S(1)} %get-tuple-element.21), channel_id=1, source_target_pairs={{1,2},{2,1},{3,4},{4,3},{5,6},{6,5},{7,8},{8,7},{9,10},{10,9},{11,... | collective-permute-start | bytes 258056 | tf_op jit(solution)/shard_map/ppermute | solution.py:34
  18.8 3.9 %copy.87 = bf16[27,256,128]{1,2,0:T(8,128)(2,1)} copy(bf16[27,256,128]{2,1,0:T(8,128)(2,1)} %param.12) | data formatting | bytes 3538944 | tf_op args[5]
  22.7 5.7 %copy.91 = bf16[27,256,256]{1,2,0:T(8,128)(2,1)} copy(bf16[27,256,256]{2,1,0:T(8,128)(2,1)} %param.10) | data formatting | bytes 7077888 | tf_op args[3]
  28.4 2.1 %copy.94 = bf16[27,128,128]{1,2,0:T(8,128)(2,1)} copy(bf16[27,128,128]{2,1,0:T(8,128)(2,1)S(1)} %copy-done.6) | data formatting | bytes 1769472 | tf_op args[1]
  36.7 5.0 %select_convert_fusion = (bf16[4,20,20,128]{3,2,1,0:T(8,128)(2,1)S(1)}, f32[4,20,20,128]{3,2,1,0:T(8,128)}) fusion(pred[20,20]{1,0:T(8,128)(4,1)S(1)} %broadcast_and_fusion.1, bf16[4,20,20,3456]{3,2,1,0:T(8,128)(2,1)S(1)} %fusion.70, bf16[3456,128,1,1]{1,0,3,2:T(8,128)(2,1)S(1)} %bitcast.105), kind=kOutput, calls=%fused_computation.125 | convolution fusion | flops 1416806400 | bytes 13173136 | tf_op jit(solution)/shard_map/dot_general | solution.py:85
  46.8 2.8 %fusion.86 = f32[128,256]{1,0:T(8,128)S(1)} fusion(bf16[128,6912]{1,0:T(8,128)(2,1)S(1)} %bitcast.100, bf16[6912,256]{1,0:T(8,128)(2,1)} %bitcast.92), kind=kOutput, calls=%fused_computation.395 | convolution fusion | flops 452984832 | bytes 5439488 | tf_op jit(solution)/shard_map/dot_general | solution.py:85
  53.9 2.1 %convolution_convert_fusion = bf16[1024,256]{1,0:T(8,128)(2,1)S(1)} fusion(bf16[1024,3456]{1,0:T(8,128)(2,1)S(1)} %bitcast.93, bf16[3456,256]{1,0:T(8,128)(2,1)S(1)} %bitcast.102), kind=kOutput, calls=%fused_computation.63 | convolution fusion | flops 1812201472 | bytes 9371648 | tf_op jit(solution)/shard_map/dot_general | solution.py:85
  58.0 7.9 %collective-permute-start.5 = (bf16[192,128]{1,0:T(8,128)(2,1)S(1)}, bf16[192,128]{1,0:T(8,128)(2,1)S(1)}, u32[]{:S(2)}, u32[]{:S(2)}) collective-permute-start(bf16[192,128]{1,0:T(8,128)(2,1)S(1)} %get-tuple-element.38), channel_id=1, source_target_pairs={{0,16},{16,0},{32,48},{48,32},{64,80},{80,64},{96,112},{112,96},{1... | collective-permute-start | bytes 147464 | tf_op jit(solution)/shard_map/ppermute | solution.py:35
  66.0 5.1 %fusion = bf16[256,3456]{1,0:T(8,128)(2,1)S(1)} fusion(bf16[4,16,16,3456]{3,2,1,0:T(8,128)(2,1)} %copy-done.2, bf16[4,16,16,128]{3,2,1,0:T(8,128)(2,1)S(1)} %get-tuple-element.10, bf16[4,16,16,128]{3,2,1,0:T(8,128)(2,1)S(1)} %slice.979), kind=kOutput, calls=%fused_computation.1 | convolution fusion | flops 1813872640 | bytes 9371648 | tf_op jit(solution)/shard_map/dot_general | solution.py:176
  71.9 3.8 %collective-permute-start.6 = (bf16[240,128]{1,0:T(8,128)(2,1)S(1)}, bf16[240,128]{1,0:T(8,128)(2,1)S(1)}, u32[]{:S(2)}, u32[]{:S(2)}) collective-permute-start(bf16[240,128]{1,0:T(8,128)(2,1)S(1)} %get-tuple-element.29), channel_id=1, source_target_pairs={{1,2},{2,1},{3,4},{4,3},{5,6},{6,5},{7,8},{8,7},{9,10},{10,9},{11,... | collective-permute-start | bytes 184328 | tf_op jit(solution)/shard_map/ppermute | solution.py:34
  102.6 5.8 %reshape.338 = bf16[200,6912]{1,0:T(8,128)(2,1)} reshape(bf16[2,10,10,6912]{3,2,1,0:T(8,128)(2,1)} %constant_dynamic-update-slice_fusion.66) | data formatting | bytes 5529600 | tf_op jit(solution)/shard_map/reshape | solution.py:81
  108.5 5.1 %fusion.4 = f32[200,1024]{1,0:T(8,128)} fusion(bf16[1024,256]{1,0:T(8,128)(2,1)S(1)} %copy-done, bf16[200,6912]{1,0:T(8,128)(2,1)} %reshape.338, bf16[6912,256]{1,0:T(8,128)(2,1)} %bitcast.91, f32[200,256]{1,0:T(8,128)} %get-tuple-element.44), kind=kOutput, calls=%fused_computation.104 | convolution fusion | flops 813107200 | bytes 7852032 | tf_op jit(solution)/shard_map/dot_general | solution.py:85
  113.6 2.8 %reshape.340 = f32[2,10,10,2,2,2,128]{6,5,4,3,2,1,0:T(2,128)} reshape(f32[200,1024]{1,0:T(8,128)} %fusion.4) | data formatting | bytes 1638400 | tf_op jit(solution)/shard_map/reshape | solution.py:104
  130.4 4.3 %copy-done.10 = bf16[4,16,16,6912]{3,2,1,0:T(8,128)(2,1)} copy-done((bf16[4,16,16,6912]{3,2,1,0:T(8,128)(2,1)}, bf16[4,16,16,6912]{3,2,1,0:T(8,128)(2,1)S(1)}, u32[]{:S(2)}) %copy-start.10) | copy-done | bytes 14155800
  134.7 2.3 %fusion.1 = bf16[8,16,3456]{2,1,0:T(8,128)(2,1)} fusion(bf16[8,16,3456]{2,1,0:T(8,128)(2,1)} %collective-permute-done.8, bf16[8,2,16,3456]{3,2,1,0:T(8,128)(2,1)S(1)} %bitcast.95, s32[]{:T(128)S(6)} %select_n.117), kind=kLoop, calls=%fused_computation.42 | loop fusion | flops 1769472 | bytes 2654212 | tf_op jit(solution)/shard_map/convert_element_type | solution.py:148
  140.4 6.0 %reduce.10 = bf16[16,27648]{1,0:T(8,128)(2,1)S(1)} reduce(bf16[16,1,27648]{2,1,0:T(2,128)(2,1)S(1)} %all_to_all.16, bf16[]{:T(256)} %broadcast.225), dimensions={1}, to_apply=%all_to_all.16.reduce_sub_computation | reduce | bytes 1769474 | tf_op jit(solution)/shard_map/all_to_all | solution.py:150
  148.0 9.8 %all-to-all-start = ((bf16[16,2,13824]{2,1,0:T(2,128)(2,1)}), bf16[16,2,13824]{2,1,0:T(2,128)(2,1)S(1)}, u32[]{:S(2)}, u32[]{:S(2)}) async-start(bf16[16,2,13824]{2,1,0:T(2,128)(2,1)} %reshape.357), calls=%async_computation | async-start | bytes 1769472 | tf_op jit(solution)/shard_map/all_to_all | solution.py:150
  157.8 10.0 %convolution_convert_fusion.1 = bf16[1024,128]{1,0:T(8,128)(2,1)} fusion(bf16[1024,6912]{1,0:T(8,128)(2,1)} %bitcast.130, bf16[6912,128]{1,0:T(8,128)(2,1)} %bitcast.101), kind=kOutput, calls=%fused_computation.100 | convolution fusion | flops 1812070400 | bytes 16187392 | tf_op jit(solution)/shard_map/dot_general | solution.py:85
  167.8 4.6 %all-to-all-done = bf16[16,2,13824]{2,1,0:T(2,128)(2,1)S(1)} async-done(((bf16[16,2,13824]{2,1,0:T(2,128)(2,1)}), bf16[16,2,13824]{2,1,0:T(2,128)(2,1)S(1)}, u32[]{:S(2)}, u32[]{:S(2)}) %all-to-all-start) | async-done | bytes 884768 | tf_op jit(solution)/shard_map/all_to_all | solution.py:150
  173.1 2.7 %convert_reduce_fusion = f32[27648]{0:T(1024)} fusion(bf16[16,1,27648]{2,1,0:T(2,128)(2,1)S(1)} %reshape.358), kind=kLoop, calls=%fused_computation.43 | loop fusion | flops 857088 | bytes 995328 | tf_op jit(solution)/shard_map/reduce_sum | solution.py:151
  175.8 3.4 %all-to-all-start.1 = ((f32[8,1,3456]{2,1,0:T(1,128)}), f32[8,1,3456]{2,1,0:T(1,128)S(1)}, u32[]{:S(2)}, u32[]{:S(2)}) async-start(f32[8,1,3456]{2,1,0:T(1,128)} %bitcast.44), calls=%async_computation.1 | async-start | bytes 221184 | tf_op jit(solution)/shard_map/all_to_all | solution.py:152
  179.2 5.9 %convolution_convert_fusion.2 = bf16[1024,128]{1,0:T(8,128)(2,1)} fusion(bf16[1024,3456]{1,0:T(8,128)(2,1)} %bitcast.131, bf16[3456,128]{1,0:T(8,128)(2,1)} %bitcast.106), kind=kOutput, calls=%fused_computation.101 | convolution fusion | flops 906100736 | bytes 8224768 | tf_op jit(solution)/shard_map/dot_general | solution.py:85
  185.0 2.9 %all-to-all-done.1 = f32[8,1,3456]{2,1,0:T(1,128)S(1)} async-done(((f32[8,1,3456]{2,1,0:T(1,128)}), f32[8,1,3456]{2,1,0:T(1,128)S(1)}, u32[]{:S(2)}, u32[]{:S(2)}) %all-to-all-start.1) | async-done | bytes 110624 | tf_op jit(solution)/shard_map/all_to_all | solution.py:152
  (303 shorter events, 70.2 us)
Async XLA Ops:
  0.6 43.5 %copy-start = (bf16[1024,256]{1,0:T(8,128)(2,1)S(1)}, bf16[1024,256]{1,0:T(8,128)(2,1)}, u32[]{:S(2)}) copy-start(bf16[1024,256]{1,0:T(8,128)(2,1)} %param.9) | copy-start | bytes 1572868
  0.6 27.8 %copy-start.6 = (bf16[27,128,128]{2,1,0:T(8,128)(2,1)S(1)}, bf16[27,128,128]{2,1,0:T(8,128)(2,1)}, u32[]{:S(2)}) copy-start(bf16[27,128,128]{2,1,0:T(8,128)(2,1)} %param.8) | copy-start | bytes 2654212
  2.4 9.4 %collective-permute-start = (bf16[256,128]{1,0:T(8,128)(2,1)S(1)}, bf16[256,128]{1,0:T(8,128)(2,1)S(1)}, u32[]{:S(2)}, u32[]{:S(2)}) collective-permute-start(bf16[256,128]{1,0:T(8,128)(2,1)S(1)} %get-tuple-element.25), channel_id=1, source_target_pairs={{16,32},{32,16},{48,64},{64,48},{80,96},{96,80},{112,128},{128,112... | collective-permute-start | bytes 196616 | tf_op jit(solution)/shard_map/ppermute | solution.py:34
  3.1 9.5 %collective-permute-start.1 = (bf16[256,128]{1,0:T(8,128)(2,1)S(1)}, bf16[256,128]{1,0:T(8,128)(2,1)S(1)}, u32[]{:S(2)}, u32[]{:S(2)}) collective-permute-start(bf16[256,128]{1,0:T(8,128)(2,1)S(1)} %get-tuple-element.26), channel_id=1, source_target_pairs={{0,16},{16,0},{32,48},{48,32},{64,80},{80,64},{96,112},{112,96},{1... | collective-permute-start | bytes 196616 | tf_op jit(solution)/shard_map/ppermute | solution.py:35
  14.9 15.7 %copy-start.1 = (bf16[4,16,16,128]{3,2,1,0:T(8,128)(2,1)S(1)}, bf16[4,16,16,128]{3,2,1,0:T(8,128)(2,1)}, u32[]{:S(2)}) copy-start(bf16[4,16,16,128]{3,2,1,0:T(8,128)(2,1)} %param.13) | copy-start | bytes 786436
  15.1 15.4 %collective-permute-start.2 = (bf16[336,128]{1,0:T(8,128)(2,1)S(1)}, bf16[336,128]{1,0:T(8,128)(2,1)S(1)}, u32[]{:S(2)}, u32[]{:S(2)}) collective-permute-start(bf16[336,128]{1,0:T(8,128)(2,1)S(1)} %get-tuple-element.21), channel_id=1, source_target_pairs={{1,2},{2,1},{3,4},{4,3},{5,6},{6,5},{7,8},{8,7},{9,10},{10,9},{11,... | collective-permute-start | bytes 258056 | tf_op jit(solution)/shard_map/ppermute | solution.py:34
  18.6 11.9 %collective-permute-start.3 = (bf16[336,128]{1,0:T(8,128)(2,1)S(1)}, bf16[336,128]{1,0:T(8,128)(2,1)S(1)}, u32[]{:S(2)}, u32[]{:S(2)}) collective-permute-start(bf16[336,128]{1,0:T(8,128)(2,1)S(1)} %get-tuple-element.22), channel_id=1, source_target_pairs={{0,1},{1,0},{2,3},{3,2},{4,5},{5,4},{6,7},{7,6},{8,9},{9,8},{10,11... | collective-permute-start | bytes 258056 | tf_op jit(solution)/shard_map/ppermute | solution.py:35
  18.8 12.6 %copy-start.5 = (bf16[4,16,16,128]{3,2,1,0:T(8,128)(2,1)S(1)}, bf16[4,16,16,128]{3,2,1,0:T(8,128)(2,1)}, u32[]{:S(2)}) copy-start(bf16[4,16,16,128]{3,2,1,0:T(8,128)(2,1)} %param.7) | copy-start | bytes 786436
  34.0 2.7 %copy-start.7 = (bf16[27,128,128]{2,1,0:T(8,128)(2,1)S(1)}, bf16[27,128,128]{2,1,0:T(8,128)(2,1)}, u32[]{:S(2)}) copy-start(bf16[27,128,128]{2,1,0:T(8,128)(2,1)} %param.8) | copy-start | bytes 2654212
  41.7 0.8 copy-start.3
  51.2 2.8 %copy-start.4 = (bf16[27,256,128]{1,2,0:T(8,128)(2,1)S(1)}, bf16[27,256,128]{1,2,0:T(8,128)(2,1)}, u32[]{:S(2)}) copy-start(bf16[27,256,128]{1,2,0:T(8,128)(2,1)} %copy.87) | copy-start | bytes 5308420
  53.9 2.9 %copy-start.2 = (bf16[4,16,16,3456]{3,2,1,0:T(8,128)(2,1)}, bf16[4,16,16,3456]{3,2,1,0:T(8,128)(2,1)S(1)}, u32[]{:S(2)}) copy-start(bf16[4,16,16,3456]{3,2,1,0:T(8,128)(2,1)S(1)} %constant_dynamic-update-slice_fusion.31) | copy-start | bytes 21233668
  53.9 2.9 %copy-start.9 = (bf16[256,1024]{1,0:T(8,128)(2,1)S(1)}, bf16[256,1024]{1,0:T(8,128)(2,1)}, u32[]{:S(2)}) copy-start(bf16[256,1024]{1,0:T(8,128)(2,1)} %param.11) | copy-start | bytes 1572868
  57.2 18.7 %copy-start.8 = (bf16[128,256]{1,0:T(8,128)(2,1)}, bf16[128,256]{1,0:T(8,128)(2,1)S(1)}, u32[]{:S(2)}) copy-start(bf16[128,256]{1,0:T(8,128)(2,1)S(1)} %fusion.5) | copy-start | bytes 196612
  57.4 13.7 %collective-permute-start.4 = (bf16[192,128]{1,0:T(8,128)(2,1)S(1)}, bf16[192,128]{1,0:T(8,128)(2,1)S(1)}, u32[]{:S(2)}, u32[]{:S(2)}) collective-permute-start(bf16[192,128]{1,0:T(8,128)(2,1)S(1)} %get-tuple-element.37), channel_id=1, source_target_pairs={{16,32},{32,16},{48,64},{64,48},{80,96},{96,80},{112,128},{128,112... | collective-permute-start | bytes 147464 | tf_op jit(solution)/shard_map/ppermute | solution.py:34
  58.0 13.1 %collective-permute-start.5 = (bf16[192,128]{1,0:T(8,128)(2,1)S(1)}, bf16[192,128]{1,0:T(8,128)(2,1)S(1)}, u32[]{:S(2)}, u32[]{:S(2)}) collective-permute-start(bf16[192,128]{1,0:T(8,128)(2,1)S(1)} %get-tuple-element.38), channel_id=1, source_target_pairs={{0,16},{16,0},{32,48},{48,32},{64,80},{80,64},{96,112},{112,96},{1... | collective-permute-start | bytes 147464 | tf_op jit(solution)/shard_map/ppermute | solution.py:35
  71.9 6.2 %collective-permute-start.6 = (bf16[240,128]{1,0:T(8,128)(2,1)S(1)}, bf16[240,128]{1,0:T(8,128)(2,1)S(1)}, u32[]{:S(2)}, u32[]{:S(2)}) collective-permute-start(bf16[240,128]{1,0:T(8,128)(2,1)S(1)} %get-tuple-element.29), channel_id=1, source_target_pairs={{1,2},{2,1},{3,4},{4,3},{5,6},{6,5},{7,8},{8,7},{9,10},{10,9},{11,... | collective-permute-start | bytes 184328 | tf_op jit(solution)/shard_map/ppermute | solution.py:34
  75.8 4.3 %collective-permute-start.7 = (bf16[240,128]{1,0:T(8,128)(2,1)S(1)}, bf16[240,128]{1,0:T(8,128)(2,1)S(1)}, u32[]{:S(2)}, u32[]{:S(2)}) collective-permute-start(bf16[240,128]{1,0:T(8,128)(2,1)S(1)} %get-tuple-element.30), channel_id=1, source_target_pairs={{0,1},{1,0},{2,3},{3,2},{4,5},{5,4},{6,7},{7,6},{8,9},{9,8},{10,11... | collective-permute-start | bytes 184328 | tf_op jit(solution)/shard_map/ppermute | solution.py:35
  78.0 50.5 %collective-permute-start.8 = (bf16[8,16,3456]{2,1,0:T(8,128)(2,1)}, bf16[8,16,3456]{2,1,0:T(8,128)(2,1)}, u32[]{:S(2)}, u32[]{:S(2)}) collective-permute-start(bf16[8,16,3456]{2,1,0:T(8,128)(2,1)} %dynamic-slice_bitcast_fusion), channel_id=1, source_target_pairs={{0,16},{16,0},{32,48},{48,32},{64,80},{80,64},{96,112},{112,96},{1... | collective-permute-start | bytes 2654216 | tf_op jit(solution)/shard_map/ppermute | solution.py:137
  127.6 2.8 %copy-start.11 = (bf16[4,16,16,3456]{3,2,1,0:T(8,128)(2,1)}, bf16[4,16,16,3456]{3,2,1,0:T(8,128)(2,1)S(1)}, u32[]{:S(2)}) copy-start(bf16[4,16,16,3456]{3,2,1,0:T(8,128)(2,1)S(1)} %constant_dynamic-update-slice_fusion.93) | copy-start | bytes 21233668
  128.5 6.2 %copy-start.10 = (bf16[4,16,16,6912]{3,2,1,0:T(8,128)(2,1)}, bf16[4,16,16,6912]{3,2,1,0:T(8,128)(2,1)S(1)}, u32[]{:S(2)}) copy-start(bf16[4,16,16,6912]{3,2,1,0:T(8,128)(2,1)S(1)} %fusion.49) | copy-start | bytes 42467332
  148.0 24.4 %all-to-all-start = ((bf16[16,2,13824]{2,1,0:T(2,128)(2,1)}), bf16[16,2,13824]{2,1,0:T(2,128)(2,1)S(1)}, u32[]{:S(2)}, u32[]{:S(2)}) async-start(bf16[16,2,13824]{2,1,0:T(2,128)(2,1)} %reshape.357), calls=%async_computation | async-start | bytes 1769472 | tf_op jit(solution)/shard_map/all_to_all | solution.py:150
  175.8 12.2 %all-to-all-start.1 = ((f32[8,1,3456]{2,1,0:T(1,128)}), f32[8,1,3456]{2,1,0:T(1,128)S(1)}, u32[]{:S(2)}, u32[]{:S(2)}) async-start(f32[8,1,3456]{2,1,0:T(1,128)} %bitcast.44), calls=%async_computation.1 | async-start | bytes 221184 | tf_op jit(solution)/shard_map/all_to_all | solution.py:152

commit v2 on v1

v2 whole, which is shorter than its diff:
```python
import math

import jax
import jax.numpy as jnp
from jax import lax
from jax.experimental import pallas as pl
from jax.experimental.pallas import tpu as pltpu
from jax.sharding import PartitionSpec as P

AXES = ("gx", "gy")
BF = jnp.bfloat16
F32 = jnp.float32


def swap_pairs(axis, offset):
    count = lax.axis_size(axis)
    pairs = []
    for low in range(offset, count - 1, 2):
        pairs += [(low, low + 1), (low + 1, low)]
    return pairs


def exchange(fields, widths, axis, dim):
    even = lax.rem(lax.axis_index(axis), 2) == 0
    firsts, lasts = [], []
    for field, width in zip(fields, widths):
        length = field.shape[dim]
        firsts.append(lax.slice_in_dim(field, 0, width, axis=dim))
        lasts.append(lax.slice_in_dim(field, length - width, length, axis=dim))
    lanes = 128

    def flat(strips):
        return jnp.concatenate([s.reshape(-1, lanes) for s in strips], axis=0)

    head, tail = flat(firsts), flat(lasts)
    far = lax.ppermute(jnp.where(even, head, tail), axis, swap_pairs(axis, 1))
    near = lax.ppermute(jnp.where(even, tail, head), axis, swap_pairs(axis, 0))
    before = jnp.where(even, far, near)
    after = jnp.where(even, near, far)
    grown, start = [], 0
    for field, strip in zip(fields, firsts):
        rows = strip.size // lanes
        grown.append(
            jnp.concatenate(
                [
                    before[start : start + rows].reshape(strip.shape),
                    field,
                    after[start : start + rows].reshape(strip.shape),
                ],
                axis=dim,
            )
        )
        start += rows
    return grown


def with_halos(fields, widths):
    fields = exchange(fields, widths, "gx", 1)
    return exchange(fields, widths, "gy", 2)


def inside(halo, extent):
    rows, cols = extent
    gx, gy = lax.axis_index("gx"), lax.axis_index("gy")
    row = gx * rows - halo + jnp.arange(rows + 2 * halo)
    col = gy * cols - halo + jnp.arange(cols + 2 * halo)
    row_in = (row >= 0) & (row < rows * lax.axis_size("gx"))
    col_in = (col >= 0) & (col < cols * lax.axis_size("gy"))
    return (row_in[:, None] & col_in[None, :])[None, :, :, None]


def silu(a):
    return a * jax.nn.sigmoid(a)


def slope(a):
    s = jax.nn.sigmoid(a)
    return s * (1.0 + a * (1.0 - s))


WIDE = 24
COARSE = 16
ONE = 128
TWO = 256


def dot(a, b):
    return jnp.dot(a, b, preferred_element_type=F32)


def dot_t(a, b):
    return lax.dot_general(a, b, (((1,), (1,)), ((), ())), preferred_element_type=F32)


def lanes(i, width=ONE):
    return pl.ds(i * width, width)


def spread(flat, plane, out, offsets, rows):
    for y in range(rows):
        for i, offset in enumerate(offsets):
            out[plane, pl.ds(y * 16, 16), lanes(i)] = flat[
                plane, pl.ds(y * WIDE + offset, 16), :
            ].astype(BF)


def taps(field, plane, depth, rows, step, mirrored):
    pieces, valid = [], []
    for oz in (-1, 0, 1):
        source = plane - oz if mirrored else plane + oz
        if 0 <= source < depth:
            valid.append(oz + 1)
            for oy in (2, 1, 0) if mirrored else (0, 1, 2):
                pieces.append(field[source, pl.ds(oy * step, rows), :])
    return jnp.concatenate(pieces, axis=1), valid[0], valid[-1] + 1


def side_by_side(weight, low, high):
    return jnp.concatenate([weight[t] for t in range(9 * low, 9 * high)], axis=1)


def forward_kernel(
    volume, cot, mask, order, w_first, w_down, w_middle, w_up,
    send, keep, skip_out, pre_first, pre_coarse, pre_middle, pre_up, upward, cot_cols,
    vol_flat, vol_cols, vol_odd, skip, blocked, coarse, coarse_cols, cot_flat, joined, joined_t,
):
    depth = 4
    rows = 20 * WIDE
    for z in range(depth):
        vol_flat[z, pl.ds(0, 22 * WIDE), :] = volume[z].astype(F32)
        vol_flat[z, pl.ds(22 * WIDE, 8), :] = jnp.zeros((8, ONE), F32)
        for i in range(3):
            vol_cols[z, :, lanes(i)] = vol_flat[z, pl.ds(i, 22 * WIDE), :].astype(BF)
            vol_odd[z, :, lanes(i)] = vol_flat[z, pl.ds(WIDE + i, rows), :].astype(BF)
        cot_flat[z, pl.ds(0, 18 * WIDE), :] = cot[z].astype(F32)
        spread(cot_flat, z, cot_cols, (2, 1, 0), 18)
    inner = mask[...] > 0.0
    for z in range(depth):
        pieces, valid = [], []
        for oz in (-1, 0, 1):
            if 0 <= z + oz < depth:
                valid.append(oz + 1)
                pieces.append(vol_cols[z + oz, pl.ds(0, rows), :])
                pieces.append(vol_odd[z + oz])
                pieces.append(vol_cols[z + oz, pl.ds(2 * WIDE, rows), :])
        taps_here = jnp.concatenate(pieces, axis=1)
        weight = w_first[pl.ds(valid[0] * 9 * ONE, len(valid) * 9 * ONE), :]
        pre = dot(taps_here, weight)
        pre_first[z] = pre
        act = jnp.where(inner, silu(pre), 0.0).astype(BF)
        skip_out[z] = act
        skip[z, pl.ds(0, rows), :] = act.astype(F32)
        skip[z, pl.ds(rows, 8), :] = jnp.zeros((8, ONE), F32)
        for y in range(16):
            joined[pl.ds(z * 256 + y * 16, 16), lanes(0)] = skip[
                z, pl.ds((y + 2) * WIDE + 2, 16), :
            ].astype(BF)
    for z in range(depth):
        for b in range(2):
            for c in range(2):
                for y in range(10):
                    start = (2 * y + b) * WIDE + c
                    blocked[pl.ds((z // 2) * 160 + y * 16, 16), lanes(4 * (z % 2) + 2 * b + c)] = skip[
                        z, pl.ds(start, 16, stride=2), :
                    ].astype(BF)
    pre = dot(blocked[...], w_down[...])
    pre_coarse[...] = pre
    act = silu(pre).astype(BF).astype(F32)
    for z in range(2):
        coarse[z, pl.ds(0, 160), :] = act[z * 160 : (z + 1) * 160]
        coarse[z, pl.ds(160, 8), :] = jnp.zeros((8, TWO), F32)
        for i in range(3):
            coarse_cols[z, :, lanes(i, TWO)] = coarse[z, pl.ds(i, 160), :].astype(BF)
    for z in range(2):
        matrix, low, high = taps(coarse_cols, z, 2, 128, 16, False)
        weight = w_middle[pl.ds(low * 9 * TWO, (high - low) * 9 * TWO), :]
        pre_middle[z] = dot(matrix, weight)
    middle = silu(pre_middle[...]).astype(BF).reshape(256, TWO)
    for k in range(8):
        a, b, c = k // 4, k // 2 % 2, k % 2
        part = dot(middle, w_up[:, lanes(k)])
        for z in range(2):
            for y in range(8):
                pre_up[2 * z + a, pl.ds((2 * y + b) * 16 + c, 8, stride=2), :] = part[
                    z * 128 + y * 16 : z * 128 + y * 16 + 8
                ]
    for z in range(depth):
        act = silu(pre_up[z]).astype(BF)
        upward[z] = act
        joined[pl.ds(z * 256, 256), lanes(1)] = act
    joined_t[...] = dot_t(order[...], joined[...]).astype(BF)
    for oz in (-1, 0, 1):
        low, high = max(0, oz), min(depth, depth + oz)
        for oy in (-1, 0, 1):
            cols = jnp.concatenate(
                [cot_cols[z - oz, pl.ds((1 - oy) * 16, 256), :] for z in range(low, high)], axis=0
            )
            part = dot(joined_t[:, pl.ds(low * 256, (high - low) * 256)], cols).astype(BF)
            at = pl.ds((3 * (oz + 1) + oy + 1) * 3 * ONE, 3 * ONE)
            send[:, at] = part[:128]
            keep[:, at] = part[128:]


def cot_kernel(cot_cols, pre_up, pre_middle, w_last, w_up, grad_skip, grad_middle, grad_up, blocked):
    for z in range(4):
        matrix, low, high = taps(cot_cols, z, 4, 256, 16, True)
        both = dot_t(matrix, side_by_side(w_last, low, high)).astype(BF)
        grad_skip[z] = both[:, :ONE]
        grad_up[z] = (both[:, ONE:].astype(F32) * slope(pre_up[z])).astype(BF).astype(F32)
    for z in range(4):
        for b in range(2):
            for c in range(2):
                for y in range(8):
                    blocked[pl.ds((z // 2) * 64 + y * 8, 8), lanes(4 * (z % 2) + 2 * b + c)] = grad_up[
                        z, pl.ds((2 * y + b) * 16 + c, 8, stride=2), :
                    ]
    back = dot_t(blocked[...].astype(BF), w_up[...])
    for z in range(2):
        for y in range(8):
            grad_middle[z, y] = (
                back[z * 64 + y * 8 : z * 64 + y * 8 + 8] * slope(pre_middle[z, pl.ds(y * 16, 8), :])
            ).astype(BF)


def logits_kernel(skip, up, w_last, logits, skip_flat, up_flat, cols):
    for z in range(4):
        skip_flat[...] = skip[z].astype(F32)
        up_flat[...] = up[z].astype(F32)
        for y in range(18):
            for i in range(3):
                cols[z, pl.ds(y * 16, 16), lanes(2 * i)] = skip_flat[
                    pl.ds((y + 1) * WIDE + 1 + i, 16), :
                ].astype(BF)
                cols[z, pl.ds(y * 16, 16), lanes(2 * i + 1)] = up_flat[
                    pl.ds(y * WIDE + i, 16), :
                ].astype(BF)
    for z in range(4):
        matrix, low, high = taps(cols, z, 4, 256, 16, False)
        weight = w_last[pl.ds(low * 9 * TWO, (high - low) * 9 * TWO), :]
        logits[z] = dot(matrix, weight).astype(BF)


def backward_kernel(
    grad_middle, grad_skip, pre_coarse, pre_first, mask, w_middle, w_down, w_first,
    grad_volume, mid_flat, mid_cols, down, first, cols,
):
    for z in range(2):
        mid_flat[z, pl.ds(0, 192), :] = grad_middle[z].astype(F32)
        mid_flat[z, pl.ds(192, 8), :] = jnp.zeros((8, TWO), F32)
        for i in range(3):
            mid_cols[z, :, lanes(i, TWO)] = mid_flat[z, pl.ds(2 - i, 192), :].astype(BF)
    for z in range(2):
        matrix, low, high = taps(mid_cols, z, 2, 160, 16, True)
        back = dot_t(matrix, side_by_side(w_middle, low, high))
        coarse = (back * slope(pre_coarse[pl.ds(z * 160, 160), :])).astype(BF)
        for k in range(8):
            a, b, c = k // 4, k // 2 % 2, k % 2
            part = dot_t(coarse, w_down[lanes(k), :])
            for y in range(10):
                start = (2 * y + b) * WIDE + c
                down[2 * z + a, pl.ds(start, 8, stride=2), :] = part[y * 16 : y * 16 + 8]
                down[2 * z + a, pl.ds(start + 16, 4, stride=2), :] = part[y * 16 + 8 : y * 16 + 12]
    inner = mask[...] > 0.0
    for z in range(4):
        rows = pl.ds(WIDE + 1, 18 * WIDE)
        value = (grad_skip[z].astype(F32) + down[z, rows, :]) * slope(pre_first[z, rows, :])
        first[z] = jnp.where(inner, value, 0.0).astype(BF).astype(F32)
        spread(first, z, cols, (2, 1, 0), 18)
    for z in range(4):
        matrix, low, high = taps(cols, z, 4, 256, 16, True)
        grad_volume[z] = dot_t(matrix, side_by_side(w_first, low, high)).astype(BF)


def call(kernel, outs, scratch, *args):
    vmem = pl.BlockSpec(memory_space=pltpu.VMEM)
    return pl.pallas_call(
        kernel,
        out_shape=[jax.ShapeDtypeStruct(shape, kind) for shape, kind in outs],
        in_specs=[vmem] * len(args),
        out_specs=[vmem] * len(outs),
        scratch_shapes=[pltpu.VMEM(shape, kind) for shape, kind in scratch],
        compiler_params=pltpu.CompilerParams(vmem_limit_bytes=50 * 2**20),
    )(*args)


def run_forward(volume_ext, cot_ext, mask, order, w_first, w_down, w_middle, w_up):
    return call(
        forward_kernel,
        [
            ((128, 27 * ONE), BF), ((128, 27 * ONE), BF), ((4, 480, ONE), BF), ((4, 480, ONE), F32),
            ((320, TWO), F32), ((2, 128, TWO), F32), ((4, 256, ONE), F32), ((4, 256, ONE), BF),
            ((4, 288, 3 * ONE), BF),
        ],
        [
            ((4, 536, ONE), F32), ((4, 528, 3 * ONE), BF), ((4, 480, 3 * ONE), BF), ((4, 488, ONE), F32),
            ((320, 8 * ONE), BF), ((2, 168, TWO), F32), ((2, 160, 3 * TWO), BF), ((4, 432, ONE), F32),
            ((1024, TWO), BF), ((TWO, 1024), BF),
        ],
        volume_ext, cot_ext, mask, order, w_first.reshape(-1, ONE), w_down, w_middle.reshape(-1, TWO), w_up,
    )


def run_cot(cot_cols, pre_up, pre_middle, w_last, w_up):
    return call(
        cot_kernel,
        [((4, 256, ONE), BF), ((2, 8, 8, TWO), BF)],
        [((4, 256, ONE), F32), ((128, 8 * ONE), F32)],
        cot_cols, pre_up, pre_middle, w_last, w_up,
    )


def run_logits(skip, up_ext, w_last):
    return call(
        logits_kernel,
        [((4, 256, ONE), BF)],
        [((480, ONE), F32), ((432, ONE), F32), ((4, 288, 3 * TWO), BF)],
        skip, up_ext, w_last.reshape(-1, ONE),
    )[0]


def run_backward(middle_ext, skip_ext, pre_coarse, pre_first, mask, w_middle, w_down, w_first):
    return call(
        backward_kernel,
        [((4, 256, ONE), BF)],
        [
            ((2, 200, TWO), F32), ((2, 192, 3 * TWO), BF), ((4, 480, ONE), F32), ((4, 432, ONE), F32),
            ((4, 288, 3 * ONE), BF),
        ],
        middle_ext, skip_ext, pre_coarse, pre_first, mask, w_middle, w_down, w_first,
    )[0]


def widen(field, cols):
    z, y, x, c = field.shape
    padded = jnp.pad(field, ((0, 0), (0, 0), (0, cols - x), (0, 0)))
    return padded.reshape(z, y * cols, c)


def flat_mask(halo, extent):
    seen = inside(halo, extent)[0, :, :, 0]
    seen = jnp.pad(seen, ((0, 0), (0, WIDE - seen.shape[1]))).reshape(-1, 1)
    return jnp.broadcast_to(seen.astype(F32), (seen.shape[0], ONE))


PARTS = (4, 2, 2, 4, 4)


def groups_over(dims):
    table = {}
    for rank in range(math.prod(PARTS)):
        place, rest = [], rank
        for size in PARTS[::-1]:
            place.insert(0, rest % size)
            rest //= size
        table.setdefault(tuple(p for d, p in enumerate(place) if d not in dims), []).append(rank)
    return list(table.values())


def core_swap(array):
    count = lax.axis_size("gx")
    return lax.ppermute(array, "gx", [(i, i ^ 1) for i in range(count)])


def send_order():
    core = lax.rem(lax.axis_index("gx"), 2)
    row = lax.broadcasted_iota(jnp.int32, (256, 256), 0)
    channel = lax.broadcasted_iota(jnp.int32, (256, 256), 1)
    half, x, y, hi, lo = row // 128, row // 32 % 4, row // 8 % 4, row // 4 % 2, row % 4
    owner = lax.rem(half + 1 - core + 2, 2)
    wanted = (((x * 2 + hi) * 2 + owner) * 4 + lo) * 4 + y
    return (channel == wanted).astype(BF)


def reduce_entries(send, keep):
    width = send.shape[1]
    got = core_swap(send)
    pair = (keep.astype(F32) + got.astype(F32)).astype(BF).reshape(16, 8, width)
    pair = lax.all_to_all(pair, AXES, 0, 0, axis_index_groups=groups_over((0, 4)), tiled=True)
    plane = pair.astype(F32).sum(0).reshape(8, 27, width // 27)
    plane = lax.all_to_all(plane, AXES, 0, 0, axis_index_groups=groups_over((1, 3)), tiled=True)
    return plane.sum(0)


def on_device(volume, w_first, w_down, w_middle, w_up, w_last, cotangent):
    depth, rows, cols, one = volume.shape
    extent = (rows, cols)

    volume_ext, cot_ext = with_halos([volume, cotangent], (3, 1))
    send, keep, skip, pre_first, pre_coarse, pre_middle, pre_up, upward, cot_cols = run_forward(
        widen(volume_ext, WIDE), widen(cot_ext, WIDE), flat_mask(2, extent), send_order(),
        w_first, w_down, w_middle, w_up,
    )
    grad_skip, grad_middle = run_cot(cot_cols, pre_up, pre_middle, w_last, w_up)

    fine = (depth, rows, cols, one)
    up_ext, skip_ext, middle_ext = with_halos(
        [upward.reshape(fine), grad_skip.reshape(fine), grad_middle], (1, 1, 2)
    )
    total = reduce_entries(send, keep)
    scale = 1.0 / math.sqrt(
        depth * rows * cols * lax.axis_size("gx") * lax.axis_size("gy")
    )
    grad_last = total * scale
    logits = run_logits(skip, widen(up_ext, WIDE), w_last).reshape(fine)
    grad_volume = run_backward(
        widen(middle_ext, COARSE), widen(skip_ext, WIDE), pre_coarse, pre_first, flat_mask(1, extent),
        w_middle, w_down, w_first,
    ).reshape(fine)
    return logits, grad_volume, grad_last


def solution(mesh):
    field = P(None, "gx", "gy", None)
    return jax.shard_map(
        on_device,
        mesh=mesh,
        in_specs=(field, P(), P(), P(), P(), P(), field),
        out_specs=(field, field, P(None, AXES)),
        check_vma=False,
    )
```

time: 193 us -> 106 us (0.55)
  the two profiles are of different devices: /device:TPU:8 before, /device:TPU:32 now
where the time goes in v2:
time: 106 us; the launch traced here: 105 us
  starting transfers between devices  44.2 us (42%)
  Pallas kernels  26.7 us (25%)
  waiting for transfers between devices  19.8 us (19%)
  local copies, waits for them, and re-layouts  6.61 us (6%)
  other arithmetic  6.51 us (6%)
  between operations  1.5 us (1%)
    pallas_call x4, Pallas kernels, call(): pl.pallas_call(kernel, out_shape=[jax.ShapeDtypeStruct(shape, kind) for s...  26.7 us
    ppermute x4, starting transfers between devices, exchange(): near = lax.ppermute(jnp.where(even, tail, head), axis, swap_pairs(axis, 0))  15.2 us
    all_to_all x1, waiting for transfers between devices, reduce_entries(): lax.all_to_all(pair, AXES, 0, 0, axis_index_groups=groups_over((0, 4)), t...  14.5 us
    ppermute x4, starting transfers between devices, exchange(): far = lax.ppermute(jnp.where(even, head, tail), axis, swap_pairs(axis, 1))  10.6 us
    all_to_all x1, starting transfers between devices, reduce_entries(): lax.all_to_all(pair, AXES, 0, 0, axis_index_groups=groups_over((0, 4)), t...  9.92 us
    all_to_all x1, starting transfers between devices, reduce_entries(): lax.all_to_all(plane, AXES, 0, 0, axis_index_groups=groups_over((1, 3)),...  8.13 us
    ppermute x4, waiting for transfers between devices, exchange(): far = lax.ppermute(jnp.where(even, head, tail), axis, swap_pairs(axis, 1))  3.43 us
    unnamed x28, local copies, waits for them, and re-layouts  2.89 us
  transfers between devices with their start and end apart: 11, of which 4 were waited for; matrix products, arithmetic and copies ran while one was open for 5% of the time, Pallas kernels for 11%

profile of v2, /device:TPU:32, one launch (start us, length us, event | category | flops | bytes accessed | tf_op | source)
XLA Modules:
  0.0 105.2 jit_solution(2818834811429185564)
XLA Ops:
  0.7 0.9 fusion.45
  1.6 0.7 fusion.46
  2.3 0.7 collective-permute-start
  3.0 7.7 %collective-permute-start.1 = (bf16[256,128]{1,0:T(8,128)(2,1)S(1)}, bf16[256,128]{1,0:T(8,128)(2,1)S(1)}, u32[]{:S(2)}, u32[]{:S(2)}) collective-permute-start(bf16[256,128]{1,0:T(8,128)(2,1)S(1)} %get-tuple-element.48), channel_id=1, source_target_pairs={{0,16},{16,0},{32,48},{48,32},{64,80},{80,64},{96,112},{112,96},{1... | collective-permute-start | bytes 196616 | tf_op jit(solution)/shard_map/ppermute | solution.py:37
  10.9 0.7 fusion.35.order
  12.4 5.4 %collective-permute-start.2 = (bf16[336,128]{1,0:T(8,128)(2,1)S(1)}, bf16[336,128]{1,0:T(8,128)(2,1)S(1)}, u32[]{:S(2)}, u32[]{:S(2)}) collective-permute-start(bf16[336,128]{1,0:T(8,128)(2,1)S(1)} %get-tuple-element.43), channel_id=1, source_target_pairs={{1,2},{2,1},{3,4},{4,3},{5,6},{6,5},{7,8},{8,7},{9,10},{10,9},{11,... | collective-permute-start | bytes 258056 | tf_op jit(solution)/shard_map/ppermute | solution.py:36
  17.9 3.4 %collective-permute-done.2 = bf16[336,128]{1,0:T(8,128)(2,1)S(1)} collective-permute-done((bf16[336,128]{1,0:T(8,128)(2,1)S(1)}, bf16[336,128]{1,0:T(8,128)(2,1)S(1)}, u32[]{:S(2)}, u32[]{:S(2)}) %collective-permute-start.2) | collective-permute-done | bytes 86048 | tf_op jit(solution)/shard_map/ppermute | solution.py:36
  21.3 1.5 %collective-permute-done.3 = bf16[336,128]{1,0:T(8,128)(2,1)S(1)} collective-permute-done((bf16[336,128]{1,0:T(8,128)(2,1)S(1)}, bf16[336,128]{1,0:T(8,128)(2,1)S(1)}, u32[]{:S(2)}, u32[]{:S(2)}) %collective-permute-start.3) | collective-permute-done | bytes 86048 | tf_op jit(solution)/shard_map/ppermute | solution.py:37
  23.3 1.2 %fusion.12 = bf16[4,22,24,128]{3,2,1,0:T(8,128)(2,1)} fusion(bf16[4,22,3,128]{3,2,1,0:T(4,128)(2,1)S(1)} %reshape.229, bf16[4,22,3,128]{3,2,1,0:T(4,128)(2,1)S(1)} %reshape.228, bf16[4,3,16,128]{3,2,1,0:T(8,128)(2,1)S(1)} %bitcast.58, bf16[4,16,16,128]{3,2,1,0:T(8,128)(2,1)S(1)} %copy-done.6, bf16[4,3,16,128]{3,2,1,0:T(8,128)(2,1)S(1)} %bitcast.56), kind=kLoop, calls=%fused_computation.16 | loop fusion | flops 4325376 | bytes 1036288 | tf_op jit(solution)/shard_map/concatenate | solution.py:44
  24.6 11.3 %shard_map.94 = (bf16[128,3456]{1,0:T(8,128)(2,1)}, bf16[128,3456]{1,0:T(8,128)(2,1)}, bf16[4,480,128]{2,1,0:T(8,128)(2,1)S(1)}, f32[4,480,128]{2,1,0:T(8,128)},...) custom-call(bf16[4,528,128]{2,1,0:T(8,128)(2,1)} %bitcast.54, ...), custom_call_target="tpu_custom_call" | custom-call | tf_op jit(solution)/shard_map/pallas_call | solution.py:276
  35.9 1.2 %copy-done.5 = bf16[4,288,384]{2,1,0:T(8,128)(2,1)S(1)} copy-done((bf16[4,288,384]{2,1,0:T(8,128)(2,1)S(1)}, bf16[4,288,384]{2,1,0:T(8,128)(2,1)}, u32[]{:S(2)}) %copy-start.5) | copy-done | bytes 884760
  37.1 3.5 %shard_map.95 = (bf16[4,256,128]{2,1,0:T(8,128)(2,1)S(1)}, bf16[2,8,8,256]{3,2,1,0:T(8,128)(2,1)S(1)}) custom-call(bf16[4,288,384]{2,1,0:T(8,128)(2,1)S(1)} %copy-done.5, f32[4,256,128]{2,1,0:T(8,128)S(1)} %get-tuple-element.17.pre_up, f32[2,128,256]{2,1,0:T(8,128)S(1)} %get-tuple-element.18.pre_middle, bf16[27,256,128]{2,1,0:T(8,128)(2,1)} %w_last.1, ...), custom_call_target="tpu_custom_call" | custom-call | tf_op jit(solution)/shard_map/pallas_call | solution.py:276
  40.7 0.7 collective-permute-start.4
  41.4 7.3 %collective-permute-start.5 = (bf16[192,128]{1,0:T(8,128)(2,1)S(1)}, bf16[192,128]{1,0:T(8,128)(2,1)S(1)}, u32[]{:S(2)}, u32[]{:S(2)}) collective-permute-start(bf16[192,128]{1,0:T(8,128)(2,1)S(1)} %get-tuple-element.58), channel_id=1, source_target_pairs={{0,16},{16,0},{32,48},{48,32},{64,80},{80,64},{96,112},{112,96},{1... | collective-permute-start | bytes 147464 | tf_op jit(solution)/shard_map/ppermute | solution.py:37
  50.2 3.9 %collective-permute-start.6 = (bf16[240,128]{1,0:T(8,128)(2,1)S(1)}, bf16[240,128]{1,0:T(8,128)(2,1)S(1)}, u32[]{:S(2)}, u32[]{:S(2)}) collective-permute-start(bf16[240,128]{1,0:T(8,128)(2,1)S(1)} %get-tuple-element.51), channel_id=1, source_target_pairs={{1,2},{2,1},{3,4},{4,3},{5,6},{6,5},{7,8},{8,7},{9,10},{10,9},{11,... | collective-permute-start | bytes 184328 | tf_op jit(solution)/shard_map/ppermute | solution.py:36
  54.2 2.3 %fusion.5 = bf16[16,8,3456]{2,1,0:T(8,128)(2,1)} fusion(bf16[128,3456]{1,0:T(8,128)(2,1)} %collective-permute-done.8, bf16[128,3456]{1,0:T(8,128)(2,1)S(1)} %copy-done.8), kind=kLoop, calls=%fused_computation.8 | loop fusion | flops 1769472 | bytes 2654208 | tf_op jit(solution)/shard_map/reshape | solution.py:377
  56.5 9.9 %all-to-all-start = ((bf16[16,8,3456]{2,1,0:T(8,128)(2,1)}), bf16[16,8,3456]{2,1,0:T(8,128)(2,1)S(1)}, u32[]{:S(2)}, u32[]{:S(2)}) async-start(bf16[16,8,3456]{2,1,0:T(8,128)(2,1)} %fusion.5), calls=%async_computation | async-start | bytes 1769472 | tf_op jit(solution)/shard_map/all_to_all | solution.py:378
  67.2 14.5 %all-to-all-done = bf16[16,8,3456]{2,1,0:T(8,128)(2,1)S(1)} async-done(((bf16[16,8,3456]{2,1,0:T(8,128)(2,1)}), bf16[16,8,3456]{2,1,0:T(8,128)(2,1)S(1)}, u32[]{:S(2)}, u32[]{:S(2)}) %all-to-all-start) | async-done | bytes 884768 | tf_op jit(solution)/shard_map/all_to_all | solution.py:378
  81.8 0.7 copy.46
  82.4 8.1 %all-to-all-start.1 = ((f32[8,27,128]{2,1,0:T(8,128)}), f32[8,27,128]{2,1,0:T(8,128)S(1)}, u32[]{:S(2)}, u32[]{:S(2)}) async-start(f32[8,27,128]{2,1,0:T(8,128)} %copy.46), calls=%async_computation.1 | async-start | bytes 262144 | tf_op jit(solution)/shard_map/all_to_all | solution.py:380
  91.1 1.3 %copy-done = bf16[27,256,128]{2,1,0:T(8,128)(2,1)S(1)} copy-done((bf16[27,256,128]{2,1,0:T(8,128)(2,1)S(1)}, bf16[27,256,128]{2,1,0:T(8,128)(2,1)}, u32[]{:S(2)}) %copy-start) | copy-done | bytes 1769496
  92.4 4.0 %shard_map.96 = bf16[4,256,128]{2,1,0:T(8,128)(2,1)} custom-call(bf16[4,480,128]{2,1,0:T(8,128)(2,1)S(1)} %get-tuple-element.14.skip, bf16[4,432,128]{2,1,0:T(8,128)(2,1)S(1)} %bitcast.47, bf16[6912,128]{1,0:T(8,128)(2,1)S(1)} %bitcast.43), custom_call_target="tpu_custom_call" | custom-call | tf_op jit(solution)/shard_map/pallas_call | solution.py:276
  96.7 7.9 %shard_map.97 = bf16[4,256,128]{2,1,0:T(8,128)(2,1)} custom-call(bf16[2,192,256]{2,1,0:T(8,128)(2,1)S(1)} %bitcast.48, bf16[4,432,128]{2,1,0:T(8,128)(2,1)S(1)} %bitcast.46, f32[320,256]{1,0:T(8,128)S(1)} %get-tuple-element.21.pre_coarse, f32[4,480,128]{2,1,0:T(8,128)S(1)} %copy-done.4, f32[432,128]{1,0:T(8,128)S(1)} %broadcast_in_dim.5.mask, ...), custom_call_target="tpu_custom_call" | custom-call | tf_op jit(solution)/shard_map/pallas_call | solution.py:276
  104.6 0.6 broadcast_multiply_fusion
  (127 shorter events, 4.3 us)
Async XLA Ops:
  0.6 11.5 %copy-start.6 = (bf16[4,16,16,128]{3,2,1,0:T(8,128)(2,1)S(1)}, bf16[4,16,16,128]{3,2,1,0:T(8,128)(2,1)}, u32[]{:S(2)}) copy-start(bf16[4,16,16,128]{3,2,1,0:T(8,128)(2,1)} %param.7) | copy-start | bytes 786436
  0.6 11.2 %copy-start.7 = (bf16[4,16,16,128]{3,2,1,0:T(8,128)(2,1)S(1)}, bf16[4,16,16,128]{3,2,1,0:T(8,128)(2,1)}, u32[]{:S(2)}) copy-start(bf16[4,16,16,128]{3,2,1,0:T(8,128)(2,1)} %param.13) | copy-start | bytes 786436
  2.3 9.4 %collective-permute-start = (bf16[256,128]{1,0:T(8,128)(2,1)S(1)}, bf16[256,128]{1,0:T(8,128)(2,1)S(1)}, u32[]{:S(2)}, u32[]{:S(2)}) collective-permute-start(bf16[256,128]{1,0:T(8,128)(2,1)S(1)} %get-tuple-element.47), channel_id=1, source_target_pairs={{16,32},{32,16},{48,64},{64,48},{80,96},{96,80},{112,128},{128,112... | collective-permute-start | bytes 196616 | tf_op jit(solution)/shard_map/ppermute | solution.py:36
  3.0 8.8 %collective-permute-start.1 = (bf16[256,128]{1,0:T(8,128)(2,1)S(1)}, bf16[256,128]{1,0:T(8,128)(2,1)S(1)}, u32[]{:S(2)}, u32[]{:S(2)}) collective-permute-start(bf16[256,128]{1,0:T(8,128)(2,1)S(1)} %get-tuple-element.48), channel_id=1, source_target_pairs={{0,16},{16,0},{32,48},{48,32},{64,80},{80,64},{96,112},{112,96},{1... | collective-permute-start | bytes 196616 | tf_op jit(solution)/shard_map/ppermute | solution.py:37
  12.4 8.9 %collective-permute-start.2 = (bf16[336,128]{1,0:T(8,128)(2,1)S(1)}, bf16[336,128]{1,0:T(8,128)(2,1)S(1)}, u32[]{:S(2)}, u32[]{:S(2)}) collective-permute-start(bf16[336,128]{1,0:T(8,128)(2,1)S(1)} %get-tuple-element.43), channel_id=1, source_target_pairs={{1,2},{2,1},{3,4},{4,3},{5,6},{6,5},{7,8},{8,7},{9,10},{10,9},{11,... | collective-permute-start | bytes 258056 | tf_op jit(solution)/shard_map/ppermute | solution.py:36
  17.8 5.0 %collective-permute-start.3 = (bf16[336,128]{1,0:T(8,128)(2,1)S(1)}, bf16[336,128]{1,0:T(8,128)(2,1)S(1)}, u32[]{:S(2)}, u32[]{:S(2)}) collective-permute-start(bf16[336,128]{1,0:T(8,128)(2,1)S(1)} %get-tuple-element.44), channel_id=1, source_target_pairs={{0,1},{1,0},{2,3},{3,2},{4,5},{5,4},{6,7},{7,6},{8,9},{9,8},{10,11... | collective-permute-start | bytes 258056 | tf_op jit(solution)/shard_map/ppermute | solution.py:37
  23.0 1.6 %copy-start.2 = (bf16[256,1024]{1,0:T(8,128)(2,1)S(1)}, bf16[256,1024]{1,0:T(8,128)(2,1)}, u32[]{:S(2)}) copy-start(bf16[256,1024]{1,0:T(8,128)(2,1)} %w_up.3) | copy-start | bytes 1572868
  23.0 1.6 %copy-start.3 = (bf16[1024,256]{1,0:T(8,128)(2,1)S(1)}, bf16[1024,256]{1,0:T(8,128)(2,1)}, u32[]{:S(2)}) copy-start(bf16[1024,256]{1,0:T(8,128)(2,1)} %w_down.3) | copy-start | bytes 1572868
  35.9 1.2 %copy-start.5 = (bf16[4,288,384]{2,1,0:T(8,128)(2,1)S(1)}, bf16[4,288,384]{2,1,0:T(8,128)(2,1)}, u32[]{:S(2)}) copy-start(bf16[4,288,384]{2,1,0:T(8,128)(2,1)} %get-tuple-element.16.cot_cols) | copy-start | bytes 2654212
  40.7 8.5 %collective-permute-start.4 = (bf16[192,128]{1,0:T(8,128)(2,1)S(1)}, bf16[192,128]{1,0:T(8,128)(2,1)S(1)}, u32[]{:S(2)}, u32[]{:S(2)}) collective-permute-start(bf16[192,128]{1,0:T(8,128)(2,1)S(1)} %get-tuple-element.57), channel_id=1, source_target_pairs={{16,32},{32,16},{48,64},{64,48},{80,96},{96,80},{112,128},{128,112... | collective-permute-start | bytes 147464 | tf_op jit(solution)/shard_map/ppermute | solution.py:36
  41.4 8.2 %collective-permute-start.5 = (bf16[192,128]{1,0:T(8,128)(2,1)S(1)}, bf16[192,128]{1,0:T(8,128)(2,1)S(1)}, u32[]{:S(2)}, u32[]{:S(2)}) collective-permute-start(bf16[192,128]{1,0:T(8,128)(2,1)S(1)} %get-tuple-element.58), channel_id=1, source_target_pairs={{0,16},{16,0},{32,48},{48,32},{64,80},{80,64},{96,112},{112,96},{1... | collective-permute-start | bytes 147464 | tf_op jit(solution)/shard_map/ppermute | solution.py:37
  48.9 5.3 %collective-permute-start.8 = (bf16[128,3456]{1,0:T(8,128)(2,1)}, bf16[128,3456]{1,0:T(8,128)(2,1)}, u32[]{:S(2)}, u32[]{:S(2)}) collective-permute-start(bf16[128,3456]{1,0:T(8,128)(2,1)} %get-tuple-element.24), channel_id=1, source_target_pairs={{0,16},{16,0},{32,48},{48,32},{64,80},{80,64},{96,112},{112,96},{1... | collective-permute-start | bytes 2654216 | tf_op jit(solution)/shard_map/ppermute | solution.py:361
  49.6 4.6 %copy-start.8 = (bf16[128,3456]{1,0:T(8,128)(2,1)S(1)}, bf16[128,3456]{1,0:T(8,128)(2,1)}, u32[]{:S(2)}) copy-start(bf16[128,3456]{1,0:T(8,128)(2,1)} %get-tuple-element.23) | copy-start | bytes 2654212
  50.2 16.4 %collective-permute-start.6 = (bf16[240,128]{1,0:T(8,128)(2,1)S(1)}, bf16[240,128]{1,0:T(8,128)(2,1)S(1)}, u32[]{:S(2)}, u32[]{:S(2)}) collective-permute-start(bf16[240,128]{1,0:T(8,128)(2,1)S(1)} %get-tuple-element.51), channel_id=1, source_target_pairs={{1,2},{2,1},{3,4},{4,3},{5,6},{6,5},{7,8},{8,7},{9,10},{10,9},{11,... | collective-permute-start | bytes 184328 | tf_op jit(solution)/shard_map/ppermute | solution.py:36
  54.1 12.5 %collective-permute-start.7 = (bf16[240,128]{1,0:T(8,128)(2,1)S(1)}, bf16[240,128]{1,0:T(8,128)(2,1)S(1)}, u32[]{:S(2)}, u32[]{:S(2)}) collective-permute-start(bf16[240,128]{1,0:T(8,128)(2,1)S(1)} %get-tuple-element.52), channel_id=1, source_target_pairs={{0,1},{1,0},{2,3},{3,2},{4,5},{5,4},{6,7},{7,6},{8,9},{9,8},{10,11... | collective-permute-start | bytes 184328 | tf_op jit(solution)/shard_map/ppermute | solution.py:37
  56.5 25.1 %all-to-all-start = ((bf16[16,8,3456]{2,1,0:T(8,128)(2,1)}), bf16[16,8,3456]{2,1,0:T(8,128)(2,1)S(1)}, u32[]{:S(2)}, u32[]{:S(2)}) async-start(bf16[16,8,3456]{2,1,0:T(8,128)(2,1)} %fusion.5), calls=%async_computation | async-start | bytes 1769472 | tf_op jit(solution)/shard_map/all_to_all | solution.py:378
  82.4 22.2 %all-to-all-start.1 = ((f32[8,27,128]{2,1,0:T(8,128)}), f32[8,27,128]{2,1,0:T(8,128)S(1)}, u32[]{:S(2)}, u32[]{:S(2)}) async-start(f32[8,27,128]{2,1,0:T(8,128)} %copy.46), calls=%async_computation.1 | async-start | bytes 262144 | tf_op jit(solution)/shard_map/all_to_all | solution.py:380
  90.9 1.5 %copy-start = (bf16[27,256,128]{2,1,0:T(8,128)(2,1)S(1)}, bf16[27,256,128]{2,1,0:T(8,128)(2,1)}, u32[]{:S(2)}) copy-start(bf16[27,256,128]{2,1,0:T(8,128)(2,1)} %w_last.1) | copy-start | bytes 5308420
  92.4 4.2 %copy-start.1 = (bf16[27,128,128]{2,1,0:T(8,128)(2,1)S(1)}, bf16[27,128,128]{2,1,0:T(8,128)(2,1)}, u32[]{:S(2)}) copy-start(bf16[27,128,128]{2,1,0:T(8,128)(2,1)} %w_first.1) | copy-start | bytes 2654212
  92.4 4.2 %copy-start.4 = (f32[4,480,128]{2,1,0:T(8,128)S(1)}, f32[4,480,128]{2,1,0:T(8,128)}, u32[]{:S(2)}) copy-start(f32[4,480,128]{2,1,0:T(8,128)} %get-tuple-element.22.pre_first) | copy-start | bytes 2949124

commit v3 on v2

v3 whole, which is shorter than its diff:
```python
import math

import jax
import jax.numpy as jnp
from jax import lax
from jax.experimental import pallas as pl
from jax.experimental.pallas import tpu as pltpu
from jax.sharding import PartitionSpec as P

AXES = ("gx", "gy")
BF = jnp.bfloat16
F32 = jnp.float32


def swap_pairs(axis, offset):
    count = lax.axis_size(axis)
    pairs = []
    for low in range(offset, count - 1, 2):
        pairs += [(low, low + 1), (low + 1, low)]
    return pairs


def exchange(fields, widths, axis, dim):
    even = lax.rem(lax.axis_index(axis), 2) == 0
    firsts, lasts = [], []
    for field, width in zip(fields, widths):
        length = field.shape[dim]
        firsts.append(lax.slice_in_dim(field, 0, width, axis=dim))
        lasts.append(lax.slice_in_dim(field, length - width, length, axis=dim))
    lanes = 128

    def flat(strips):
        return jnp.concatenate([s.reshape(-1, lanes) for s in strips], axis=0)

    head, tail = flat(firsts), flat(lasts)
    far = lax.ppermute(jnp.where(even, head, tail), axis, swap_pairs(axis, 1))
    near = lax.ppermute(jnp.where(even, tail, head), axis, swap_pairs(axis, 0))
    before = jnp.where(even, far, near)
    after = jnp.where(even, near, far)
    grown, start = [], 0
    for field, strip in zip(fields, firsts):
        rows = strip.size // lanes
        grown.append(
            jnp.concatenate(
                [
                    before[start : start + rows].reshape(strip.shape),
                    field,
                    after[start : start + rows].reshape(strip.shape),
                ],
                axis=dim,
            )
        )
        start += rows
    return grown


def with_halos(fields, widths):
    fields = exchange(fields, widths, "gx", 1)
    return exchange(fields, widths, "gy", 2)


def inside(halo, extent):
    rows, cols = extent
    gx, gy = lax.axis_index("gx"), lax.axis_index("gy")
    row = gx * rows - halo + jnp.arange(rows + 2 * halo)
    col = gy * cols - halo + jnp.arange(cols + 2 * halo)
    row_in = (row >= 0) & (row < rows * lax.axis_size("gx"))
    col_in = (col >= 0) & (col < cols * lax.axis_size("gy"))
    return (row_in[:, None] & col_in[None, :])[None, :, :, None]


def silu(a):
    return a * jax.nn.sigmoid(a)


def slope(a):
    s = jax.nn.sigmoid(a)
    return s * (1.0 + a * (1.0 - s))


WIDE = 24
COARSE = 16
ONE = 128
TWO = 256


def dot(a, b):
    return jnp.dot(a, b, preferred_element_type=F32)


def dot_t(a, b):
    return lax.dot_general(a, b, (((1,), (1,)), ((), ())), preferred_element_type=F32)


def lanes(i, width=ONE):
    return pl.ds(i * width, width)


def spread(flat, plane, out, offsets, rows):
    for y in range(rows):
        for i, offset in enumerate(offsets):
            out[plane, pl.ds(y * 16, 16), lanes(i)] = flat[
                plane, pl.ds(y * WIDE + offset, 16), :
            ].astype(BF)


def taps(field, planes, rows, step, mirrored):
    order = (2, 1, 0) if mirrored else (0, 1, 2)
    pieces = [field[p, pl.ds(oy * step, rows), :] for p in planes for oy in order]
    return jnp.concatenate(pieces, axis=1)


def side_by_side(weight, low, high):
    return jnp.concatenate([weight[t] for t in range(9 * low, 9 * high)], axis=1)


def pair_weight(weight, first, planes):
    size = weight.shape[0] // 3
    blocks = []
    for p in planes:
        both = []
        for out in (first, first + 1):
            oz = p - out + 1
            both.append(
                weight[pl.ds(oz * size, size), :] if 0 <= oz <= 2 else jnp.zeros((size, ONE), BF)
            )
        blocks.append(jnp.concatenate(both, axis=1))
    return jnp.concatenate(blocks, axis=0)


def pair_weight_t(weight, first, planes):
    both = []
    for out in (first, first + 1):
        blocks = []
        for p in planes:
            oz = out - p + 1
            if 0 <= oz <= 2:
                blocks.append(side_by_side(weight, oz, oz + 1))
            else:
                blocks.append(jnp.zeros((ONE, 9 * ONE), BF))
        both.append(jnp.concatenate(blocks, axis=1))
    return jnp.concatenate(both, axis=0)


PAIRS = ((0, (0, 1, 2)), (2, (1, 2, 3)))


def fetch(sems, *pairs):
    copies = []
    for i, (source, target) in enumerate(pairs):
        copy = pltpu.make_async_copy(source, target, sems.at[i])
        copy.start()
        copies.append(copy)
    return copies


def forward_kernel(
    volume, cot, mask, order, w_first_in, w_down_in, w_middle_in, w_up_in,
    send, keep, skip_out, pre_first_out, pre_coarse, pre_middle, pre_up, upward,
    vol_flat, vol_cols, vol_odd, skip, blocked, coarse, coarse_cols, cot_flat, cot_cols, joined, joined_t,
    pre_first, w_first, w_down, w_middle, w_up, sems, out_sems,
):
    depth = 4
    rows = 20 * WIDE
    arrive = fetch(
        sems, (w_first_in, w_first), (w_down_in, w_down), (w_middle_in, w_middle), (w_up_in, w_up)
    )
    for z in range(depth):
        vol_flat[z, pl.ds(0, 22 * WIDE), :] = volume[z].astype(F32)
        vol_flat[z, pl.ds(22 * WIDE, 8), :] = jnp.zeros((8, ONE), F32)
        for i in range(3):
            vol_cols[z, :, lanes(i)] = vol_flat[z, pl.ds(i, 22 * WIDE), :].astype(BF)
            vol_odd[z, :, lanes(i)] = vol_flat[z, pl.ds(WIDE + i, rows), :].astype(BF)
        cot_flat[z, pl.ds(0, 18 * WIDE), :] = cot[z].astype(F32)
        spread(cot_flat, z, cot_cols, (2, 1, 0), 18)
    inner = mask[...] > 0.0
    arrive[0].wait()
    leave = []
    for first, planes in PAIRS:
        pieces = []
        for p in planes:
            pieces.append(vol_cols[p, pl.ds(0, rows), :])
            pieces.append(vol_odd[p])
            pieces.append(vol_cols[p, pl.ds(2 * WIDE, rows), :])
        both = dot(jnp.concatenate(pieces, axis=1), pair_weight(w_first, first, planes))
        for z, pre in ((first, both[:, :ONE]), (first + 1, both[:, ONE:])):
            pre_first[z] = pre
            act = jnp.where(inner, silu(pre), 0.0).astype(BF)
            skip_out[z] = act
            skip[z, pl.ds(0, rows), :] = act.astype(F32)
            skip[z, pl.ds(rows, 8), :] = jnp.zeros((8, ONE), F32)
            for y in range(16):
                joined[pl.ds(z * 256 + y * 16, 16), lanes(0)] = skip[
                    z, pl.ds((y + 2) * WIDE + 2, 16), :
                ].astype(BF)
            for b in range(2):
                for c in range(2):
                    for y in range(10):
                        start = (2 * y + b) * WIDE + c
                        blocked[
                            pl.ds((z // 2) * 160 + y * 16, 16), lanes(4 * (z % 2) + 2 * b + c)
                        ] = skip[z, pl.ds(start, 16, stride=2), :].astype(BF)
    leave.append(pltpu.make_async_copy(pre_first, pre_first_out, out_sems.at[0]))
    leave[-1].start()
    arrive[1].wait()
    pre = dot(blocked[...], w_down[...])
    pre_coarse[...] = pre
    act = silu(pre).astype(BF).astype(F32)
    for z in range(2):
        coarse[z, pl.ds(0, 160), :] = act[z * 160 : (z + 1) * 160]
        coarse[z, pl.ds(160, 8), :] = jnp.zeros((8, TWO), F32)
        for i in range(3):
            coarse_cols[z, :, lanes(i, TWO)] = coarse[z, pl.ds(i, 160), :].astype(BF)
    arrive[2].wait()
    for z in range(2):
        weight = w_middle[pl.ds((1 - z) * 9 * TWO, 18 * TWO), :]
        pre_middle[z] = dot(taps(coarse_cols, (0, 1), 128, 16, False), weight)
    middle = silu(pre_middle[...]).astype(BF).reshape(256, TWO)
    arrive[3].wait()
    for k in range(8):
        a, b, c = k // 4, k // 2 % 2, k % 2
        part = dot(middle, w_up[:, lanes(k)])
        for z in range(2):
            for y in range(8):
                pre_up[2 * z + a, pl.ds((2 * y + b) * 16 + c, 8, stride=2), :] = part[
                    z * 128 + y * 16 : z * 128 + y * 16 + 8
                ]
    for z in range(depth):
        act = silu(pre_up[z]).astype(BF)
        upward[z] = act
        joined[pl.ds(z * 256, 256), lanes(1)] = act
    joined_t[...] = dot_t(order[...], joined[...]).astype(BF)
    for oz in (-1, 0, 1):
        low, high = max(0, oz), min(depth, depth + oz)
        cols = jnp.concatenate(
            [taps(cot_cols, (z - oz,), 256, 16, True) for z in range(low, high)], axis=0
        )
        part = dot(joined_t[:, pl.ds(low * 256, (high - low) * 256)], cols).astype(BF)
        at = pl.ds((oz + 1) * 9 * ONE, 9 * ONE)
        send[:, at] = part[:128]
        keep[:, at] = part[128:]
    for copy in leave:
        copy.wait()


def cot_kernel(
    cot, pre_up, pre_middle, w_last_in, w_up_in,
    grad_skip, grad_middle,
    cot_flat, cot_cols, grad_up, blocked, w_last, w_up, sems,
):
    arrive = fetch(sems, (w_last_in, w_last), (w_up_in, w_up))
    for z in range(4):
        cot_flat[z] = cot[z].astype(F32)
        spread(cot_flat, z, cot_cols, (2, 1, 0), 18)
    arrive[0].wait()
    for z in range(4):
        low, high = max(0, z - 1), min(4, z + 2)
        matrix = taps(cot_cols, range(high - 1, low - 1, -1), 256, 16, True)
        both = dot_t(matrix, side_by_side(w_last, z - high + 2, z - low + 2)).astype(BF)
        grad_skip[z] = both[:, :ONE]
        grad_up[z] = (both[:, ONE:].astype(F32) * slope(pre_up[z])).astype(BF).astype(F32)
        for b in range(2):
            for c in range(2):
                for y in range(8):
                    blocked[pl.ds((z // 2) * 64 + y * 8, 8), lanes(4 * (z % 2) + 2 * b + c)] = grad_up[
                        z, pl.ds((2 * y + b) * 16 + c, 8, stride=2), :
                    ]
    arrive[1].wait()
    back = dot_t(blocked[...].astype(BF), w_up[...])
    for z in range(2):
        for y in range(8):
            grad_middle[z, y] = (
                back[z * 64 + y * 8 : z * 64 + y * 8 + 8] * slope(pre_middle[z, pl.ds(y * 16, 8), :])
            ).astype(BF)


def back_kernel(
    skip, up, grad_mid, grad_skip, pre_coarse, pre_first_in, mask, w_last_in, w_middle_in, w_down_in, w_first_in,
    logits, grad_volume,
    skip_flat, up_flat, join_cols, mid_flat, mid_cols, down, first_flat, cols,
    pre_first, w_last, w_middle, w_down, w_first, sems,
):
    arrive = fetch(
        sems, (w_last_in, w_last), (w_middle_in, w_middle), (w_down_in, w_down), (w_first_in, w_first),
        (pre_first_in, pre_first),
    )
    for z in range(4):
        skip_flat[...] = skip[z].astype(F32)
        up_flat[...] = up[z].astype(F32)
        for y in range(18):
            for i in range(3):
                join_cols[z, pl.ds(y * 16, 16), lanes(2 * i)] = skip_flat[
                    pl.ds((y + 1) * WIDE + 1 + i, 16), :
                ].astype(BF)
                join_cols[z, pl.ds(y * 16, 16), lanes(2 * i + 1)] = up_flat[
                    pl.ds(y * WIDE + i, 16), :
                ].astype(BF)
    arrive[0].wait()
    for first, planes in PAIRS:
        both = dot(taps(join_cols, planes, 256, 16, False), pair_weight(w_last, first, planes)).astype(BF)
        logits[first] = both[:, :ONE]
        logits[first + 1] = both[:, ONE:]
    for z in range(2):
        mid_flat[z, pl.ds(0, 192), :] = grad_mid[z].astype(F32)
        mid_flat[z, pl.ds(192, 8), :] = jnp.zeros((8, TWO), F32)
        for i in range(3):
            mid_cols[z, :, lanes(i, TWO)] = mid_flat[z, pl.ds(2 - i, 192), :].astype(BF)
    arrive[1].wait()
    arrive[2].wait()
    for z in range(2):
        back = dot_t(taps(mid_cols, (1, 0), 160, 16, True), side_by_side(w_middle, z, z + 2))
        coarse = (back * slope(pre_coarse[pl.ds(z * 160, 160), :])).astype(BF)
        for k in range(8):
            a, b, c = k // 4, k // 2 % 2, k % 2
            part = dot_t(coarse, w_down[lanes(k), :])
            for y in range(10):
                start = (2 * y + b) * WIDE + c
                down[2 * z + a, pl.ds(start, 8, stride=2), :] = part[y * 16 : y * 16 + 8]
                down[2 * z + a, pl.ds(start + 16, 4, stride=2), :] = part[y * 16 + 8 : y * 16 + 12]
    inner = mask[...] > 0.0
    arrive[4].wait()
    for z in range(4):
        rows = pl.ds(WIDE + 1, 18 * WIDE)
        value = (grad_skip[z].astype(F32) + down[z, rows, :]) * slope(pre_first[z, rows, :])
        first_flat[z] = jnp.where(inner, value, 0.0).astype(BF).astype(F32)
        spread(first_flat, z, cols, (2, 1, 0), 18)
    arrive[3].wait()
    for first, planes in PAIRS:
        both = dot_t(taps(cols, planes, 256, 16, True), pair_weight_t(w_first, first, planes)).astype(BF)
        grad_volume[first] = both[:, :ONE]
        grad_volume[first + 1] = both[:, ONE:]


def pair_kernel(one, other, out):
    out[...] = (one[...].astype(F32) + other[...].astype(F32)).astype(BF)


VMEM = pl.BlockSpec(memory_space=pltpu.VMEM)
ANY = pl.BlockSpec(memory_space=pl.ANY)


def call(kernel, outs, scratch, in_specs, out_specs, *args):
    return pl.pallas_call(
        kernel,
        out_shape=[jax.ShapeDtypeStruct(shape, kind) for shape, kind in outs],
        in_specs=in_specs,
        out_specs=out_specs,
        scratch_shapes=[
            pltpu.SemaphoreType.DMA((shape,)) if kind is None else pltpu.VMEM(shape, kind)
            for shape, kind in scratch
        ],
        compiler_params=pltpu.CompilerParams(vmem_limit_bytes=50 * 2**20),
    )(*args)


def run_forward(volume_ext, cot_ext, mask, order, w_first, w_down, w_middle, w_up):
    return call(
        forward_kernel,
        [
            ((128, 27 * ONE), BF), ((128, 27 * ONE), BF), ((4, 480, ONE), BF), ((4, 480, ONE), F32),
            ((320, TWO), F32), ((2, 128, TWO), F32), ((4, 256, ONE), F32), ((4, 256, ONE), BF),
        ],
        [
            ((4, 536, ONE), F32), ((4, 528, 3 * ONE), BF), ((4, 480, 3 * ONE), BF), ((4, 488, ONE), F32),
            ((320, 8 * ONE), BF), ((2, 168, TWO), F32), ((2, 160, 3 * TWO), BF), ((4, 432, ONE), F32),
            ((4, 288, 3 * ONE), BF), ((1024, TWO), BF), ((TWO, 1024), BF), ((4, 480, ONE), F32),
            ((27 * ONE, ONE), BF), ((8 * ONE, TWO), BF), ((27 * TWO, TWO), BF), ((TWO, 8 * ONE), BF),
            (4, None), (1, None),
        ],
        [VMEM] * 4 + [ANY] * 4,
        [VMEM] * 3 + [ANY] + [VMEM] * 4,
        volume_ext, cot_ext, mask, order, w_first.reshape(-1, ONE), w_down, w_middle.reshape(-1, TWO), w_up,
    )


def run_cot(cot_ext, pre_up, pre_middle, w_last, w_up):
    return call(
        cot_kernel,
        [((4, 256, ONE), BF), ((2, 8, 8, TWO), BF)],
        [
            ((4, 432, ONE), F32), ((4, 288, 3 * ONE), BF), ((4, 256, ONE), F32), ((128, 8 * ONE), F32),
            ((27, TWO, ONE), BF), ((TWO, 8 * ONE), BF), (2, None),
        ],
        [VMEM] * 3 + [ANY] * 2,
        [VMEM] * 2,
        cot_ext, pre_up, pre_middle, w_last, w_up,
    )


def run_back(skip, up_ext, middle_ext, skip_ext, pre_coarse, pre_first, mask, w_last, w_middle, w_down, w_first):
    return call(
        back_kernel,
        [((4, 256, ONE), BF), ((4, 256, ONE), BF)],
        [
            ((480, ONE), F32), ((432, ONE), F32), ((4, 288, 3 * TWO), BF),
            ((2, 200, TWO), F32), ((2, 192, 3 * TWO), BF), ((4, 480, ONE), F32), ((4, 432, ONE), F32),
            ((4, 288, 3 * ONE), BF), ((4, 480, ONE), F32),
            ((27 * TWO, ONE), BF), ((27, TWO, TWO), BF), ((8 * ONE, TWO), BF), ((27, ONE, ONE), BF), (5, None),
        ],
        [VMEM] * 5 + [ANY, VMEM] + [ANY] * 4,
        [VMEM] * 2,
        skip, up_ext, middle_ext, skip_ext, pre_coarse, pre_first, mask,
        w_last.reshape(-1, ONE), w_middle, w_down, w_first,
    )


def run_pair(one, other):
    return call(pair_kernel, [(one.shape, BF)], [], [VMEM] * 2, [VMEM], one, other)[0]


def widen(field, cols):
    z, y, x, c = field.shape
    padded = jnp.pad(field, ((0, 0), (0, 0), (0, cols - x), (0, 0)))
    return padded.reshape(z, y * cols, c)


def flat_mask(halo, extent):
    seen = inside(halo, extent)[0, :, :, 0]
    seen = jnp.pad(seen, ((0, 0), (0, WIDE - seen.shape[1]))).reshape(-1, 1)
    return jnp.broadcast_to(seen.astype(F32), (seen.shape[0], ONE))


PARTS = (4, 2, 2, 4, 4)


def groups_over(dims):
    table = {}
    for rank in range(math.prod(PARTS)):
        place, rest = [], rank
        for size in PARTS[::-1]:
            place.insert(0, rest % size)
            rest //= size
        table.setdefault(tuple(p for d, p in enumerate(place) if d not in dims), []).append(rank)
    return list(table.values())


def core_swap(array):
    count = lax.axis_size("gx")
    return lax.ppermute(array, "gx", [(i, i ^ 1) for i in range(count)])


def send_order():
    core = lax.rem(lax.axis_index("gx"), 2)
    row = lax.broadcasted_iota(jnp.int32, (256, 256), 0)
    channel = lax.broadcasted_iota(jnp.int32, (256, 256), 1)
    half, x, y, hi, lo = row // 128, row // 32 % 4, row // 8 % 4, row // 4 % 2, row % 4
    owner = lax.rem(half + 1 - core + 2, 2)
    wanted = (((x * 2 + hi) * 2 + owner) * 4 + lo) * 4 + y
    return (channel == wanted).astype(BF)


def on_device(volume, w_first, w_down, w_middle, w_up, w_last, cotangent):
    depth, rows, cols, one = volume.shape
    extent = (rows, cols)
    fine = (depth, rows, cols, one)

    volume_ext, cot_ext = with_halos([volume, cotangent], (3, 1))
    cot_ext = widen(cot_ext, WIDE)
    send, keep, skip, pre_first, pre_coarse, pre_middle, pre_up, upward = run_forward(
        widen(volume_ext, WIDE), cot_ext, flat_mask(2, extent), send_order(), w_first, w_down, w_middle, w_up
    )
    got = core_swap(send)
    grad_skip, grad_middle = run_cot(cot_ext, pre_up, pre_middle, w_last, w_up)
    pair = run_pair(keep, got)
    pair, upward, grad_skip, grad_middle = lax.optimization_barrier(
        (pair, upward, grad_skip, grad_middle)
    )
    pair = pair.reshape(16, 8, 27 * one)
    pair = lax.all_to_all(pair, AXES, 0, 0, axis_index_groups=groups_over((0, 4)), tiled=True)
    up_ext, skip_ext, middle_ext = with_halos(
        [upward.reshape(fine), grad_skip.reshape(fine), grad_middle], (1, 1, 2)
    )
    plane = pair.astype(F32).sum(0).reshape(8, 27, one)
    plane, up_ext, skip_ext, middle_ext = lax.optimization_barrier(
        (plane, up_ext, skip_ext, middle_ext)
    )
    plane = lax.all_to_all(plane, AXES, 0, 0, axis_index_groups=groups_over((1, 3)), tiled=True)
    logits, grad_volume = run_back(
        skip, widen(up_ext, WIDE), widen(middle_ext, COARSE), widen(skip_ext, WIDE), pre_coarse, pre_first,
        flat_mask(1, extent), w_last, w_middle, w_down, w_first,
    )
    scale = 1.0 / math.sqrt(
        depth * rows * cols * lax.axis_size("gx") * lax.axis_size("gy")
    )
    return logits.reshape(fine), grad_volume.reshape(fine), plane.sum(0) * scale


def solution(mesh):
    field = P(None, "gx", "gy", None)
    return jax.shard_map(
        on_device,
        mesh=mesh,
        in_specs=(field, P(), P(), P(), P(), P(), field),
        out_specs=(field, field, P(None, AXES)),
        check_vma=False,
    )
```

time: 106 us -> 102 us (0.962)
  Pallas kernels: 26.7 us -> 23.2 us
  other arithmetic: 6.51 us -> 4.24 us
  starting transfers between devices: 44.2 us -> 45.8 us
    pallas_call x4, Pallas kernels: 26.7 us -> 23.2 us  [call(): pl.pallas_call(kernel, out_shape=[jax.ShapeDtypeStruct(shape, kind) for s...]
    reshape x1 -> x0, other arithmetic: 2.29 us -> none  [reduce_entries(): pair = (keep.astype(F32) + got.astype(F32)).astype(BF).reshape(16, 8, width)]
    ppermute x4, starting transfers between devices: 15.2 us -> 16.7 us  [exchange(): near = lax.ppermute(jnp.where(even, tail, head), axis, swap_pairs(axis, 0))]
    all_to_all x2, waiting for transfers between devices: 14.5 us -> 13.4 us  [the longest x1 13.4 us: on_device(): lax.all_to_all(pair, AXES, 0, 0, axis_index_groups=groups_over((0, 4)), t...]
    unnamed x28 -> x30, local copies, waits for them, and re-layouts: 2.89 us -> 2.46 us
  transfers between devices with their start and end apart: 11 -> 11, of which waited for: 4 -> 4; matrix products, arithmetic and copies ran while one was open for 5% -> 3% of each run, Pallas kernels for 11% -> 12%
where the time goes in v3:
time: 102 us; the launch traced here: 101 us
  starting transfers between devices  45.8 us (45%)
  Pallas kernels  23.2 us (23%)
  waiting for transfers between devices  19 us (19%)
  local copies, waits for them, and re-layouts  6.8 us (7%)
  other arithmetic  4.24 us (4%)
  between operations  1.48 us (1%)
    pallas_call x4, Pallas kernels, call(): pl.pallas_call(kernel, out_shape=[jax.ShapeDtypeStruct(shape, kind) for s...  23.2 us
    ppermute x4, starting transfers between devices, exchange(): near = lax.ppermute(jnp.where(even, tail, head), axis, swap_pairs(axis, 0))  16.7 us
    all_to_all x1, waiting for transfers between devices, on_device(): lax.all_to_all(pair, AXES, 0, 0, axis_index_groups=groups_over((0, 4)), t...  13.4 us
    ppermute x4, starting transfers between devices, exchange(): far = lax.ppermute(jnp.where(even, head, tail), axis, swap_pairs(axis, 1))  10.9 us
    all_to_all x1, starting transfers between devices, on_device(): lax.all_to_all(plane, AXES, 0, 0, axis_index_groups=groups_over((1, 3)),...  9.48 us
    all_to_all x1, starting transfers between devices, on_device(): lax.all_to_all(pair, AXES, 0, 0, axis_index_groups=groups_over((0, 4)), t...  8.79 us
    ppermute x4, waiting for transfers between devices, exchange(): far = lax.ppermute(jnp.where(even, head, tail), axis, swap_pairs(axis, 1))  3.26 us
    unnamed x30, local copies, waits for them, and re-layouts  2.46 us
  transfers between devices with their start and end apart: 11, of which 4 were waited for; matrix products, arithmetic and copies ran while one was open for 3% of the time, Pallas kernels for 12%

profile of v3, /device:TPU:32, one launch (start us, length us, event | category | flops | bytes accessed | tf_op | source)
XLA Modules:
  0.0 100.6 jit_solution(4259233126010362547)
XLA Ops:
  0.7 0.9 fusion.39
  1.6 0.7 fusion.40
  2.3 0.7 collective-permute-start
  3.0 7.7 %collective-permute-start.1 = (bf16[256,128]{1,0:T(8,128)(2,1)S(1)}, bf16[256,128]{1,0:T(8,128)(2,1)S(1)}, u32[]{:S(2)}, u32[]{:S(2)}) collective-permute-start(bf16[256,128]{1,0:T(8,128)(2,1)S(1)} %get-tuple-element.66), channel_id=1, source_target_pairs={{0,16},{16,0},{32,48},{48,32},{64,80},{80,64},{96,112},{112,96},{1... | collective-permute-start | bytes 196616 | tf_op jit(solution)/shard_map/ppermute | solution.py:37
  10.8 0.8 fusion.31.order
  12.3 5.4 %collective-permute-start.2 = (bf16[336,128]{1,0:T(8,128)(2,1)S(1)}, bf16[336,128]{1,0:T(8,128)(2,1)S(1)}, u32[]{:S(2)}, u32[]{:S(2)}) collective-permute-start(bf16[336,128]{1,0:T(8,128)(2,1)S(1)} %get-tuple-element.61), channel_id=1, source_target_pairs={{1,2},{2,1},{3,4},{4,3},{5,6},{6,5},{7,8},{8,7},{9,10},{10,9},{11,... | collective-permute-start | bytes 258056 | tf_op jit(solution)/shard_map/ppermute | solution.py:36
  17.9 3.3 %collective-permute-done.2 = bf16[336,128]{1,0:T(8,128)(2,1)S(1)} collective-permute-done((bf16[336,128]{1,0:T(8,128)(2,1)S(1)}, bf16[336,128]{1,0:T(8,128)(2,1)S(1)}, u32[]{:S(2)}, u32[]{:S(2)}) %collective-permute-start.2) | collective-permute-done | bytes 86048 | tf_op jit(solution)/shard_map/ppermute | solution.py:36
  21.2 1.7 %collective-permute-done.3 = bf16[336,128]{1,0:T(8,128)(2,1)S(1)} collective-permute-done((bf16[336,128]{1,0:T(8,128)(2,1)S(1)}, bf16[336,128]{1,0:T(8,128)(2,1)S(1)}, u32[]{:S(2)}, u32[]{:S(2)}) %collective-permute-start.3) | collective-permute-done | bytes 86048 | tf_op jit(solution)/shard_map/ppermute | solution.py:37
  23.3 1.1 %fusion.11 = bf16[4,22,24,128]{3,2,1,0:T(8,128)(2,1)} fusion(bf16[4,22,3,128]{3,2,1,0:T(4,128)(2,1)S(1)} %reshape.229, bf16[4,22,3,128]{3,2,1,0:T(4,128)(2,1)S(1)} %reshape.228, bf16[4,3,16,128]{3,2,1,0:T(8,128)(2,1)S(1)} %bitcast.58, bf16[4,16,16,128]{3,2,1,0:T(8,128)(2,1)S(1)} %copy-done.7, bf16[4,3,16,128]{3,2,1,0:T(8,128)(2,1)S(1)} %bitcast.56), kind=kLoop, calls=%fused_computation.14 | loop fusion | flops 4325376 | bytes 1036288 | tf_op jit(solution)/shard_map/concatenate | solution.py:44
  24.6 9.8 %shard_map.94 = (bf16[128,3456]{1,0:T(8,128)(2,1)}, bf16[128,3456]{1,0:T(8,128)(2,1)}, bf16[4,480,128]{2,1,0:T(8,128)(2,1)S(1)}, f32[4,480,128]{2,1,0:T(8,128)},...) custom-call(bf16[4,528,128]{2,1,0:T(8,128)(2,1)} %bitcast.54, ...), custom_call_target="tpu_custom_call" | custom-call | tf_op jit(solution)/shard_map/pallas_call | solution.py:343
  34.4 0.7 copy-done.5
  35.1 2.9 %shard_map.96 = (bf16[4,256,128]{2,1,0:T(8,128)(2,1)S(1)}, bf16[2,8,8,256]{3,2,1,0:T(8,128)(2,1)S(1)}) custom-call(bf16[4,432,128]{2,1,0:T(8,128)(2,1)S(1)} %bitcast.44, f32[4,256,128]{2,1,0:T(8,128)S(1)} %get-tuple-element.27.pre_up, f32[2,128,256]{2,1,0:T(8,128)S(1)} %get-tuple-element.28.pre_middle, bf16[27,256,128]{2,1,0:T(8,128)(2,1)S(1)} %copy-done, ...), custom_call_target="tpu_custom_call" | custom-call | tf_op jit(solution)/shard_map/pallas_call | solution.py:343
  38.0 1.1 %shard_map.95 = bf16[128,3456]{1,0:T(8,128)(2,1)} custom-call(bf16[128,3456]{1,0:T(8,128)(2,1)S(1)} %copy-done.4, bf16[128,3456]{1,0:T(8,128)(2,1)S(1)} %collective-permute-done.4.other), custom_call_target="tpu_custom_call" | custom-call | tf_op jit(solution)/shard_map/pallas_call | solution.py:343
  39.3 0.7 collective-permute-start.5
  39.9 8.7 %collective-permute-start.6 = (bf16[192,128]{1,0:T(8,128)(2,1)S(1)}, bf16[192,128]{1,0:T(8,128)(2,1)S(1)}, u32[]{:S(2)}, u32[]{:S(2)}) collective-permute-start(bf16[192,128]{1,0:T(8,128)(2,1)S(1)} %get-tuple-element.76), channel_id=1, source_target_pairs={{0,16},{16,0},{32,48},{48,32},{64,80},{80,64},{96,112},{112,96},{1... | collective-permute-start | bytes 147464 | tf_op jit(solution)/shard_map/ppermute | solution.py:37
  48.8 0.7 collective-permute-done.6
  50.2 4.2 %collective-permute-start.7 = (bf16[240,128]{1,0:T(8,128)(2,1)S(1)}, bf16[240,128]{1,0:T(8,128)(2,1)S(1)}, u32[]{:S(2)}, u32[]{:S(2)}) collective-permute-start(bf16[240,128]{1,0:T(8,128)(2,1)S(1)} %get-tuple-element.69), channel_id=1, source_target_pairs={{1,2},{2,1},{3,4},{4,3},{5,6},{6,5},{7,8},{8,7},{9,10},{10,9},{11,... | collective-permute-start | bytes 184328 | tf_op jit(solution)/shard_map/ppermute | solution.py:36
  54.5 8.8 %all-to-all-start = ((bf16[16,8,3456]{2,1,0:T(8,128)(2,1)}), bf16[16,8,3456]{2,1,0:T(8,128)(2,1)S(1)}, u32[]{:S(2)}, u32[]{:S(2)}) async-start(bf16[16,8,3456]{2,1,0:T(8,128)(2,1)} %bitcast.12), calls=%async_computation | async-start | bytes 1769472 | tf_op jit(solution)/shard_map/all_to_all | solution.py:469
  63.5 0.6 reshape.259
  65.1 13.4 %all-to-all-done = bf16[16,8,3456]{2,1,0:T(8,128)(2,1)S(1)} async-done(((bf16[16,8,3456]{2,1,0:T(8,128)(2,1)}), bf16[16,8,3456]{2,1,0:T(8,128)(2,1)S(1)}, u32[]{:S(2)}, u32[]{:S(2)}) %all-to-all-start) | async-done | bytes 884768 | tf_op jit(solution)/shard_map/all_to_all | solution.py:469
  78.6 0.7 copy.46
  79.3 9.5 %all-to-all-start.1 = ((f32[8,27,128]{2,1,0:T(8,128)}), f32[8,27,128]{2,1,0:T(8,128)S(1)}, u32[]{:S(2)}, u32[]{:S(2)}) async-start(f32[8,27,128]{2,1,0:T(8,128)} %copy.46), calls=%async_computation.1 | async-start | bytes 262144 | tf_op jit(solution)/shard_map/all_to_all | solution.py:477
  89.5 0.9 copy-done.1
  90.5 9.5 %shard_map.97 = (bf16[4,256,128]{2,1,0:T(8,128)(2,1)}, bf16[4,256,128]{2,1,0:T(8,128)(2,1)}) custom-call(bf16[4,480,128]{2,1,0:T(8,128)(2,1)S(1)} %get-tuple-element.23.skip, bf16[4,432,128]{2,1,0:T(8,128)(2,1)S(1)} %bitcast.46, bf16[2,192,256]{2,1,0:T(8,128)(2,1)S(1)} %bitcast.48, bf16[4,432,128]{2,1,0:T(8,128)(2,1)S(1)} %bitcast.47, ...), custom_call_target="tpu_custom_call" | custom-call | tf_op jit(solution)/shard_map/pallas_call | solution.py:343
  (129 shorter events, 4.8 us)
Async XLA Ops:
  0.6 11.4 %copy-start.7 = (bf16[4,16,16,128]{3,2,1,0:T(8,128)(2,1)S(1)}, bf16[4,16,16,128]{3,2,1,0:T(8,128)(2,1)}, u32[]{:S(2)}) copy-start(bf16[4,16,16,128]{3,2,1,0:T(8,128)(2,1)} %param.7) | copy-start | bytes 786436
  0.6 11.1 %copy-start.8 = (bf16[4,16,16,128]{3,2,1,0:T(8,128)(2,1)S(1)}, bf16[4,16,16,128]{3,2,1,0:T(8,128)(2,1)}, u32[]{:S(2)}) copy-start(bf16[4,16,16,128]{3,2,1,0:T(8,128)(2,1)} %param.13) | copy-start | bytes 786436
  2.3 9.4 %collective-permute-start = (bf16[256,128]{1,0:T(8,128)(2,1)S(1)}, bf16[256,128]{1,0:T(8,128)(2,1)S(1)}, u32[]{:S(2)}, u32[]{:S(2)}) collective-permute-start(bf16[256,128]{1,0:T(8,128)(2,1)S(1)} %get-tuple-element.65), channel_id=1, source_target_pairs={{16,32},{32,16},{48,64},{64,48},{80,96},{96,80},{112,128},{128,112... | collective-permute-start | bytes 196616 | tf_op jit(solution)/shard_map/ppermute | solution.py:36
  3.0 8.7 %collective-permute-start.1 = (bf16[256,128]{1,0:T(8,128)(2,1)S(1)}, bf16[256,128]{1,0:T(8,128)(2,1)S(1)}, u32[]{:S(2)}, u32[]{:S(2)}) collective-permute-start(bf16[256,128]{1,0:T(8,128)(2,1)S(1)} %get-tuple-element.66), channel_id=1, source_target_pairs={{0,16},{16,0},{32,48},{48,32},{64,80},{80,64},{96,112},{112,96},{1... | collective-permute-start | bytes 196616 | tf_op jit(solution)/shard_map/ppermute | solution.py:37
  12.3 8.8 %collective-permute-start.2 = (bf16[336,128]{1,0:T(8,128)(2,1)S(1)}, bf16[336,128]{1,0:T(8,128)(2,1)S(1)}, u32[]{:S(2)}, u32[]{:S(2)}) collective-permute-start(bf16[336,128]{1,0:T(8,128)(2,1)S(1)} %get-tuple-element.61), channel_id=1, source_target_pairs={{1,2},{2,1},{3,4},{4,3},{5,6},{6,5},{7,8},{8,7},{9,10},{10,9},{11,... | collective-permute-start | bytes 258056 | tf_op jit(solution)/shard_map/ppermute | solution.py:36
  17.7 5.1 %collective-permute-start.3 = (bf16[336,128]{1,0:T(8,128)(2,1)S(1)}, bf16[336,128]{1,0:T(8,128)(2,1)S(1)}, u32[]{:S(2)}, u32[]{:S(2)}) collective-permute-start(bf16[336,128]{1,0:T(8,128)(2,1)S(1)} %get-tuple-element.62), channel_id=1, source_target_pairs={{0,1},{1,0},{2,3},{3,2},{4,5},{5,4},{6,7},{7,6},{8,9},{9,8},{10,11... | collective-permute-start | bytes 258056 | tf_op jit(solution)/shard_map/ppermute | solution.py:37
  23.0 1.6 %copy-start.2 = (bf16[256,1024]{1,0:T(8,128)(2,1)S(1)}, bf16[256,1024]{1,0:T(8,128)(2,1)}, u32[]{:S(2)}) copy-start(bf16[256,1024]{1,0:T(8,128)(2,1)} %w_up_in.3) | copy-start | bytes 1572868
  23.0 1.6 %copy-start.3 = (bf16[1024,256]{1,0:T(8,128)(2,1)S(1)}, bf16[1024,256]{1,0:T(8,128)(2,1)}, u32[]{:S(2)}) copy-start(bf16[1024,256]{1,0:T(8,128)(2,1)} %w_down_in.3) | copy-start | bytes 1572868
  24.6 10.5 %copy-start = (bf16[27,256,128]{2,1,0:T(8,128)(2,1)S(1)}, bf16[27,256,128]{2,1,0:T(8,128)(2,1)}, u32[]{:S(2)}) copy-start(bf16[27,256,128]{2,1,0:T(8,128)(2,1)} %w_last_in.1) | copy-start | bytes 5308420
  34.4 0.7 copy-start.5
  35.1 2.9 %collective-permute-start.4 = (bf16[128,3456]{1,0:T(8,128)(2,1)}, bf16[128,3456]{1,0:T(8,128)(2,1)S(1)}, u32[]{:S(2)}, u32[]{:S(2)}) collective-permute-start(bf16[128,3456]{1,0:T(8,128)(2,1)} %get-tuple-element.25), channel_id=1, source_target_pairs={{0,16},{16,0},{32,48},{48,32},{64,80},{80,64},{96,112},{112,96},{1... | collective-permute-start | bytes 2654216 | tf_op jit(solution)/shard_map/ppermute | solution.py:439
  35.1 2.9 %copy-start.4 = (bf16[128,3456]{1,0:T(8,128)(2,1)S(1)}, bf16[128,3456]{1,0:T(8,128)(2,1)}, u32[]{:S(2)}) copy-start(bf16[128,3456]{1,0:T(8,128)(2,1)} %get-tuple-element.24.one) | copy-start | bytes 2654212
  39.3 9.6 %collective-permute-start.5 = (bf16[192,128]{1,0:T(8,128)(2,1)S(1)}, bf16[192,128]{1,0:T(8,128)(2,1)S(1)}, u32[]{:S(2)}, u32[]{:S(2)}) collective-permute-start(bf16[192,128]{1,0:T(8,128)(2,1)S(1)} %get-tuple-element.75), channel_id=1, source_target_pairs={{16,32},{32,16},{48,64},{64,48},{80,96},{96,80},{112,128},{128,112... | collective-permute-start | bytes 147464 | tf_op jit(solution)/shard_map/ppermute | solution.py:36
  39.9 9.6 %collective-permute-start.6 = (bf16[192,128]{1,0:T(8,128)(2,1)S(1)}, bf16[192,128]{1,0:T(8,128)(2,1)S(1)}, u32[]{:S(2)}, u32[]{:S(2)}) collective-permute-start(bf16[192,128]{1,0:T(8,128)(2,1)S(1)} %get-tuple-element.76), channel_id=1, source_target_pairs={{0,16},{16,0},{32,48},{48,32},{64,80},{80,64},{96,112},{112,96},{1... | collective-permute-start | bytes 147464 | tf_op jit(solution)/shard_map/ppermute | solution.py:37
  50.2 13.1 %collective-permute-start.7 = (bf16[240,128]{1,0:T(8,128)(2,1)S(1)}, bf16[240,128]{1,0:T(8,128)(2,1)S(1)}, u32[]{:S(2)}, u32[]{:S(2)}) collective-permute-start(bf16[240,128]{1,0:T(8,128)(2,1)S(1)} %get-tuple-element.69), channel_id=1, source_target_pairs={{1,2},{2,1},{3,4},{4,3},{5,6},{6,5},{7,8},{8,7},{9,10},{10,9},{11,... | collective-permute-start | bytes 184328 | tf_op jit(solution)/shard_map/ppermute | solution.py:36
  54.4 8.9 %collective-permute-start.8 = (bf16[240,128]{1,0:T(8,128)(2,1)S(1)}, bf16[240,128]{1,0:T(8,128)(2,1)S(1)}, u32[]{:S(2)}, u32[]{:S(2)}) collective-permute-start(bf16[240,128]{1,0:T(8,128)(2,1)S(1)} %get-tuple-element.70), channel_id=1, source_target_pairs={{0,1},{1,0},{2,3},{3,2},{4,5},{5,4},{6,7},{7,6},{8,9},{9,8},{10,11... | collective-permute-start | bytes 184328 | tf_op jit(solution)/shard_map/ppermute | solution.py:37
  54.5 24.0 %all-to-all-start = ((bf16[16,8,3456]{2,1,0:T(8,128)(2,1)}), bf16[16,8,3456]{2,1,0:T(8,128)(2,1)S(1)}, u32[]{:S(2)}, u32[]{:S(2)}) async-start(bf16[16,8,3456]{2,1,0:T(8,128)(2,1)} %bitcast.12), calls=%async_computation | async-start | bytes 1769472 | tf_op jit(solution)/shard_map/all_to_all | solution.py:469
  64.1 0.7 copy-start.9
  79.3 20.7 %all-to-all-start.1 = ((f32[8,27,128]{2,1,0:T(8,128)}), f32[8,27,128]{2,1,0:T(8,128)S(1)}, u32[]{:S(2)}, u32[]{:S(2)}) async-start(f32[8,27,128]{2,1,0:T(8,128)} %copy.46), calls=%async_computation.1 | async-start | bytes 262144 | tf_op jit(solution)/shard_map/all_to_all | solution.py:477
  89.2 1.2 %copy-start.1 = (bf16[27,128,128]{2,1,0:T(8,128)(2,1)S(1)}, bf16[27,128,128]{2,1,0:T(8,128)(2,1)}, u32[]{:S(2)}) copy-start(bf16[27,128,128]{2,1,0:T(8,128)(2,1)} %w_first_in.1) | copy-start | bytes 2654212
  89.2 1.2 %copy-start.6 = (f32[320,256]{1,0:T(8,128)S(1)}, f32[320,256]{1,0:T(8,128)}, u32[]{:S(2)}) copy-start(f32[320,256]{1,0:T(8,128)} %copy-done.5) | copy-start | bytes 983044

commit v4 on v3

--- a/solution.py
+++ b/solution.py
@@ -471,9 +471,6 @@
         [upward.reshape(fine), grad_skip.reshape(fine), grad_middle], (1, 1, 2)
     )
     plane = pair.astype(F32).sum(0).reshape(8, 27, one)
-    plane, up_ext, skip_ext, middle_ext = lax.optimization_barrier(
-        (plane, up_ext, skip_ext, middle_ext)
-    )
     plane = lax.all_to_all(plane, AXES, 0, 0, axis_index_groups=groups_over((1, 3)), tiled=True)
     logits, grad_volume = run_back(
         skip, widen(up_ext, WIDE), widen(middle_ext, COARSE), widen(skip_ext, WIDE), pre_coarse, pre_first,

time: 102 us -> 96 us (0.941)
  starting transfers between devices: 45.8 us -> 40 us
  waiting for transfers between devices: 19 us -> 13.9 us
  local copies, waits for them, and re-layouts: 6.8 us -> 11.2 us
  Pallas kernels: 23.2 us -> 24.4 us
    all_to_all x1, waiting for transfers between devices: 13.4 us -> 1.25 us  [on_device(): lax.all_to_all(pair, AXES, 0, 0, axis_index_groups=groups_over((0, 4)), t...]
    all_to_all x1, starting transfers between devices: 9.48 us -> 4.38 us  [on_device(): lax.all_to_all(plane, AXES, 0, 0, axis_index_groups=groups_over((1, 3)),...]
    unnamed x30 -> x48, local copies, waits for them, and re-layouts: 2.46 us -> 7.53 us
    ppermute x4, waiting for transfers between devices: 3.26 us -> 7.36 us  [exchange(): far = lax.ppermute(jnp.where(even, head, tail), axis, swap_pairs(axis, 1))]
    ppermute x4, waiting for transfers between devices: 2.39 us -> 5.28 us  [exchange(): near = lax.ppermute(jnp.where(even, tail, head), axis, swap_pairs(axis, 0))]
    all_to_all x1, starting transfers between devices: 8.79 us -> 6.69 us  [on_device(): lax.all_to_all(pair, AXES, 0, 0, axis_index_groups=groups_over((0, 4)), t...]
    ppermute x4, starting transfers between devices: 10.9 us -> 12.3 us  [exchange(): far = lax.ppermute(jnp.where(even, head, tail), axis, swap_pairs(axis, 1))]
    pallas_call x4, Pallas kernels: 23.2 us -> 24.4 us  [call(): pl.pallas_call(kernel, out_shape=[jax.ShapeDtypeStruct(shape, kind) for s...]
  transfers between devices with their start and end apart: 11 -> 11, of which waited for: 4 -> 5; matrix products, arithmetic and copies ran while one was open for 3% -> 3% of each run, Pallas kernels for 12% -> 13%
where the time goes in v4:
time: 96 us; the launch traced here: 95.4 us
  starting transfers between devices  40 us (42%)
  Pallas kernels  24.4 us (25%)
  waiting for transfers between devices  13.9 us (14%)
  local copies, waits for them, and re-layouts  11.2 us (12%)
  other arithmetic  4.27 us (4%)
  between operations  1.53 us (2%)
    pallas_call x4, Pallas kernels, call(): pl.pallas_call(kernel, out_shape=[jax.ShapeDtypeStruct(shape, kind) for s...  24.4 us
    ppermute x4, starting transfers between devices, exchange(): near = lax.ppermute(jnp.where(even, tail, head), axis, swap_pairs(axis, 0))  16.7 us
    ppermute x4, starting transfers between devices, exchange(): far = lax.ppermute(jnp.where(even, head, tail), axis, swap_pairs(axis, 1))  12.3 us
    unnamed x48, local copies, waits for them, and re-layouts  7.53 us
    ppermute x4, waiting for transfers between devices, exchange(): far = lax.ppermute(jnp.where(even, head, tail), axis, swap_pairs(axis, 1))  7.36 us
    all_to_all x1, starting transfers between devices, on_device(): lax.all_to_all(pair, AXES, 0, 0, axis_index_groups=groups_over((0, 4)), t...  6.69 us
    ppermute x4, waiting for transfers between devices, exchange(): near = lax.ppermute(jnp.where(even, tail, head), axis, swap_pairs(axis, 0))  5.28 us
    all_to_all x1, starting transfers between devices, on_device(): lax.all_to_all(plane, AXES, 0, 0, axis_index_groups=groups_over((1, 3)),...  4.38 us
  transfers between devices with their start and end apart: 11, of which 5 were waited for; matrix products, arithmetic and copies ran while one was open for 3% of the time, Pallas kernels for 13%

profile of v4, /device:TPU:32, one launch (start us, length us, event | category | flops | bytes accessed | tf_op | source)
XLA Modules:
  0.0 95.4 jit_solution(9937370877011502160)
XLA Ops:
  0.7 0.9 fusion.44
  1.6 0.7 fusion.45
  3.0 7.7 %collective-permute-start.1 = (bf16[256,128]{1,0:T(8,128)(2,1)S(1)}, bf16[256,128]{1,0:T(8,128)(2,1)S(1)}, u32[]{:S(2)}, u32[]{:S(2)}) collective-permute-start(bf16[256,128]{1,0:T(8,128)(2,1)S(1)} %get-tuple-element.58), channel_id=1, source_target_pairs={{0,16},{16,0},{32,48},{48,32},{64,80},{80,64},{96,112},{112,96},{1... | collective-permute-start | bytes 196616 | tf_op jit(solution)/shard_map/ppermute | solution.py:37
  10.8 0.8 fusion.34.order
  12.3 5.4 %collective-permute-start.2 = (bf16[336,128]{1,0:T(8,128)(2,1)S(1)}, bf16[336,128]{1,0:T(8,128)(2,1)S(1)}, u32[]{:S(2)}, u32[]{:S(2)}) collective-permute-start(bf16[336,128]{1,0:T(8,128)(2,1)S(1)} %get-tuple-element.53), channel_id=1, source_target_pairs={{1,2},{2,1},{3,4},{4,3},{5,6},{6,5},{7,8},{8,7},{9,10},{10,9},{11,... | collective-permute-start | bytes 258056 | tf_op jit(solution)/shard_map/ppermute | solution.py:36
  17.9 3.3 %collective-permute-done.2 = bf16[336,128]{1,0:T(8,128)(2,1)S(1)} collective-permute-done((bf16[336,128]{1,0:T(8,128)(2,1)S(1)}, bf16[336,128]{1,0:T(8,128)(2,1)S(1)}, u32[]{:S(2)}, u32[]{:S(2)}) %collective-permute-start.2) | collective-permute-done | bytes 86048 | tf_op jit(solution)/shard_map/ppermute | solution.py:36
  21.2 1.7 %collective-permute-done.3 = bf16[336,128]{1,0:T(8,128)(2,1)S(1)} collective-permute-done((bf16[336,128]{1,0:T(8,128)(2,1)S(1)}, bf16[336,128]{1,0:T(8,128)(2,1)S(1)}, u32[]{:S(2)}, u32[]{:S(2)}) %collective-permute-start.3) | collective-permute-done | bytes 86048 | tf_op jit(solution)/shard_map/ppermute | solution.py:37
  23.3 1.2 %fusion.11 = bf16[4,22,24,128]{3,2,1,0:T(8,128)(2,1)} fusion(bf16[4,22,3,128]{3,2,1,0:T(4,128)(2,1)S(1)} %reshape.229, bf16[4,22,3,128]{3,2,1,0:T(4,128)(2,1)S(1)} %reshape.228, bf16[4,3,16,128]{3,2,1,0:T(8,128)(2,1)S(1)} %bitcast.58, bf16[4,16,16,128]{3,2,1,0:T(8,128)(2,1)S(1)} %copy-done.17, bf16[4,3,16,128]{3,2,1,0:T(8,128)(2,1)S(1)} %bitcast.56), kind=kLoop, calls=%fused_computation.14 | loop fusion | flops 4325376 | bytes 1036288 | tf_op jit(solution)/shard_map/concatenate | solution.py:44
  24.7 9.8 %shard_map.94 = (bf16[128,3456]{1,0:T(8,128)(2,1)}, bf16[128,3456]{1,0:T(8,128)(2,1)}, bf16[4,480,128]{2,1,0:T(8,128)(2,1)S(1)}, f32[4,480,128]{2,1,0:T(8,128)},...) custom-call(bf16[4,528,128]{2,1,0:T(8,128)(2,1)} %bitcast.54, ...), custom_call_target="tpu_custom_call" | custom-call | tf_op jit(solution)/shard_map/pallas_call | solution.py:343
  34.4 0.8 copy-done.5
  35.2 0.8 copy-done.7
  38.2 1.0 %copy-done.6 = f32[4,256,128]{2,1,0:T(8,128)S(1)} copy-done((f32[4,256,128]{2,1,0:T(8,128)S(1)}, f32[4,256,128]{2,1,0:T(8,128)}, u32[]{:S(2)}) %copy-start.6) | copy-done | bytes 524312
  39.2 0.9 copy-done.14
  40.2 2.9 %shard_map.96 = (bf16[4,256,128]{2,1,0:T(8,128)(2,1)S(1)}, bf16[2,8,8,256]{3,2,1,0:T(8,128)(2,1)S(1)}) custom-call(bf16[4,432,128]{2,1,0:T(8,128)(2,1)S(1)} %bitcast.44, f32[4,256,128]{2,1,0:T(8,128)S(1)} %copy-done.6, f32[2,128,256]{2,1,0:T(8,128)S(1)} %copy-done.14, bf16[27,256,128]{2,1,0:T(8,128)(2,1)S(1)} %copy-done, bf16[256,1024]{1,0:T(8,128)(2,1)S(1)} %copy-done.2), custom_call_target="tpu_custom_call" | custom-call | tf_op jit(solution)/shard_map/pallas_call | solution.py:343
  43.1 2.3 %shard_map.95 = bf16[128,3456]{1,0:T(8,128)(2,1)} custom-call(bf16[128,3456]{1,0:T(8,128)(2,1)S(1)} %copy-done.4, bf16[128,3456]{1,0:T(8,128)(2,1)} %collective-permute-done.4.other), custom_call_target="tpu_custom_call" | custom-call | tf_op jit(solution)/shard_map/pallas_call | solution.py:343
  46.2 8.7 %collective-permute-start.6 = (bf16[192,128]{1,0:T(8,128)(2,1)S(1)}, bf16[192,128]{1,0:T(8,128)(2,1)S(1)}, u32[]{:S(2)}, u32[]{:S(2)}) collective-permute-start(bf16[192,128]{1,0:T(8,128)(2,1)S(1)} %get-tuple-element.68), channel_id=1, source_target_pairs={{0,16},{16,0},{32,48},{48,32},{64,80},{80,64},{96,112},{112,96},{1... | collective-permute-start | bytes 147464 | tf_op jit(solution)/shard_map/ppermute | solution.py:37
  55.1 6.7 %all-to-all-start = ((bf16[16,8,3456]{2,1,0:T(8,128)(2,1)}), bf16[16,8,3456]{2,1,0:T(8,128)(2,1)S(1)}, u32[]{:S(2)}, u32[]{:S(2)}) async-start(bf16[16,8,3456]{2,1,0:T(8,128)(2,1)} %bitcast.28), calls=%async_computation | async-start | bytes 1769472 | tf_op jit(solution)/shard_map/all_to_all | solution.py:469
  63.0 5.6 %collective-permute-start.7 = (bf16[240,128]{1,0:T(8,128)(2,1)S(1)}, bf16[240,128]{1,0:T(8,128)(2,1)S(1)}, u32[]{:S(2)}, u32[]{:S(2)}) collective-permute-start(bf16[240,128]{1,0:T(8,128)(2,1)S(1)} %get-tuple-element.61), channel_id=1, source_target_pairs={{1,2},{2,1},{3,4},{4,3},{5,6},{6,5},{7,8},{8,7},{9,10},{10,9},{11,... | collective-permute-start | bytes 184328 | tf_op jit(solution)/shard_map/ppermute | solution.py:36
  68.7 4.1 %collective-permute-done.7 = bf16[240,128]{1,0:T(8,128)(2,1)S(1)} collective-permute-done((bf16[240,128]{1,0:T(8,128)(2,1)S(1)}, bf16[240,128]{1,0:T(8,128)(2,1)S(1)}, u32[]{:S(2)}, u32[]{:S(2)}) %collective-permute-start.7) | collective-permute-done | bytes 61472 | tf_op jit(solution)/shard_map/ppermute | solution.py:36
  72.8 3.6 %collective-permute-done.8 = bf16[240,128]{1,0:T(8,128)(2,1)S(1)} collective-permute-done((bf16[240,128]{1,0:T(8,128)(2,1)S(1)}, bf16[240,128]{1,0:T(8,128)(2,1)S(1)}, u32[]{:S(2)}, u32[]{:S(2)}) %collective-permute-start.8) | collective-permute-done | bytes 61472 | tf_op jit(solution)/shard_map/ppermute | solution.py:37
  77.1 1.3 %all-to-all-done = bf16[16,8,3456]{2,1,0:T(8,128)(2,1)S(1)} async-done(((bf16[16,8,3456]{2,1,0:T(8,128)(2,1)}), bf16[16,8,3456]{2,1,0:T(8,128)(2,1)S(1)}, u32[]{:S(2)}, u32[]{:S(2)}) %all-to-all-start) | async-done | bytes 884768 | tf_op jit(solution)/shard_map/all_to_all | solution.py:469
  79.1 4.4 %all-to-all-start.1 = ((f32[8,27,128]{2,1,0:T(8,128)}), f32[8,27,128]{2,1,0:T(8,128)S(1)}, u32[]{:S(2)}, u32[]{:S(2)}) async-start(f32[8,27,128]{2,1,0:T(8,128)} %copy.46), calls=%async_computation.1 | async-start | bytes 262144 | tf_op jit(solution)/shard_map/all_to_all | solution.py:474
  84.3 0.8 copy-done.1
  85.2 9.5 %shard_map.97 = (bf16[4,256,128]{2,1,0:T(8,128)(2,1)}, bf16[4,256,128]{2,1,0:T(8,128)(2,1)}) custom-call(bf16[4,480,128]{2,1,0:T(8,128)(2,1)S(1)} %copy-done.8, bf16[4,432,128]{2,1,0:T(8,128)(2,1)S(1)} %bitcast.47, bf16[2,192,256]{2,1,0:T(8,128)(2,1)S(1)} %bitcast.48, bf16[4,432,128]{2,1,0:T(8,128)(2,1)S(1)} %bitcast.46, f32[320,256]{1,0:T(8,128)S(1)} %copy-done.12, ...), custom_call_target="tpu_custom_call" | custom-call | tf_op jit(solution)/shard_map/pallas_call | solution.py:343
  (146 shorter events, 9.1 us)
Async XLA Ops:
  0.6 11.4 %copy-start.17 = (bf16[4,16,16,128]{3,2,1,0:T(8,128)(2,1)S(1)}, bf16[4,16,16,128]{3,2,1,0:T(8,128)(2,1)}, u32[]{:S(2)}) copy-start(bf16[4,16,16,128]{3,2,1,0:T(8,128)(2,1)} %param.7) | copy-start | bytes 786436
  0.6 11.1 %copy-start.18 = (bf16[4,16,16,128]{3,2,1,0:T(8,128)(2,1)S(1)}, bf16[4,16,16,128]{3,2,1,0:T(8,128)(2,1)}, u32[]{:S(2)}) copy-start(bf16[4,16,16,128]{3,2,1,0:T(8,128)(2,1)} %param.13) | copy-start | bytes 786436
  2.3 9.4 %collective-permute-start = (bf16[256,128]{1,0:T(8,128)(2,1)S(1)}, bf16[256,128]{1,0:T(8,128)(2,1)S(1)}, u32[]{:S(2)}, u32[]{:S(2)}) collective-permute-start(bf16[256,128]{1,0:T(8,128)(2,1)S(1)} %get-tuple-element.57), channel_id=1, source_target_pairs={{16,32},{32,16},{48,64},{64,48},{80,96},{96,80},{112,128},{128,112... | collective-permute-start | bytes 196616 | tf_op jit(solution)/shard_map/ppermute | solution.py:36
  3.0 8.7 %collective-permute-start.1 = (bf16[256,128]{1,0:T(8,128)(2,1)S(1)}, bf16[256,128]{1,0:T(8,128)(2,1)S(1)}, u32[]{:S(2)}, u32[]{:S(2)}) collective-permute-start(bf16[256,128]{1,0:T(8,128)(2,1)S(1)} %get-tuple-element.58), channel_id=1, source_target_pairs={{0,16},{16,0},{32,48},{48,32},{64,80},{80,64},{96,112},{112,96},{1... | collective-permute-start | bytes 196616 | tf_op jit(solution)/shard_map/ppermute | solution.py:37
  12.3 8.8 %collective-permute-start.2 = (bf16[336,128]{1,0:T(8,128)(2,1)S(1)}, bf16[336,128]{1,0:T(8,128)(2,1)S(1)}, u32[]{:S(2)}, u32[]{:S(2)}) collective-permute-start(bf16[336,128]{1,0:T(8,128)(2,1)S(1)} %get-tuple-element.53), channel_id=1, source_target_pairs={{1,2},{2,1},{3,4},{4,3},{5,6},{6,5},{7,8},{8,7},{9,10},{10,9},{11,... | collective-permute-start | bytes 258056 | tf_op jit(solution)/shard_map/ppermute | solution.py:36
  17.7 5.1 %collective-permute-start.3 = (bf16[336,128]{1,0:T(8,128)(2,1)S(1)}, bf16[336,128]{1,0:T(8,128)(2,1)S(1)}, u32[]{:S(2)}, u32[]{:S(2)}) collective-permute-start(bf16[336,128]{1,0:T(8,128)(2,1)S(1)} %get-tuple-element.54), channel_id=1, source_target_pairs={{0,1},{1,0},{2,3},{3,2},{4,5},{5,4},{6,7},{7,6},{8,9},{9,8},{10,11... | collective-permute-start | bytes 258056 | tf_op jit(solution)/shard_map/ppermute | solution.py:37
  23.0 1.6 %copy-start.2 = (bf16[256,1024]{1,0:T(8,128)(2,1)S(1)}, bf16[256,1024]{1,0:T(8,128)(2,1)}, u32[]{:S(2)}) copy-start(bf16[256,1024]{1,0:T(8,128)(2,1)} %w_up_in.3) | copy-start | bytes 1572868
  23.0 1.6 %copy-start.3 = (bf16[1024,256]{1,0:T(8,128)(2,1)S(1)}, bf16[1024,256]{1,0:T(8,128)(2,1)}, u32[]{:S(2)}) copy-start(bf16[1024,256]{1,0:T(8,128)(2,1)} %w_down_in.3) | copy-start | bytes 1572868
  24.7 13.5 %copy-start = (bf16[27,256,128]{2,1,0:T(8,128)(2,1)S(1)}, bf16[27,256,128]{2,1,0:T(8,128)(2,1)}, u32[]{:S(2)}) copy-start(bf16[27,256,128]{2,1,0:T(8,128)(2,1)} %w_last_in.1) | copy-start | bytes 5308420
  38.1 4.9 %collective-permute-start.4 = (bf16[128,3456]{1,0:T(8,128)(2,1)}, bf16[128,3456]{1,0:T(8,128)(2,1)}, u32[]{:S(2)}, u32[]{:S(2)}) collective-permute-start(bf16[128,3456]{1,0:T(8,128)(2,1)} %get-tuple-element.21), channel_id=1, source_target_pairs={{0,16},{16,0},{32,48},{48,32},{64,80},{80,64},{96,112},{112,96},{1... | collective-permute-start | bytes 2654216 | tf_op jit(solution)/shard_map/ppermute | solution.py:439
  38.2 1.0 %copy-start.6 = (f32[4,256,128]{2,1,0:T(8,128)S(1)}, f32[4,256,128]{2,1,0:T(8,128)}, u32[]{:S(2)}) copy-start(f32[4,256,128]{2,1,0:T(8,128)} %copy-done.5) | copy-start | bytes 1572868
  39.2 0.9 copy-start.14
  40.2 2.9 %copy-start.4 = (bf16[128,3456]{1,0:T(8,128)(2,1)S(1)}, bf16[128,3456]{1,0:T(8,128)(2,1)}, u32[]{:S(2)}) copy-start(bf16[128,3456]{1,0:T(8,128)(2,1)} %get-tuple-element.20.one) | copy-start | bytes 2654212
  43.0 2.4 %copy-start.15 = (bf16[2,8,8,256]{3,2,1,0:T(8,128)(2,1)}, bf16[2,8,8,256]{3,2,1,0:T(8,128)(2,1)S(1)}, u32[]{:S(2)}) copy-start(bf16[2,8,8,256]{3,2,1,0:T(8,128)(2,1)S(1)} %get-tuple-element.29) | copy-start | bytes 196612
  43.1 2.4 %copy-start.10 = (bf16[4,256,128]{2,1,0:T(8,128)(2,1)S(1)}, bf16[4,256,128]{2,1,0:T(8,128)(2,1)}, u32[]{:S(2)}) copy-start(bf16[4,256,128]{2,1,0:T(8,128)(2,1)} %copy-done.9) | copy-start | bytes 786436
  45.5 16.3 %collective-permute-start.5 = (bf16[192,128]{1,0:T(8,128)(2,1)S(1)}, bf16[192,128]{1,0:T(8,128)(2,1)S(1)}, u32[]{:S(2)}, u32[]{:S(2)}) collective-permute-start(bf16[192,128]{1,0:T(8,128)(2,1)S(1)} %get-tuple-element.67), channel_id=1, source_target_pairs={{16,32},{32,16},{48,64},{64,48},{80,96},{96,80},{112,128},{128,112... | collective-permute-start | bytes 147464 | tf_op jit(solution)/shard_map/ppermute | solution.py:36
  46.2 15.7 %collective-permute-start.6 = (bf16[192,128]{1,0:T(8,128)(2,1)S(1)}, bf16[192,128]{1,0:T(8,128)(2,1)S(1)}, u32[]{:S(2)}, u32[]{:S(2)}) collective-permute-start(bf16[192,128]{1,0:T(8,128)(2,1)S(1)} %get-tuple-element.68), channel_id=1, source_target_pairs={{0,16},{16,0},{32,48},{48,32},{64,80},{80,64},{96,112},{112,96},{1... | collective-permute-start | bytes 147464 | tf_op jit(solution)/shard_map/ppermute | solution.py:37
  55.1 23.2 %all-to-all-start = ((bf16[16,8,3456]{2,1,0:T(8,128)(2,1)}), bf16[16,8,3456]{2,1,0:T(8,128)(2,1)S(1)}, u32[]{:S(2)}, u32[]{:S(2)}) async-start(bf16[16,8,3456]{2,1,0:T(8,128)(2,1)} %bitcast.28), calls=%async_computation | async-start | bytes 1769472 | tf_op jit(solution)/shard_map/all_to_all | solution.py:469
  63.0 9.9 %collective-permute-start.7 = (bf16[240,128]{1,0:T(8,128)(2,1)S(1)}, bf16[240,128]{1,0:T(8,128)(2,1)S(1)}, u32[]{:S(2)}, u32[]{:S(2)}) collective-permute-start(bf16[240,128]{1,0:T(8,128)(2,1)S(1)} %get-tuple-element.61), channel_id=1, source_target_pairs={{1,2},{2,1},{3,4},{4,3},{5,6},{6,5},{7,8},{8,7},{9,10},{10,9},{11,... | collective-permute-start | bytes 184328 | tf_op jit(solution)/shard_map/ppermute | solution.py:36
  68.5 7.9 %collective-permute-start.8 = (bf16[240,128]{1,0:T(8,128)(2,1)S(1)}, bf16[240,128]{1,0:T(8,128)(2,1)S(1)}, u32[]{:S(2)}, u32[]{:S(2)}) collective-permute-start(bf16[240,128]{1,0:T(8,128)(2,1)S(1)} %get-tuple-element.62), channel_id=1, source_target_pairs={{0,1},{1,0},{2,3},{3,2},{4,5},{5,4},{6,7},{7,6},{8,9},{9,8},{10,11... | collective-permute-start | bytes 184328 | tf_op jit(solution)/shard_map/ppermute | solution.py:37
  79.1 15.6 %all-to-all-start.1 = ((f32[8,27,128]{2,1,0:T(8,128)}), f32[8,27,128]{2,1,0:T(8,128)S(1)}, u32[]{:S(2)}, u32[]{:S(2)}) async-start(f32[8,27,128]{2,1,0:T(8,128)} %copy.46), calls=%async_computation.1 | async-start | bytes 262144 | tf_op jit(solution)/shard_map/all_to_all | solution.py:474
  83.9 1.2 %copy-start.1 = (bf16[27,128,128]{2,1,0:T(8,128)(2,1)S(1)}, bf16[27,128,128]{2,1,0:T(8,128)(2,1)}, u32[]{:S(2)}) copy-start(bf16[27,128,128]{2,1,0:T(8,128)(2,1)} %w_first_in.1) | copy-start | bytes 2654212
  83.9 1.3 %copy-start.8 = (bf16[4,480,128]{2,1,0:T(8,128)(2,1)S(1)}, bf16[4,480,128]{2,1,0:T(8,128)(2,1)}, u32[]{:S(2)}) copy-start(bf16[4,480,128]{2,1,0:T(8,128)(2,1)} %copy-done.7) | copy-start | bytes 1474564
  83.9 1.4 %copy-start.12 = (f32[320,256]{1,0:T(8,128)S(1)}, f32[320,256]{1,0:T(8,128)}, u32[]{:S(2)}) copy-start(f32[320,256]{1,0:T(8,128)} %copy-done.11) | copy-start | bytes 983044
  (6 other events, 4.6 us)

commit v5 on v4

--- a/solution.py
+++ b/solution.py
@@ -145,6 +145,9 @@
 PAIRS = ((0, (0, 1, 2)), (2, (1, 2, 3)))
 
 
+AT_FIRST, AT_SKIP, AT_COARSE, AT_MIDDLE, AT_UP, KEPT = 0, 960, 1920, 2240, 2496, 3008
+
+
 def fetch(sems, *pairs):
     copies = []
     for i, (source, target) in enumerate(pairs):
@@ -156,9 +159,10 @@
 
 def forward_kernel(
     volume, cot, mask, order, w_first_in, w_down_in, w_middle_in, w_up_in,
-    send, keep, skip_out, pre_first_out, pre_coarse, pre_middle, pre_up, upward,
+    send_out, keep_out, kept_out,
     vol_flat, vol_cols, vol_odd, skip, blocked, coarse, coarse_cols, cot_flat, cot_cols, joined, joined_t,
-    pre_first, w_first, w_down, w_middle, w_up, sems, out_sems,
+    send, keep, kept, pre_up,
+    w_first, w_down, w_middle, w_up, sems, out_sems,
 ):
     depth = 4
     rows = 20 * WIDE
@@ -176,6 +180,15 @@
     inner = mask[...] > 0.0
     arrive[0].wait()
     leave = []
+
+    def put(source, target):
+        copy = pltpu.make_async_copy(source, target, out_sems.at[len(leave)])
+        copy.start()
+        leave.append(copy)
+
+    def put_rows(start, count):
+        put(kept.at[pl.ds(start, count), :], kept_out.at[pl.ds(start, count), :])
+
     for first, planes in PAIRS:
         pieces = []
         for p in planes:
@@ -183,11 +196,11 @@
             pieces.append(vol_odd[p])
             pieces.append(vol_cols[p, pl.ds(2 * WIDE, rows), :])
         both = dot(jnp.concatenate(pieces, axis=1), pair_weight(w_first, first, planes))
+        kept[pl.ds(AT_FIRST + first // 2 * rows, rows), :] = both
         for z, pre in ((first, both[:, :ONE]), (first + 1, both[:, ONE:])):
-            pre_first[z] = pre
-            act = jnp.where(inner, silu(pre), 0.0).astype(BF)
-            skip_out[z] = act
-            skip[z, pl.ds(0, rows), :] = act.astype(F32)
+            act = jnp.where(inner, silu(pre), 0.0).astype(BF).astype(F32)
+            kept[pl.ds(AT_SKIP + first // 2 * rows, rows), lanes(z % 2)] = act
+            skip[z, pl.ds(0, rows), :] = act
             skip[z, pl.ds(rows, 8), :] = jnp.zeros((8, ONE), F32)
             for y in range(16):
                 joined[pl.ds(z * 256 + y * 16, 16), lanes(0)] = skip[
@@ -200,11 +213,10 @@
                         blocked[
                             pl.ds((z // 2) * 160 + y * 16, 16), lanes(4 * (z % 2) + 2 * b + c)
                         ] = skip[z, pl.ds(start, 16, stride=2), :].astype(BF)
-    leave.append(pltpu.make_async_copy(pre_first, pre_first_out, out_sems.at[0]))
-    leave[-1].start()
+    put_rows(AT_FIRST, AT_COARSE - AT_FIRST)
     arrive[1].wait()
     pre = dot(blocked[...], w_down[...])
-    pre_coarse[...] = pre
+    kept[pl.ds(AT_COARSE, 320), :] = pre
     act = silu(pre).astype(BF).astype(F32)
     for z in range(2):
         coarse[z, pl.ds(0, 160), :] = act[z * 160 : (z + 1) * 160]
@@ -214,8 +226,8 @@
     arrive[2].wait()
     for z in range(2):
         weight = w_middle[pl.ds((1 - z) * 9 * TWO, 18 * TWO), :]
-        pre_middle[z] = dot(taps(coarse_cols, (0, 1), 128, 16, False), weight)
-    middle = silu(pre_middle[...]).astype(BF).reshape(256, TWO)
+        kept[pl.ds(AT_MIDDLE + z * 128, 128), :] = dot(taps(coarse_cols, (0, 1), 128, 16, False), weight)
+    middle = silu(kept[pl.ds(AT_MIDDLE, 256), :]).astype(BF)
     arrive[3].wait()
     for k in range(8):
         a, b, c = k // 4, k // 2 % 2, k % 2
@@ -226,9 +238,10 @@
                     z * 128 + y * 16 : z * 128 + y * 16 + 8
                 ]
     for z in range(depth):
-        act = silu(pre_up[z]).astype(BF)
-        upward[z] = act
-        joined[pl.ds(z * 256, 256), lanes(1)] = act
+        pre = pre_up[z]
+        kept[pl.ds(AT_UP + z // 2 * 256, 256), lanes(z % 2)] = pre
+        joined[pl.ds(z * 256, 256), lanes(1)] = silu(pre).astype(BF)
+    put_rows(AT_COARSE, KEPT - AT_COARSE)
     joined_t[...] = dot_t(order[...], joined[...]).astype(BF)
     for oz in (-1, 0, 1):
         low, high = max(0, oz), min(depth, depth + oz)
@@ -239,26 +252,33 @@
         at = pl.ds((oz + 1) * 9 * ONE, 9 * ONE)
         send[:, at] = part[:128]
         keep[:, at] = part[128:]
+        put(send.at[:, at], send_out.at[:, at])
+        put(keep.at[:, at], keep_out.at[:, at])
     for copy in leave:
         copy.wait()
 
 
 def cot_kernel(
-    cot, pre_up, pre_middle, w_last_in, w_up_in,
-    grad_skip, grad_middle,
-    cot_flat, cot_cols, grad_up, blocked, w_last, w_up, sems,
+    cot, kept_in, w_last_in, w_up_in,
+    upward, grad_skip, grad_middle,
+    cot_flat, cot_cols, grad_up, blocked, w_last, w_up, kept, sems,
 ):
-    arrive = fetch(sems, (w_last_in, w_last), (w_up_in, w_up))
+    arrive = fetch(
+        sems, (w_last_in, w_last), (w_up_in, w_up), (kept_in.at[pl.ds(AT_MIDDLE, KEPT - AT_MIDDLE), :], kept)
+    )
     for z in range(4):
         cot_flat[z] = cot[z].astype(F32)
         spread(cot_flat, z, cot_cols, (2, 1, 0), 18)
     arrive[0].wait()
+    arrive[2].wait()
     for z in range(4):
         low, high = max(0, z - 1), min(4, z + 2)
         matrix = taps(cot_cols, range(high - 1, low - 1, -1), 256, 16, True)
         both = dot_t(matrix, side_by_side(w_last, z - high + 2, z - low + 2)).astype(BF)
         grad_skip[z] = both[:, :ONE]
-        grad_up[z] = (both[:, ONE:].astype(F32) * slope(pre_up[z])).astype(BF).astype(F32)
+        pre = kept[pl.ds(AT_UP - AT_MIDDLE + z // 2 * 256, 256), lanes(z % 2)]
+        upward[z] = silu(pre).astype(BF)
+        grad_up[z] = (both[:, ONE:].astype(F32) * slope(pre)).astype(BF).astype(F32)
         for b in range(2):
             for c in range(2):
                 for y in range(8):
@@ -270,32 +290,35 @@
     for z in range(2):
         for y in range(8):
             grad_middle[z, y] = (
-                back[z * 64 + y * 8 : z * 64 + y * 8 + 8] * slope(pre_middle[z, pl.ds(y * 16, 8), :])
+                back[z * 64 + y * 8 : z * 64 + y * 8 + 8] * slope(kept[pl.ds(z * 128 + y * 16, 8), :])
             ).astype(BF)
 
 
 def back_kernel(
-    skip, up, grad_mid, grad_skip, pre_coarse, pre_first_in, mask, w_last_in, w_middle_in, w_down_in, w_first_in,
+    kept_in, up, grad_mid, grad_skip, mask, w_last_in, w_middle_in, w_down_in, w_first_in,
     logits, grad_volume,
-    skip_flat, up_flat, join_cols, mid_flat, mid_cols, down, first_flat, cols,
-    pre_first, w_last, w_middle, w_down, w_first, sems,
+    up_flat, join_cols, mid_flat, mid_cols, down, first_flat, cols,
+    kept, w_last, w_middle, w_down, w_first, sems,
 ):
+    def rows_of(start, end):
+        return kept_in.at[pl.ds(start, end - start), :], kept.at[pl.ds(start, end - start), :]
+
     arrive = fetch(
-        sems, (w_last_in, w_last), (w_middle_in, w_middle), (w_down_in, w_down), (w_first_in, w_first),
-        (pre_first_in, pre_first),
-    )
+        sems, rows_of(AT_SKIP, AT_COARSE), (w_last_in, w_last), (w_middle_in, w_middle),
+        rows_of(AT_COARSE, AT_MIDDLE), (w_down_in, w_down), rows_of(AT_FIRST, AT_SKIP), (w_first_in, w_first),
+    )
+    arrive[0].wait()
     for z in range(4):
-        skip_flat[...] = skip[z].astype(F32)
         up_flat[...] = up[z].astype(F32)
         for y in range(18):
             for i in range(3):
-                join_cols[z, pl.ds(y * 16, 16), lanes(2 * i)] = skip_flat[
-                    pl.ds((y + 1) * WIDE + 1 + i, 16), :
+                join_cols[z, pl.ds(y * 16, 16), lanes(2 * i)] = kept[
+                    pl.ds(AT_SKIP + z // 2 * 480 + (y + 1) * WIDE + 1 + i, 16), lanes(z % 2)
                 ].astype(BF)
                 join_cols[z, pl.ds(y * 16, 16), lanes(2 * i + 1)] = up_flat[
                     pl.ds(y * WIDE + i, 16), :
                 ].astype(BF)
-    arrive[0].wait()
+    arrive[1].wait()
     for first, planes in PAIRS:
         both = dot(taps(join_cols, planes, 256, 16, False), pair_weight(w_last, first, planes)).astype(BF)
         logits[first] = both[:, :ONE]
@@ -305,11 +328,12 @@
         mid_flat[z, pl.ds(192, 8), :] = jnp.zeros((8, TWO), F32)
         for i in range(3):
             mid_cols[z, :, lanes(i, TWO)] = mid_flat[z, pl.ds(2 - i, 192), :].astype(BF)
-    arrive[1].wait()
     arrive[2].wait()
+    arrive[3].wait()
+    arrive[4].wait()
     for z in range(2):
         back = dot_t(taps(mid_cols, (1, 0), 160, 16, True), side_by_side(w_middle, z, z + 2))
-        coarse = (back * slope(pre_coarse[pl.ds(z * 160, 160), :])).astype(BF)
+        coarse = (back * slope(kept[pl.ds(AT_COARSE + z * 160, 160), :])).astype(BF)
         for k in range(8):
             a, b, c = k // 4, k // 2 % 2, k % 2
             part = dot_t(coarse, w_down[lanes(k), :])
@@ -318,13 +342,14 @@
                 down[2 * z + a, pl.ds(start, 8, stride=2), :] = part[y * 16 : y * 16 + 8]
                 down[2 * z + a, pl.ds(start + 16, 4, stride=2), :] = part[y * 16 + 8 : y * 16 + 12]
     inner = mask[...] > 0.0
-    arrive[4].wait()
+    arrive[5].wait()
     for z in range(4):
         rows = pl.ds(WIDE + 1, 18 * WIDE)
-        value = (grad_skip[z].astype(F32) + down[z, rows, :]) * slope(pre_first[z, rows, :])
+        pre = kept[pl.ds(AT_FIRST + z // 2 * 480 + WIDE + 1, 18 * WIDE), lanes(z % 2)]
+        value = (grad_skip[z].astype(F32) + down[z, rows, :]) * slope(pre)
         first_flat[z] = jnp.where(inner, value, 0.0).astype(BF).astype(F32)
         spread(first_flat, z, cols, (2, 1, 0), 18)
-    arrive[3].wait()
+    arrive[6].wait()
     for first, planes in PAIRS:
         both = dot_t(taps(cols, planes, 256, 16, True), pair_weight_t(w_first, first, planes)).astype(BF)
         grad_volume[first] = both[:, :ONE]
@@ -336,7 +361,7 @@
 
 
 VMEM = pl.BlockSpec(memory_space=pltpu.VMEM)
-ANY = pl.BlockSpec(memory_space=pl.ANY)
+HBM = pl.BlockSpec(memory_space=pltpu.HBM)
 
 
 def call(kernel, outs, scratch, in_specs, out_specs, *args):
@@ -357,50 +382,49 @@
     return call(
         forward_kernel,
         [
-            ((128, 27 * ONE), BF), ((128, 27 * ONE), BF), ((4, 480, ONE), BF), ((4, 480, ONE), F32),
-            ((320, TWO), F32), ((2, 128, TWO), F32), ((4, 256, ONE), F32), ((4, 256, ONE), BF),
+            ((128, 27 * ONE), BF), ((128, 27 * ONE), BF), ((KEPT, TWO), F32),
         ],
         [
             ((4, 536, ONE), F32), ((4, 528, 3 * ONE), BF), ((4, 480, 3 * ONE), BF), ((4, 488, ONE), F32),
             ((320, 8 * ONE), BF), ((2, 168, TWO), F32), ((2, 160, 3 * TWO), BF), ((4, 432, ONE), F32),
-            ((4, 288, 3 * ONE), BF), ((1024, TWO), BF), ((TWO, 1024), BF), ((4, 480, ONE), F32),
+            ((4, 288, 3 * ONE), BF), ((1024, TWO), BF), ((TWO, 1024), BF),
+            ((128, 27 * ONE), BF), ((128, 27 * ONE), BF), ((KEPT, TWO), F32), ((4, 256, ONE), F32),
             ((27 * ONE, ONE), BF), ((8 * ONE, TWO), BF), ((27 * TWO, TWO), BF), ((TWO, 8 * ONE), BF),
-            (4, None), (1, None),
+            (4, None), (8, None),
         ],
-        [VMEM] * 4 + [ANY] * 4,
-        [VMEM] * 3 + [ANY] + [VMEM] * 4,
+        [VMEM] * 4 + [HBM] * 4,
+        [HBM] * 3,
         volume_ext, cot_ext, mask, order, w_first.reshape(-1, ONE), w_down, w_middle.reshape(-1, TWO), w_up,
     )
 
 
-def run_cot(cot_ext, pre_up, pre_middle, w_last, w_up):
+def run_cot(cot_ext, kept, w_last, w_up):
     return call(
         cot_kernel,
-        [((4, 256, ONE), BF), ((2, 8, 8, TWO), BF)],
+        [((4, 256, ONE), BF), ((4, 256, ONE), BF), ((2, 8, 8, TWO), BF)],
         [
             ((4, 432, ONE), F32), ((4, 288, 3 * ONE), BF), ((4, 256, ONE), F32), ((128, 8 * ONE), F32),
-            ((27, TWO, ONE), BF), ((TWO, 8 * ONE), BF), (2, None),
+            ((27, TWO, ONE), BF), ((TWO, 8 * ONE), BF), ((KEPT - AT_MIDDLE, TWO), F32), (3, None),
         ],
-        [VMEM] * 3 + [ANY] * 2,
-        [VMEM] * 2,
-        cot_ext, pre_up, pre_middle, w_last, w_up,
-    )
-
-
-def run_back(skip, up_ext, middle_ext, skip_ext, pre_coarse, pre_first, mask, w_last, w_middle, w_down, w_first):
+        [VMEM] + [HBM] * 3,
+        [VMEM] * 3,
+        cot_ext, kept, w_last, w_up,
+    )
+
+
+def run_back(kept, up_ext, middle_ext, skip_ext, mask, w_last, w_middle, w_down, w_first):
     return call(
         back_kernel,
         [((4, 256, ONE), BF), ((4, 256, ONE), BF)],
         [
-            ((480, ONE), F32), ((432, ONE), F32), ((4, 288, 3 * TWO), BF),
+            ((432, ONE), F32), ((4, 288, 3 * TWO), BF),
             ((2, 200, TWO), F32), ((2, 192, 3 * TWO), BF), ((4, 480, ONE), F32), ((4, 432, ONE), F32),
-            ((4, 288, 3 * ONE), BF), ((4, 480, ONE), F32),
-            ((27 * TWO, ONE), BF), ((27, TWO, TWO), BF), ((8 * ONE, TWO), BF), ((27, ONE, ONE), BF), (5, None),
+            ((4, 288, 3 * ONE), BF), ((AT_MIDDLE, TWO), F32),
+            ((27 * TWO, ONE), BF), ((27, TWO, TWO), BF), ((8 * ONE, TWO), BF), ((27, ONE, ONE), BF), (7, None),
         ],
-        [VMEM] * 5 + [ANY, VMEM] + [ANY] * 4,
+        [HBM] + [VMEM] * 4 + [HBM] * 4,
         [VMEM] * 2,
-        skip, up_ext, middle_ext, skip_ext, pre_coarse, pre_first, mask,
-        w_last.reshape(-1, ONE), w_middle, w_down, w_first,
+        kept, up_ext, middle_ext, skip_ext, mask, w_last.reshape(-1, ONE), w_middle, w_down, w_first,
     )
 
 
@@ -456,11 +480,11 @@
 
     volume_ext, cot_ext = with_halos([volume, cotangent], (3, 1))
     cot_ext = widen(cot_ext, WIDE)
-    send, keep, skip, pre_first, pre_coarse, pre_middle, pre_up, upward = run_forward(
+    send, keep, kept = run_forward(
         widen(volume_ext, WIDE), cot_ext, flat_mask(2, extent), send_order(), w_first, w_down, w_middle, w_up
     )
     got = core_swap(send)
-    grad_skip, grad_middle = run_cot(cot_ext, pre_up, pre_middle, w_last, w_up)
+    upward, grad_skip, grad_middle = run_cot(cot_ext, kept, w_last, w_up)
     pair = run_pair(keep, got)
     pair, upward, grad_skip, grad_middle = lax.optimization_barrier(
         (pair, upward, grad_skip, grad_middle)
@@ -473,8 +497,7 @@
     plane = pair.astype(F32).sum(0).reshape(8, 27, one)
     plane = lax.all_to_all(plane, AXES, 0, 0, axis_index_groups=groups_over((1, 3)), tiled=True)
     logits, grad_volume = run_back(
-        skip, widen(up_ext, WIDE), widen(middle_ext, COARSE), widen(skip_ext, WIDE), pre_coarse, pre_first,
-        flat_mask(1, extent), w_last, w_middle, w_down, w_first,
+        kept, widen(up_ext, WIDE), widen(middle_ext, COARSE), widen(skip_ext, WIDE), flat_mask(1, extent), w_last, w_middle, w_down, w_first,
     )
     scale = 1.0 / math.sqrt(
         depth * rows * cols * lax.axis_size("gx") * lax.axis_size("gy")

time: 96 us -> 90.4 us (0.942)
  local copies, waits for them, and re-layouts: 11.2 us -> 6.43 us
    unnamed x48 -> x32, local copies, waits for them, and re-layouts: 7.53 us -> 2.72 us
  transfers between devices with their start and end apart: 11 -> 11, of which waited for: 5 -> 5; matrix products, arithmetic and copies ran while one was open for 3% -> 3% of each run, Pallas kernels for 13% -> 15%
where the time goes in v5:
time: 90.4 us; the launch traced here: 89.8 us
  starting transfers between devices  40.1 us (44%)
  Pallas kernels  24.4 us (27%)
  waiting for transfers between devices  13.9 us (15%)
  local copies, waits for them, and re-layouts  6.43 us (7%)
  other arithmetic  3.46 us (4%)
  between operations  1.49 us (2%)
    pallas_call x4, Pallas kernels, call(): pl.pallas_call(kernel, out_shape=[jax.ShapeDtypeStruct(shape, kind) for s...  24.4 us
    ppermute x4, starting transfers between devices, exchange(): near = lax.ppermute(jnp.where(even, tail, head), axis, swap_pairs(axis, 0))  16.6 us
    ppermute x4, starting transfers between devices, exchange(): far = lax.ppermute(jnp.where(even, head, tail), axis, swap_pairs(axis, 1))  12.3 us
    ppermute x4, waiting for transfers between devices, exchange(): far = lax.ppermute(jnp.where(even, head, tail), axis, swap_pairs(axis, 1))  7.33 us
    all_to_all x1, starting transfers between devices, on_device(): lax.all_to_all(pair, AXES, 0, 0, axis_index_groups=groups_over((0, 4)), t...  6.7 us
    ppermute x4, waiting for transfers between devices, exchange(): near = lax.ppermute(jnp.where(even, tail, head), axis, swap_pairs(axis, 0))  5.32 us
    all_to_all x1, starting transfers between devices, on_device(): lax.all_to_all(plane, AXES, 0, 0, axis_index_groups=groups_over((1, 3)),...  4.38 us
    unnamed x32, local copies, waits for them, and re-layouts  2.72 us
  transfers between devices with their start and end apart: 11, of which 5 were waited for; matrix products, arithmetic and copies ran while one was open for 3% of the time, Pallas kernels for 15%

profile of v5, /device:TPU:32, one launch (start us, length us, event | category | flops | bytes accessed | tf_op | source)
XLA Modules:
  0.0 89.8 jit_solution(8359396298743411619)
XLA Ops:
  0.7 0.8 fusion.45
  1.5 0.8 fusion.44
  2.3 0.7 collective-permute-start
  3.0 7.7 %collective-permute-start.1 = (bf16[256,128]{1,0:T(8,128)(2,1)S(1)}, bf16[256,128]{1,0:T(8,128)(2,1)S(1)}, u32[]{:S(2)}, u32[]{:S(2)}) collective-permute-start(bf16[256,128]{1,0:T(8,128)(2,1)S(1)} %get-tuple-element.50), channel_id=1, source_target_pairs={{0,16},{16,0},{32,48},{48,32},{64,80},{80,64},{96,112},{112,96},{1... | collective-permute-start | bytes 196616 | tf_op jit(solution)/shard_map/ppermute | solution.py:37
  10.8 0.8 fusion.34.order
  12.3 5.4 %collective-permute-start.2 = (bf16[336,128]{1,0:T(8,128)(2,1)S(1)}, bf16[336,128]{1,0:T(8,128)(2,1)S(1)}, u32[]{:S(2)}, u32[]{:S(2)}) collective-permute-start(bf16[336,128]{1,0:T(8,128)(2,1)S(1)} %get-tuple-element.45), channel_id=1, source_target_pairs={{1,2},{2,1},{3,4},{4,3},{5,6},{6,5},{7,8},{8,7},{9,10},{10,9},{11,... | collective-permute-start | bytes 258056 | tf_op jit(solution)/shard_map/ppermute | solution.py:36
  17.9 3.3 %collective-permute-done.2 = bf16[336,128]{1,0:T(8,128)(2,1)S(1)} collective-permute-done((bf16[336,128]{1,0:T(8,128)(2,1)S(1)}, bf16[336,128]{1,0:T(8,128)(2,1)S(1)}, u32[]{:S(2)}, u32[]{:S(2)}) %collective-permute-start.2) | collective-permute-done | bytes 86048 | tf_op jit(solution)/shard_map/ppermute | solution.py:36
  21.2 1.7 %collective-permute-done.3 = bf16[336,128]{1,0:T(8,128)(2,1)S(1)} collective-permute-done((bf16[336,128]{1,0:T(8,128)(2,1)S(1)}, bf16[336,128]{1,0:T(8,128)(2,1)S(1)}, u32[]{:S(2)}, u32[]{:S(2)}) %collective-permute-start.3) | collective-permute-done | bytes 86048 | tf_op jit(solution)/shard_map/ppermute | solution.py:37
  24.2 8.4 %shard_map.94 = (bf16[128,3456]{1,0:T(8,128)(2,1)}, bf16[128,3456]{1,0:T(8,128)(2,1)}, f32[3008,256]{1,0:T(8,128)}) custom-call(bf16[4,528,128]{2,1,0:T(8,128)(2,1)S(1)} %bitcast.46, bf16[4,432,128]{2,1,0:T(8,128)(2,1)S(1)} %bitcast.43, f32[480,128]{1,0:T(8,128)S(1)} %broadcast_in_dim.4.mask, bf16[256,256]{1,0:T(8,128)(2,1)S(1)} %fusion.34.order, ...), custom_call_target="tpu_custom_call" | custom-call | tf_op jit(solution)/shard_map/pallas_call | solution.py:368
  32.8 3.8 %shard_map.96 = (bf16[4,256,128]{2,1,0:T(8,128)(2,1)S(1)}, bf16[4,256,128]{2,1,0:T(8,128)(2,1)S(1)}, bf16[2,8,8,256]{3,2,1,0:T(8,128)(2,1)S(1)}) custom-call(bf16[4,432,128]{2,1,0:T(8,128)(2,1)S(1)} %bitcast.44, f32[3008,256]{1,0:T(8,128)} %get-tuple-element.15.kept_in, bf16[27,256,128]{2,1,0:T(8,128)(2,1)S(1)} %copy-done, bf16[256,1024]{1,0:T(8,128)(2,1)S(1)} %copy-done.3), custom_call_target="tpu_custom_call" | custom-call | tf_op jit(solution)/shard_map/pallas_call | solution.py:368
  36.6 0.7 copy-done.5
  37.3 2.3 %shard_map.95 = bf16[128,3456]{1,0:T(8,128)(2,1)} custom-call(bf16[128,3456]{1,0:T(8,128)(2,1)S(1)} %copy-done.4, bf16[128,3456]{1,0:T(8,128)(2,1)} %collective-permute-done.4.other), custom_call_target="tpu_custom_call" | custom-call | tf_op jit(solution)/shard_map/pallas_call | solution.py:368
  39.8 0.7 collective-permute-start.5
  40.4 8.7 %collective-permute-start.6 = (bf16[192,128]{1,0:T(8,128)(2,1)S(1)}, bf16[192,128]{1,0:T(8,128)(2,1)S(1)}, u32[]{:S(2)}, u32[]{:S(2)}) collective-permute-start(bf16[192,128]{1,0:T(8,128)(2,1)S(1)} %get-tuple-element.60), channel_id=1, source_target_pairs={{0,16},{16,0},{32,48},{48,32},{64,80},{80,64},{96,112},{112,96},{1... | collective-permute-start | bytes 147464 | tf_op jit(solution)/shard_map/ppermute | solution.py:37
  49.4 6.7 %all-to-all-start = ((bf16[16,8,3456]{2,1,0:T(8,128)(2,1)}), bf16[16,8,3456]{2,1,0:T(8,128)(2,1)S(1)}, u32[]{:S(2)}, u32[]{:S(2)}) async-start(bf16[16,8,3456]{2,1,0:T(8,128)(2,1)} %bitcast.28), calls=%async_computation | async-start | bytes 1769472 | tf_op jit(solution)/shard_map/all_to_all | solution.py:493
  57.2 5.6 %collective-permute-start.7 = (bf16[240,128]{1,0:T(8,128)(2,1)S(1)}, bf16[240,128]{1,0:T(8,128)(2,1)S(1)}, u32[]{:S(2)}, u32[]{:S(2)}) collective-permute-start(bf16[240,128]{1,0:T(8,128)(2,1)S(1)} %get-tuple-element.53), channel_id=1, source_target_pairs={{1,2},{2,1},{3,4},{4,3},{5,6},{6,5},{7,8},{8,7},{9,10},{10,9},{11,... | collective-permute-start | bytes 184328 | tf_op jit(solution)/shard_map/ppermute | solution.py:36
  63.0 4.1 %collective-permute-done.7 = bf16[240,128]{1,0:T(8,128)(2,1)S(1)} collective-permute-done((bf16[240,128]{1,0:T(8,128)(2,1)S(1)}, bf16[240,128]{1,0:T(8,128)(2,1)S(1)}, u32[]{:S(2)}, u32[]{:S(2)}) %collective-permute-start.7) | collective-permute-done | bytes 61472 | tf_op jit(solution)/shard_map/ppermute | solution.py:36
  67.0 3.7 %collective-permute-done.8 = bf16[240,128]{1,0:T(8,128)(2,1)S(1)} collective-permute-done((bf16[240,128]{1,0:T(8,128)(2,1)S(1)}, bf16[240,128]{1,0:T(8,128)(2,1)S(1)}, u32[]{:S(2)}, u32[]{:S(2)}) %collective-permute-start.8) | collective-permute-done | bytes 61472 | tf_op jit(solution)/shard_map/ppermute | solution.py:37
  71.3 1.2 %all-to-all-done = bf16[16,8,3456]{2,1,0:T(8,128)(2,1)S(1)} async-done(((bf16[16,8,3456]{2,1,0:T(8,128)(2,1)}), bf16[16,8,3456]{2,1,0:T(8,128)(2,1)S(1)}, u32[]{:S(2)}, u32[]{:S(2)}) %all-to-all-start) | async-done | bytes 884768 | tf_op jit(solution)/shard_map/all_to_all | solution.py:493
  72.6 0.7 copy.46
  73.3 4.4 %all-to-all-start.1 = ((f32[8,27,128]{2,1,0:T(8,128)}), f32[8,27,128]{2,1,0:T(8,128)S(1)}, u32[]{:S(2)}, u32[]{:S(2)}) async-start(f32[8,27,128]{2,1,0:T(8,128)} %copy.46), calls=%async_computation.1 | async-start | bytes 262144 | tf_op jit(solution)/shard_map/all_to_all | solution.py:498
  78.5 0.8 copy-done.1
  79.2 9.9 %shard_map.97 = (bf16[4,256,128]{2,1,0:T(8,128)(2,1)}, bf16[4,256,128]{2,1,0:T(8,128)(2,1)}) custom-call(f32[3008,256]{1,0:T(8,128)} %get-tuple-element.15.kept_in, bf16[4,432,128]{2,1,0:T(8,128)(2,1)S(1)} %bitcast.47, bf16[2,192,256]{2,1,0:T(8,128)(2,1)S(1)} %bitcast.49, bf16[4,432,128]{2,1,0:T(8,128)(2,1)S(1)} %bitcast.48, ...), custom_call_target="tpu_custom_call" | custom-call | tf_op jit(solution)/shard_map/pallas_call | solution.py:368
  89.2 0.6 broadcast_multiply_fusion
  (130 shorter events, 5.0 us)
Async XLA Ops:
  0.6 11.3 %copy-start.10 = (bf16[4,16,16,128]{3,2,1,0:T(8,128)(2,1)S(1)}, bf16[4,16,16,128]{3,2,1,0:T(8,128)(2,1)}, u32[]{:S(2)}) copy-start(bf16[4,16,16,128]{3,2,1,0:T(8,128)(2,1)} %param.13) | copy-start | bytes 786436
  0.6 11.1 %copy-start.9 = (bf16[4,16,16,128]{3,2,1,0:T(8,128)(2,1)S(1)}, bf16[4,16,16,128]{3,2,1,0:T(8,128)(2,1)}, u32[]{:S(2)}) copy-start(bf16[4,16,16,128]{3,2,1,0:T(8,128)(2,1)} %param.7) | copy-start | bytes 786436
  2.3 9.4 %collective-permute-start = (bf16[256,128]{1,0:T(8,128)(2,1)S(1)}, bf16[256,128]{1,0:T(8,128)(2,1)S(1)}, u32[]{:S(2)}, u32[]{:S(2)}) collective-permute-start(bf16[256,128]{1,0:T(8,128)(2,1)S(1)} %get-tuple-element.49), channel_id=1, source_target_pairs={{16,32},{32,16},{48,64},{64,48},{80,96},{96,80},{112,128},{128,112... | collective-permute-start | bytes 196616 | tf_op jit(solution)/shard_map/ppermute | solution.py:36
  3.0 8.7 %collective-permute-start.1 = (bf16[256,128]{1,0:T(8,128)(2,1)S(1)}, bf16[256,128]{1,0:T(8,128)(2,1)S(1)}, u32[]{:S(2)}, u32[]{:S(2)}) collective-permute-start(bf16[256,128]{1,0:T(8,128)(2,1)S(1)} %get-tuple-element.50), channel_id=1, source_target_pairs={{0,16},{16,0},{32,48},{48,32},{64,80},{80,64},{96,112},{112,96},{1... | collective-permute-start | bytes 196616 | tf_op jit(solution)/shard_map/ppermute | solution.py:37
  12.3 8.8 %collective-permute-start.2 = (bf16[336,128]{1,0:T(8,128)(2,1)S(1)}, bf16[336,128]{1,0:T(8,128)(2,1)S(1)}, u32[]{:S(2)}, u32[]{:S(2)}) collective-permute-start(bf16[336,128]{1,0:T(8,128)(2,1)S(1)} %get-tuple-element.45), channel_id=1, source_target_pairs={{1,2},{2,1},{3,4},{4,3},{5,6},{6,5},{7,8},{8,7},{9,10},{10,9},{11,... | collective-permute-start | bytes 258056 | tf_op jit(solution)/shard_map/ppermute | solution.py:36
  17.7 5.1 %collective-permute-start.3 = (bf16[336,128]{1,0:T(8,128)(2,1)S(1)}, bf16[336,128]{1,0:T(8,128)(2,1)S(1)}, u32[]{:S(2)}, u32[]{:S(2)}) collective-permute-start(bf16[336,128]{1,0:T(8,128)(2,1)S(1)} %get-tuple-element.46), channel_id=1, source_target_pairs={{0,1},{1,0},{2,3},{3,2},{4,5},{5,4},{6,7},{7,6},{8,9},{9,8},{10,11... | collective-permute-start | bytes 258056 | tf_op jit(solution)/shard_map/ppermute | solution.py:37
  23.0 1.0 %copy-start.2 = (bf16[1024,256]{1,0:T(8,128)(2,1)S(1)}, bf16[1024,256]{1,0:T(8,128)(2,1)}, u32[]{:S(2)}) copy-start(bf16[1024,256]{1,0:T(8,128)(2,1)} %w_down_in.3) | copy-start | bytes 1572868
  23.0 1.2 %copy-start.3 = (bf16[256,1024]{1,0:T(8,128)(2,1)S(1)}, bf16[256,1024]{1,0:T(8,128)(2,1)}, u32[]{:S(2)}) copy-start(bf16[256,1024]{1,0:T(8,128)(2,1)} %w_up_in.3) | copy-start | bytes 1572868
  24.2 8.5 %copy-start = (bf16[27,256,128]{2,1,0:T(8,128)(2,1)S(1)}, bf16[27,256,128]{2,1,0:T(8,128)(2,1)}, u32[]{:S(2)}) copy-start(bf16[27,256,128]{2,1,0:T(8,128)(2,1)} %w_last_in.1) | copy-start | bytes 5308420
  32.6 4.7 %collective-permute-start.4 = (bf16[128,3456]{1,0:T(8,128)(2,1)}, bf16[128,3456]{1,0:T(8,128)(2,1)}, u32[]{:S(2)}, u32[]{:S(2)}) collective-permute-start(bf16[128,3456]{1,0:T(8,128)(2,1)} %get-tuple-element.17), channel_id=1, source_target_pairs={{0,16},{16,0},{32,48},{48,32},{64,80},{80,64},{96,112},{112,96},{1... | collective-permute-start | bytes 2654216 | tf_op jit(solution)/shard_map/ppermute | solution.py:463
  32.7 4.6 %copy-start.4 = (bf16[128,3456]{1,0:T(8,128)(2,1)S(1)}, bf16[128,3456]{1,0:T(8,128)(2,1)}, u32[]{:S(2)}) copy-start(bf16[128,3456]{1,0:T(8,128)(2,1)} %get-tuple-element.16.one) | copy-start | bytes 2654212
  36.6 0.7 copy-start.5
  37.3 2.3 %copy-start.7 = (bf16[2,8,8,256]{3,2,1,0:T(8,128)(2,1)}, bf16[2,8,8,256]{3,2,1,0:T(8,128)(2,1)S(1)}, u32[]{:S(2)}) copy-start(bf16[2,8,8,256]{3,2,1,0:T(8,128)(2,1)S(1)} %get-tuple-element.23) | copy-start | bytes 196612
  37.3 2.4 %copy-start.6 = (bf16[4,256,128]{2,1,0:T(8,128)(2,1)S(1)}, bf16[4,256,128]{2,1,0:T(8,128)(2,1)}, u32[]{:S(2)}) copy-start(bf16[4,256,128]{2,1,0:T(8,128)(2,1)} %copy-done.5) | copy-start | bytes 786436
  39.8 16.3 %collective-permute-start.5 = (bf16[192,128]{1,0:T(8,128)(2,1)S(1)}, bf16[192,128]{1,0:T(8,128)(2,1)S(1)}, u32[]{:S(2)}, u32[]{:S(2)}) collective-permute-start(bf16[192,128]{1,0:T(8,128)(2,1)S(1)} %get-tuple-element.59), channel_id=1, source_target_pairs={{16,32},{32,16},{48,64},{64,48},{80,96},{96,80},{112,128},{128,112... | collective-permute-start | bytes 147464 | tf_op jit(solution)/shard_map/ppermute | solution.py:36
  40.4 15.7 %collective-permute-start.6 = (bf16[192,128]{1,0:T(8,128)(2,1)S(1)}, bf16[192,128]{1,0:T(8,128)(2,1)S(1)}, u32[]{:S(2)}, u32[]{:S(2)}) collective-permute-start(bf16[192,128]{1,0:T(8,128)(2,1)S(1)} %get-tuple-element.60), channel_id=1, source_target_pairs={{0,16},{16,0},{32,48},{48,32},{64,80},{80,64},{96,112},{112,96},{1... | collective-permute-start | bytes 147464 | tf_op jit(solution)/shard_map/ppermute | solution.py:37
  49.4 23.1 %all-to-all-start = ((bf16[16,8,3456]{2,1,0:T(8,128)(2,1)}), bf16[16,8,3456]{2,1,0:T(8,128)(2,1)S(1)}, u32[]{:S(2)}, u32[]{:S(2)}) async-start(bf16[16,8,3456]{2,1,0:T(8,128)(2,1)} %bitcast.28), calls=%async_computation | async-start | bytes 1769472 | tf_op jit(solution)/shard_map/all_to_all | solution.py:493
  56.1 0.8 copy-start.8
  57.2 9.9 %collective-permute-start.7 = (bf16[240,128]{1,0:T(8,128)(2,1)S(1)}, bf16[240,128]{1,0:T(8,128)(2,1)S(1)}, u32[]{:S(2)}, u32[]{:S(2)}) collective-permute-start(bf16[240,128]{1,0:T(8,128)(2,1)S(1)} %get-tuple-element.53), channel_id=1, source_target_pairs={{1,2},{2,1},{3,4},{4,3},{5,6},{6,5},{7,8},{8,7},{9,10},{10,9},{11,... | collective-permute-start | bytes 184328 | tf_op jit(solution)/shard_map/ppermute | solution.py:36
  62.8 7.9 %collective-permute-start.8 = (bf16[240,128]{1,0:T(8,128)(2,1)S(1)}, bf16[240,128]{1,0:T(8,128)(2,1)S(1)}, u32[]{:S(2)}, u32[]{:S(2)}) collective-permute-start(bf16[240,128]{1,0:T(8,128)(2,1)S(1)} %get-tuple-element.54), channel_id=1, source_target_pairs={{0,1},{1,0},{2,3},{3,2},{4,5},{5,4},{6,7},{7,6},{8,9},{9,8},{10,11... | collective-permute-start | bytes 184328 | tf_op jit(solution)/shard_map/ppermute | solution.py:37
  73.3 15.8 %all-to-all-start.1 = ((f32[8,27,128]{2,1,0:T(8,128)}), f32[8,27,128]{2,1,0:T(8,128)S(1)}, u32[]{:S(2)}, u32[]{:S(2)}) async-start(f32[8,27,128]{2,1,0:T(8,128)} %copy.46), calls=%async_computation.1 | async-start | bytes 262144 | tf_op jit(solution)/shard_map/all_to_all | solution.py:498
  78.1 1.2 %copy-start.1 = (bf16[27,128,128]{2,1,0:T(8,128)(2,1)S(1)}, bf16[27,128,128]{2,1,0:T(8,128)(2,1)}, u32[]{:S(2)}) copy-start(bf16[27,128,128]{2,1,0:T(8,128)(2,1)} %w_first_in.1) | copy-start | bytes 2654212

commit v6 on v5

--- a/solution.py
+++ b/solution.py
@@ -54,9 +54,10 @@
     return grown
 
 
-def with_halos(fields, widths):
-    fields = exchange(fields, widths, "gx", 1)
-    return exchange(fields, widths, "gy", 2)
+def with_halos(fields, widths, axes=("gx", "gy")):
+    for axis in axes:
+        fields = exchange(fields, widths, axis, 1 if axis == "gx" else 2)
+    return fields
 
 
 def inside(halo, extent):
@@ -478,7 +479,7 @@
     extent = (rows, cols)
     fine = (depth, rows, cols, one)
 
-    volume_ext, cot_ext = with_halos([volume, cotangent], (3, 1))
+    volume_ext, cot_ext = with_halos([volume, cotangent], (3, 1), ("gy", "gx"))
     cot_ext = widen(cot_ext, WIDE)
     send, keep, kept = run_forward(
         widen(volume_ext, WIDE), cot_ext, flat_mask(2, extent), send_order(), w_first, w_down, w_middle, w_up

time: 90.4 us -> 89.5 us (0.990)
  waiting for transfers between devices: 13.9 us -> 11.3 us
  starting transfers between devices: 40.1 us -> 41.3 us
    ppermute x4, waiting for transfers between devices: 7.33 us -> 5.23 us  [exchange(): far = lax.ppermute(jnp.where(even, head, tail), axis, swap_pairs(axis, 1))]
    all_to_all x1, starting transfers between devices: 6.7 us -> 5.41 us  [on_device(): lax.all_to_all(pair, AXES, 0, 0, axis_index_groups=groups_over((0, 4)), t...]
    ppermute x1, starting transfers between devices: 0.09 us -> 1.24 us  [core_swap(): return lax.ppermute(array, 'gx', [(i, i ^ 1) for i in range(count)])]
    all_to_all x1, starting transfers between devices: 4.38 us -> 5.36 us  [on_device(): lax.all_to_all(plane, AXES, 0, 0, axis_index_groups=groups_over((1, 3)),...]
    unnamed x32 -> x34, local copies, waits for them, and re-layouts: 2.72 us -> 2.83 us
  transfers between devices with their start and end apart: 11 -> 11, of which waited for: 5 -> 6; matrix products, arithmetic and copies ran while one was open for 3% -> 3% of each run, Pallas kernels for 15% -> 15%
where the time goes in v6:
time: 89.5 us; the launch traced here: 88.9 us
  starting transfers between devices  41.3 us (46%)
  Pallas kernels  24.5 us (27%)
  waiting for transfers between devices  11.3 us (13%)
  local copies, waits for them, and re-layouts  7.11 us (8%)
  other arithmetic  3.18 us (4%)
  between operations  1.53 us (2%)
    pallas_call x4, Pallas kernels, call(): pl.pallas_call(kernel, out_shape=[jax.ShapeDtypeStruct(shape, kind) for s...  24.5 us
    ppermute x4, starting transfers between devices, exchange(): near = lax.ppermute(jnp.where(even, tail, head), axis, swap_pairs(axis, 0))  16.6 us
    ppermute x4, starting transfers between devices, exchange(): far = lax.ppermute(jnp.where(even, head, tail), axis, swap_pairs(axis, 1))  12.7 us
    all_to_all x1, starting transfers between devices, on_device(): lax.all_to_all(pair, AXES, 0, 0, axis_index_groups=groups_over((0, 4)), t...  5.41 us
    all_to_all x1, starting transfers between devices, on_device(): lax.all_to_all(plane, AXES, 0, 0, axis_index_groups=groups_over((1, 3)),...  5.36 us
    ppermute x4, waiting for transfers between devices, exchange(): far = lax.ppermute(jnp.where(even, head, tail), axis, swap_pairs(axis, 1))  5.23 us
    ppermute x4, waiting for transfers between devices, exchange(): near = lax.ppermute(jnp.where(even, tail, head), axis, swap_pairs(axis, 0))  4.99 us
    unnamed x34, local copies, waits for them, and re-layouts  2.83 us
  transfers between devices with their start and end apart: 11, of which 6 were waited for; matrix products, arithmetic and copies ran while one was open for 3% of the time, Pallas kernels for 15%

profile of v6, /device:TPU:32, one launch (start us, length us, event | category | flops | bytes accessed | tf_op | source)
XLA Modules:
  0.0 88.9 jit_solution(1478723891132732940)
XLA Ops:
  0.6 1.1 %fusion.44 = (bf16[4,16,1,128]{3,2,1,0:T(2,128)(2,1)S(1)}, bf16[4,16,1,128]{3,2,1,0:T(2,128)(2,1)S(1)}) fusion(bf16[4,16,16,128]{3,2,1,0:T(8,128)(2,1)} %param.13), kind=kLoop, calls=%fused_computation.138 | loop fusion | bytes 65536 | tf_op jit(solution)/shard_map/slice | solution.py:28
  1.7 1.0 %fusion.43 = (bf16[4,16,3,128]{3,2,1,0:T(4,128)(2,1)S(1)}, bf16[4,16,3,128]{3,2,1,0:T(4,128)(2,1)S(1)}) fusion(bf16[4,16,16,128]{3,2,1,0:T(8,128)(2,1)} %param.7), kind=kLoop, calls=%fused_computation.137 | loop fusion | bytes 196608 | tf_op jit(solution)/shard_map/slice | solution.py:28
  2.9 4.6 %collective-permute-start = (bf16[256,128]{1,0:T(8,128)(2,1)S(1)}, bf16[256,128]{1,0:T(8,128)(2,1)S(1)}, u32[]{:S(2)}, u32[]{:S(2)}) collective-permute-start(bf16[256,128]{1,0:T(8,128)(2,1)S(1)} %get-tuple-element.49), channel_id=1, source_target_pairs={{1,2},{2,1},{3,4},{4,3},{5,6},{6,5},{7,8},{8,7},{9,10},{10,9},{11,... | collective-permute-start | bytes 196616 | tf_op jit(solution)/shard_map/ppermute | solution.py:36
  7.5 0.7 collective-permute-start.1
  8.3 0.8 fusion.34.order
  9.2 2.1 %collective-permute-done = bf16[256,128]{1,0:T(8,128)(2,1)S(1)} collective-permute-done((bf16[256,128]{1,0:T(8,128)(2,1)S(1)}, bf16[256,128]{1,0:T(8,128)(2,1)S(1)}, u32[]{:S(2)}, u32[]{:S(2)}) %collective-permute-start) | collective-permute-done | bytes 65568 | tf_op jit(solution)/shard_map/ppermute | solution.py:36
  12.4 0.7 collective-permute-start.2
  13.1 8.6 %collective-permute-start.3 = (bf16[336,128]{1,0:T(8,128)(2,1)S(1)}, bf16[336,128]{1,0:T(8,128)(2,1)S(1)}, u32[]{:S(2)}, u32[]{:S(2)}) collective-permute-start(bf16[336,128]{1,0:T(8,128)(2,1)S(1)} %get-tuple-element.46), channel_id=1, source_target_pairs={{0,16},{16,0},{32,48},{48,32},{64,80},{80,64},{96,112},{112,96},{1... | collective-permute-start | bytes 258056 | tf_op jit(solution)/shard_map/ppermute | solution.py:37
  21.8 0.8 collective-permute-done.3
  24.0 8.4 %shard_map.94 = (bf16[128,3456]{1,0:T(8,128)(2,1)}, bf16[128,3456]{1,0:T(8,128)(2,1)}, f32[3008,256]{1,0:T(8,128)}) custom-call(bf16[4,528,128]{2,1,0:T(8,128)(2,1)S(1)} %bitcast.42, bf16[4,432,128]{2,1,0:T(8,128)(2,1)S(1)} %bitcast.39, f32[480,128]{1,0:T(8,128)S(1)} %broadcast_in_dim.4.mask, bf16[256,256]{1,0:T(8,128)(2,1)S(1)} %fusion.34.order, ...), custom_call_target="tpu_custom_call" | custom-call | tf_op jit(solution)/shard_map/pallas_call | solution.py:369
  32.4 1.2 %collective-permute-start.4 = (bf16[128,3456]{1,0:T(8,128)(2,1)}, bf16[128,3456]{1,0:T(8,128)(2,1)}, u32[]{:S(2)}, u32[]{:S(2)}) collective-permute-start(bf16[128,3456]{1,0:T(8,128)(2,1)} %get-tuple-element.17), channel_id=1, source_target_pairs={{0,16},{16,0},{32,48},{48,32},{64,80},{80,64},{96,112},{112,96},{1... | collective-permute-start | bytes 2654216 | tf_op jit(solution)/shard_map/ppermute | solution.py:464
  33.7 3.9 %shard_map.96 = (bf16[4,256,128]{2,1,0:T(8,128)(2,1)S(1)}, bf16[4,256,128]{2,1,0:T(8,128)(2,1)S(1)}, bf16[2,8,8,256]{3,2,1,0:T(8,128)(2,1)S(1)}) custom-call(bf16[4,432,128]{2,1,0:T(8,128)(2,1)S(1)} %bitcast.40, f32[3008,256]{1,0:T(8,128)} %get-tuple-element.15.kept_in, bf16[27,256,128]{2,1,0:T(8,128)(2,1)S(1)} %copy-done, bf16[256,1024]{1,0:T(8,128)(2,1)S(1)} %copy-done.3), custom_call_target="tpu_custom_call" | custom-call | tf_op jit(solution)/shard_map/pallas_call | solution.py:369
  37.6 0.7 copy-done.5
  38.3 2.3 %shard_map.95 = bf16[128,3456]{1,0:T(8,128)(2,1)} custom-call(bf16[128,3456]{1,0:T(8,128)(2,1)S(1)} %copy-done.4, bf16[128,3456]{1,0:T(8,128)(2,1)} %collective-permute-done.4.other), custom_call_target="tpu_custom_call" | custom-call | tf_op jit(solution)/shard_map/pallas_call | solution.py:369
  41.4 7.2 %collective-permute-start.6 = (bf16[192,128]{1,0:T(8,128)(2,1)S(1)}, bf16[192,128]{1,0:T(8,128)(2,1)S(1)}, u32[]{:S(2)}, u32[]{:S(2)}) collective-permute-start(bf16[192,128]{1,0:T(8,128)(2,1)S(1)} %get-tuple-element.60), channel_id=1, source_target_pairs={{0,16},{16,0},{32,48},{48,32},{64,80},{80,64},{96,112},{112,96},{1... | collective-permute-start | bytes 147464 | tf_op jit(solution)/shard_map/ppermute | solution.py:37
  48.8 5.4 %all-to-all-start = ((bf16[16,8,3456]{2,1,0:T(8,128)(2,1)}), bf16[16,8,3456]{2,1,0:T(8,128)(2,1)S(1)}, u32[]{:S(2)}, u32[]{:S(2)}) async-start(bf16[16,8,3456]{2,1,0:T(8,128)(2,1)} %bitcast.24), calls=%async_computation | async-start | bytes 1769472 | tf_op jit(solution)/shard_map/all_to_all | solution.py:494
  55.3 6.8 %collective-permute-start.7 = (bf16[240,128]{1,0:T(8,128)(2,1)S(1)}, bf16[240,128]{1,0:T(8,128)(2,1)S(1)}, u32[]{:S(2)}, u32[]{:S(2)}) collective-permute-start(bf16[240,128]{1,0:T(8,128)(2,1)S(1)} %get-tuple-element.53), channel_id=1, source_target_pairs={{1,2},{2,1},{3,4},{4,3},{5,6},{6,5},{7,8},{8,7},{9,10},{10,9},{11,... | collective-permute-start | bytes 184328 | tf_op jit(solution)/shard_map/ppermute | solution.py:36
  62.3 3.1 %collective-permute-done.7 = bf16[240,128]{1,0:T(8,128)(2,1)S(1)} collective-permute-done((bf16[240,128]{1,0:T(8,128)(2,1)S(1)}, bf16[240,128]{1,0:T(8,128)(2,1)S(1)}, u32[]{:S(2)}, u32[]{:S(2)}) %collective-permute-start.7) | collective-permute-done | bytes 61472 | tf_op jit(solution)/shard_map/ppermute | solution.py:36
  65.4 3.6 %collective-permute-done.8 = bf16[240,128]{1,0:T(8,128)(2,1)S(1)} collective-permute-done((bf16[240,128]{1,0:T(8,128)(2,1)S(1)}, bf16[240,128]{1,0:T(8,128)(2,1)S(1)}, u32[]{:S(2)}, u32[]{:S(2)}) %collective-permute-start.8) | collective-permute-done | bytes 61472 | tf_op jit(solution)/shard_map/ppermute | solution.py:37
  69.6 1.0 %all-to-all-done = bf16[16,8,3456]{2,1,0:T(8,128)(2,1)S(1)} async-done(((bf16[16,8,3456]{2,1,0:T(8,128)(2,1)}), bf16[16,8,3456]{2,1,0:T(8,128)(2,1)S(1)}, u32[]{:S(2)}, u32[]{:S(2)}) %all-to-all-start) | async-done | bytes 884768 | tf_op jit(solution)/shard_map/all_to_all | solution.py:494
  70.8 0.7 copy.54
  71.4 5.4 %all-to-all-start.1 = ((f32[8,27,128]{2,1,0:T(8,128)}), f32[8,27,128]{2,1,0:T(8,128)S(1)}, u32[]{:S(2)}, u32[]{:S(2)}) async-start(f32[8,27,128]{2,1,0:T(8,128)} %copy.54), calls=%async_computation.1 | async-start | bytes 262144 | tf_op jit(solution)/shard_map/all_to_all | solution.py:499
  77.6 0.8 copy-done.1
  78.4 9.9 %shard_map.97 = (bf16[4,256,128]{2,1,0:T(8,128)(2,1)}, bf16[4,256,128]{2,1,0:T(8,128)(2,1)}) custom-call(f32[3008,256]{1,0:T(8,128)} %get-tuple-element.15.kept_in, bf16[4,432,128]{2,1,0:T(8,128)(2,1)S(1)} %bitcast.43, bf16[2,192,256]{2,1,0:T(8,128)(2,1)S(1)} %bitcast.45, bf16[4,432,128]{2,1,0:T(8,128)(2,1)S(1)} %bitcast.44, ...), custom_call_target="tpu_custom_call" | custom-call | tf_op jit(solution)/shard_map/pallas_call | solution.py:369
  (138 shorter events, 6.6 us)
Async XLA Ops:
  0.6 11.4 %copy-start.9 = (bf16[4,16,16,128]{3,2,1,0:T(8,128)(2,1)S(1)}, bf16[4,16,16,128]{3,2,1,0:T(8,128)(2,1)}, u32[]{:S(2)}) copy-start(bf16[4,16,16,128]{3,2,1,0:T(8,128)(2,1)} %param.7) | copy-start | bytes 786436
  2.9 9.4 %copy-start.10 = (bf16[4,16,16,128]{3,2,1,0:T(8,128)(2,1)S(1)}, bf16[4,16,16,128]{3,2,1,0:T(8,128)(2,1)}, u32[]{:S(2)}) copy-start(bf16[4,16,16,128]{3,2,1,0:T(8,128)(2,1)} %param.13) | copy-start | bytes 786436
  2.9 8.4 %collective-permute-start = (bf16[256,128]{1,0:T(8,128)(2,1)S(1)}, bf16[256,128]{1,0:T(8,128)(2,1)S(1)}, u32[]{:S(2)}, u32[]{:S(2)}) collective-permute-start(bf16[256,128]{1,0:T(8,128)(2,1)S(1)} %get-tuple-element.49), channel_id=1, source_target_pairs={{1,2},{2,1},{3,4},{4,3},{5,6},{6,5},{7,8},{8,7},{9,10},{10,9},{11,... | collective-permute-start | bytes 196616 | tf_op jit(solution)/shard_map/ppermute | solution.py:36
  7.5 4.4 %collective-permute-start.1 = (bf16[256,128]{1,0:T(8,128)(2,1)S(1)}, bf16[256,128]{1,0:T(8,128)(2,1)S(1)}, u32[]{:S(2)}, u32[]{:S(2)}) collective-permute-start(bf16[256,128]{1,0:T(8,128)(2,1)S(1)} %get-tuple-element.50), channel_id=1, source_target_pairs={{0,1},{1,0},{2,3},{3,2},{4,5},{5,4},{6,7},{7,6},{8,9},{9,8},{10,11... | collective-permute-start | bytes 196616 | tf_op jit(solution)/shard_map/ppermute | solution.py:37
  12.4 9.4 %collective-permute-start.2 = (bf16[336,128]{1,0:T(8,128)(2,1)S(1)}, bf16[336,128]{1,0:T(8,128)(2,1)S(1)}, u32[]{:S(2)}, u32[]{:S(2)}) collective-permute-start(bf16[336,128]{1,0:T(8,128)(2,1)S(1)} %get-tuple-element.45), channel_id=1, source_target_pairs={{16,32},{32,16},{48,64},{64,48},{80,96},{96,80},{112,128},{128,112... | collective-permute-start | bytes 258056 | tf_op jit(solution)/shard_map/ppermute | solution.py:36
  13.1 9.6 %collective-permute-start.3 = (bf16[336,128]{1,0:T(8,128)(2,1)S(1)}, bf16[336,128]{1,0:T(8,128)(2,1)S(1)}, u32[]{:S(2)}, u32[]{:S(2)}) collective-permute-start(bf16[336,128]{1,0:T(8,128)(2,1)S(1)} %get-tuple-element.46), channel_id=1, source_target_pairs={{0,16},{16,0},{32,48},{48,32},{64,80},{80,64},{96,112},{112,96},{1... | collective-permute-start | bytes 258056 | tf_op jit(solution)/shard_map/ppermute | solution.py:37
  22.8 1.0 %copy-start.2 = (bf16[1024,256]{1,0:T(8,128)(2,1)S(1)}, bf16[1024,256]{1,0:T(8,128)(2,1)}, u32[]{:S(2)}) copy-start(bf16[1024,256]{1,0:T(8,128)(2,1)} %w_down_in.3) | copy-start | bytes 1572868
  22.8 1.2 %copy-start.3 = (bf16[256,1024]{1,0:T(8,128)(2,1)S(1)}, bf16[256,1024]{1,0:T(8,128)(2,1)}, u32[]{:S(2)}) copy-start(bf16[256,1024]{1,0:T(8,128)(2,1)} %w_up_in.3) | copy-start | bytes 1572868
  24.0 9.7 %copy-start = (bf16[27,256,128]{2,1,0:T(8,128)(2,1)S(1)}, bf16[27,256,128]{2,1,0:T(8,128)(2,1)}, u32[]{:S(2)}) copy-start(bf16[27,256,128]{2,1,0:T(8,128)(2,1)} %w_last_in.1) | copy-start | bytes 5308420
  32.4 5.8 %collective-permute-start.4 = (bf16[128,3456]{1,0:T(8,128)(2,1)}, bf16[128,3456]{1,0:T(8,128)(2,1)}, u32[]{:S(2)}, u32[]{:S(2)}) collective-permute-start(bf16[128,3456]{1,0:T(8,128)(2,1)} %get-tuple-element.17), channel_id=1, source_target_pairs={{0,16},{16,0},{32,48},{48,32},{64,80},{80,64},{96,112},{112,96},{1... | collective-permute-start | bytes 2654216 | tf_op jit(solution)/shard_map/ppermute | solution.py:464
  33.7 4.6 %copy-start.4 = (bf16[128,3456]{1,0:T(8,128)(2,1)S(1)}, bf16[128,3456]{1,0:T(8,128)(2,1)}, u32[]{:S(2)}) copy-start(bf16[128,3456]{1,0:T(8,128)(2,1)} %get-tuple-element.16.one) | copy-start | bytes 2654212
  37.5 0.7 copy-start.5
  38.3 2.4 %copy-start.7 = (bf16[2,8,8,256]{3,2,1,0:T(8,128)(2,1)}, bf16[2,8,8,256]{3,2,1,0:T(8,128)(2,1)S(1)}, u32[]{:S(2)}) copy-start(bf16[2,8,8,256]{3,2,1,0:T(8,128)(2,1)S(1)} %get-tuple-element.23) | copy-start | bytes 196612
  38.3 2.4 %copy-start.6 = (bf16[4,256,128]{2,1,0:T(8,128)(2,1)S(1)}, bf16[4,256,128]{2,1,0:T(8,128)(2,1)}, u32[]{:S(2)}) copy-start(bf16[4,256,128]{2,1,0:T(8,128)(2,1)} %copy-done.5) | copy-start | bytes 786436
  40.7 13.5 %collective-permute-start.5 = (bf16[192,128]{1,0:T(8,128)(2,1)S(1)}, bf16[192,128]{1,0:T(8,128)(2,1)S(1)}, u32[]{:S(2)}, u32[]{:S(2)}) collective-permute-start(bf16[192,128]{1,0:T(8,128)(2,1)S(1)} %get-tuple-element.59), channel_id=1, source_target_pairs={{16,32},{32,16},{48,64},{64,48},{80,96},{96,80},{112,128},{128,112... | collective-permute-start | bytes 147464 | tf_op jit(solution)/shard_map/ppermute | solution.py:36
  41.4 12.8 %collective-permute-start.6 = (bf16[192,128]{1,0:T(8,128)(2,1)S(1)}, bf16[192,128]{1,0:T(8,128)(2,1)S(1)}, u32[]{:S(2)}, u32[]{:S(2)}) collective-permute-start(bf16[192,128]{1,0:T(8,128)(2,1)S(1)} %get-tuple-element.60), channel_id=1, source_target_pairs={{0,16},{16,0},{32,48},{48,32},{64,80},{80,64},{96,112},{112,96},{1... | collective-permute-start | bytes 147464 | tf_op jit(solution)/shard_map/ppermute | solution.py:37
  48.8 21.9 %all-to-all-start = ((bf16[16,8,3456]{2,1,0:T(8,128)(2,1)}), bf16[16,8,3456]{2,1,0:T(8,128)(2,1)S(1)}, u32[]{:S(2)}, u32[]{:S(2)}) async-start(bf16[16,8,3456]{2,1,0:T(8,128)(2,1)} %bitcast.24), calls=%async_computation | async-start | bytes 1769472 | tf_op jit(solution)/shard_map/all_to_all | solution.py:494
  54.2 0.8 copy-start.8
  55.3 10.1 %collective-permute-start.7 = (bf16[240,128]{1,0:T(8,128)(2,1)S(1)}, bf16[240,128]{1,0:T(8,128)(2,1)S(1)}, u32[]{:S(2)}, u32[]{:S(2)}) collective-permute-start(bf16[240,128]{1,0:T(8,128)(2,1)S(1)} %get-tuple-element.53), channel_id=1, source_target_pairs={{1,2},{2,1},{3,4},{4,3},{5,6},{6,5},{7,8},{8,7},{9,10},{10,9},{11,... | collective-permute-start | bytes 184328 | tf_op jit(solution)/shard_map/ppermute | solution.py:36
  62.1 6.9 %collective-permute-start.8 = (bf16[240,128]{1,0:T(8,128)(2,1)S(1)}, bf16[240,128]{1,0:T(8,128)(2,1)S(1)}, u32[]{:S(2)}, u32[]{:S(2)}) collective-permute-start(bf16[240,128]{1,0:T(8,128)(2,1)S(1)} %get-tuple-element.54), channel_id=1, source_target_pairs={{0,1},{1,0},{2,3},{3,2},{4,5},{5,4},{6,7},{7,6},{8,9},{9,8},{10,11... | collective-permute-start | bytes 184328 | tf_op jit(solution)/shard_map/ppermute | solution.py:37
  71.4 16.8 %all-to-all-start.1 = ((f32[8,27,128]{2,1,0:T(8,128)}), f32[8,27,128]{2,1,0:T(8,128)S(1)}, u32[]{:S(2)}, u32[]{:S(2)}) async-start(f32[8,27,128]{2,1,0:T(8,128)} %copy.54), calls=%async_computation.1 | async-start | bytes 262144 | tf_op jit(solution)/shard_map/all_to_all | solution.py:499
  77.2 1.2 %copy-start.1 = (bf16[27,128,128]{2,1,0:T(8,128)(2,1)S(1)}, bf16[27,128,128]{2,1,0:T(8,128)(2,1)}, u32[]{:S(2)}) copy-start(bf16[27,128,128]{2,1,0:T(8,128)(2,1)} %w_first_in.1) | copy-start | bytes 2654212

commit v7 on v6

--- a/solution.py
+++ b/solution.py
@@ -375,7 +375,7 @@
             pltpu.SemaphoreType.DMA((shape,)) if kind is None else pltpu.VMEM(shape, kind)
             for shape, kind in scratch
         ],
-        compiler_params=pltpu.CompilerParams(vmem_limit_bytes=50 * 2**20),
+        compiler_params=pltpu.CompilerParams(vmem_limit_bytes=51 * 2**20),
     )(*args)
 
 

time: 89.5 us -> 87.5 us (0.978)
  Pallas kernels: 24.5 us -> 23.3 us
  local copies, waits for them, and re-layouts: 7.11 us -> 5.93 us
    unnamed x34 -> x24, local copies, waits for them, and re-layouts: 2.83 us -> 1.65 us
    pallas_call x4, Pallas kernels: 24.5 us -> 23.3 us  [call(): pl.pallas_call(kernel, out_shape=[jax.ShapeDtypeStruct(shape, kind) for s...]
  transfers between devices with their start and end apart: 11 -> 11, of which waited for: 6 -> 6; matrix products, arithmetic and copies ran while one was open for 3% -> 3% of each run, Pallas kernels for 15% -> 16%
where the time goes in v7:
time: 87.5 us; the launch traced here: 87 us
  starting transfers between devices  41.3 us (47%)
  Pallas kernels  23.3 us (27%)
  waiting for transfers between devices  11.7 us (13%)
  local copies, waits for them, and re-layouts  5.93 us (7%)
  other arithmetic  3.17 us (4%)
  between operations  1.52 us (2%)
    pallas_call x4, Pallas kernels, call(): pl.pallas_call(kernel, out_shape=[jax.ShapeDtypeStruct(shape, kind) for s...  23.3 us
    ppermute x4, starting transfers between devices, exchange(): near = lax.ppermute(jnp.where(even, tail, head), axis, swap_pairs(axis, 0))  16.6 us
    ppermute x4, starting transfers between devices, exchange(): far = lax.ppermute(jnp.where(even, head, tail), axis, swap_pairs(axis, 1))  12.7 us
    all_to_all x1, starting transfers between devices, on_device(): lax.all_to_all(pair, AXES, 0, 0, axis_index_groups=groups_over((0, 4)), t...  5.4 us
    ppermute x4, waiting for transfers between devices, exchange(): far = lax.ppermute(jnp.where(even, head, tail), axis, swap_pairs(axis, 1))  5.37 us
    all_to_all x1, starting transfers between devices, on_device(): lax.all_to_all(plane, AXES, 0, 0, axis_index_groups=groups_over((1, 3)),...  5.35 us
    ppermute x4, waiting for transfers between devices, exchange(): near = lax.ppermute(jnp.where(even, tail, head), axis, swap_pairs(axis, 0))  5.23 us
    slice x6, local copies, waits for them, and re-layouts, exchange(): firsts.append(lax.slice_in_dim(field, 0, width, axis=dim))  2.14 us
  transfers between devices with their start and end apart: 11, of which 6 were waited for; matrix products, arithmetic and copies ran while one was open for 3% of the time, Pallas kernels for 16%

profile of v7, /device:TPU:32, one launch (start us, length us, event | category | flops | bytes accessed | tf_op | source)
XLA Modules:
  0.0 87.0 jit_solution(351805374899261815)
XLA Ops:
  0.6 1.1 %fusion.44 = (bf16[4,16,1,128]{3,2,1,0:T(2,128)(2,1)S(1)}, bf16[4,16,1,128]{3,2,1,0:T(2,128)(2,1)S(1)}) fusion(bf16[4,16,16,128]{3,2,1,0:T(8,128)(2,1)} %param.13), kind=kLoop, calls=%fused_computation.138 | loop fusion | bytes 65536 | tf_op jit(solution)/shard_map/slice | solution.py:28
  1.7 1.0 %fusion.43 = (bf16[4,16,3,128]{3,2,1,0:T(4,128)(2,1)S(1)}, bf16[4,16,3,128]{3,2,1,0:T(4,128)(2,1)S(1)}) fusion(bf16[4,16,16,128]{3,2,1,0:T(8,128)(2,1)} %param.7), kind=kLoop, calls=%fused_computation.137 | loop fusion | bytes 196608 | tf_op jit(solution)/shard_map/slice | solution.py:28
  2.9 4.6 %collective-permute-start = (bf16[256,128]{1,0:T(8,128)(2,1)S(1)}, bf16[256,128]{1,0:T(8,128)(2,1)S(1)}, u32[]{:S(2)}, u32[]{:S(2)}) collective-permute-start(bf16[256,128]{1,0:T(8,128)(2,1)S(1)} %get-tuple-element.49), channel_id=1, source_target_pairs={{1,2},{2,1},{3,4},{4,3},{5,6},{6,5},{7,8},{8,7},{9,10},{10,9},{11,... | collective-permute-start | bytes 196616 | tf_op jit(solution)/shard_map/ppermute | solution.py:36
  7.5 0.7 collective-permute-start.1
  8.3 0.8 fusion.34.order
  9.2 2.1 %collective-permute-done = bf16[256,128]{1,0:T(8,128)(2,1)S(1)} collective-permute-done((bf16[256,128]{1,0:T(8,128)(2,1)S(1)}, bf16[256,128]{1,0:T(8,128)(2,1)S(1)}, u32[]{:S(2)}, u32[]{:S(2)}) %collective-permute-start) | collective-permute-done | bytes 65568 | tf_op jit(solution)/shard_map/ppermute | solution.py:36
  12.4 0.7 collective-permute-start.2
  13.1 8.6 %collective-permute-start.3 = (bf16[336,128]{1,0:T(8,128)(2,1)S(1)}, bf16[336,128]{1,0:T(8,128)(2,1)S(1)}, u32[]{:S(2)}, u32[]{:S(2)}) collective-permute-start(bf16[336,128]{1,0:T(8,128)(2,1)S(1)} %get-tuple-element.46), channel_id=1, source_target_pairs={{0,16},{16,0},{32,48},{48,32},{64,80},{80,64},{96,112},{112,96},{1... | collective-permute-start | bytes 258056 | tf_op jit(solution)/shard_map/ppermute | solution.py:37
  21.8 0.8 collective-permute-done.3
  24.0 8.3 %shard_map.94 = (bf16[128,3456]{1,0:T(8,128)(2,1)}, bf16[128,3456]{1,0:T(8,128)(2,1)}, f32[3008,256]{1,0:T(8,128)}) custom-call(bf16[4,528,128]{2,1,0:T(8,128)(2,1)S(1)} %bitcast.41, bf16[4,432,128]{2,1,0:T(8,128)(2,1)S(1)} %bitcast.38, f32[480,128]{1,0:T(8,128)S(1)} %broadcast_in_dim.4.mask, bf16[256,256]{1,0:T(8,128)(2,1)S(1)} %fusion.34.order, ...), custom_call_target="tpu_custom_call" | custom-call | tf_op jit(solution)/shard_map/pallas_call | solution.py:369
  32.3 1.3 %collective-permute-start.4 = (bf16[128,3456]{1,0:T(8,128)(2,1)}, bf16[128,3456]{1,0:T(8,128)(2,1)S(1)}, u32[]{:S(2)}, u32[]{:S(2)}) collective-permute-start(bf16[128,3456]{1,0:T(8,128)(2,1)} %get-tuple-element.17), channel_id=1, source_target_pairs={{0,16},{16,0},{32,48},{48,32},{64,80},{80,64},{96,112},{112,96},{1... | collective-permute-start | bytes 2654216 | tf_op jit(solution)/shard_map/ppermute | solution.py:464
  33.5 4.1 %shard_map.96 = (bf16[4,256,128]{2,1,0:T(8,128)(2,1)S(1)}, bf16[4,256,128]{2,1,0:T(8,128)(2,1)S(1)}, bf16[2,8,8,256]{3,2,1,0:T(8,128)(2,1)S(1)}) custom-call(bf16[4,432,128]{2,1,0:T(8,128)(2,1)S(1)} %bitcast.39, f32[3008,256]{1,0:T(8,128)} %get-tuple-element.15.kept_in, bf16[27,256,128]{2,1,0:T(8,128)(2,1)} %w_last_in.1, bf16[256,1024]{1,0:T(8,128)(2,1)S(1)} %copy-done.2), custom_call_target="tpu_custom_call" | custom-call | tf_op jit(solution)/shard_map/pallas_call | solution.py:369
  37.6 1.1 %shard_map.95 = bf16[128,3456]{1,0:T(8,128)(2,1)} custom-call(bf16[128,3456]{1,0:T(8,128)(2,1)S(1)} %copy-done.3, bf16[128,3456]{1,0:T(8,128)(2,1)S(1)} %collective-permute-done.4.other), custom_call_target="tpu_custom_call" | custom-call | tf_op jit(solution)/shard_map/pallas_call | solution.py:369
  38.9 0.7 collective-permute-start.5
  39.5 7.2 %collective-permute-start.6 = (bf16[192,128]{1,0:T(8,128)(2,1)S(1)}, bf16[192,128]{1,0:T(8,128)(2,1)S(1)}, u32[]{:S(2)}, u32[]{:S(2)}) collective-permute-start(bf16[192,128]{1,0:T(8,128)(2,1)S(1)} %get-tuple-element.60), channel_id=1, source_target_pairs={{0,16},{16,0},{32,48},{48,32},{64,80},{80,64},{96,112},{112,96},{1... | collective-permute-start | bytes 147464 | tf_op jit(solution)/shard_map/ppermute | solution.py:37
  46.9 5.4 %all-to-all-start = ((bf16[16,8,3456]{2,1,0:T(8,128)(2,1)}), bf16[16,8,3456]{2,1,0:T(8,128)(2,1)S(1)}, u32[]{:S(2)}, u32[]{:S(2)}) async-start(bf16[16,8,3456]{2,1,0:T(8,128)(2,1)} %bitcast.24), calls=%async_computation | async-start | bytes 1769472 | tf_op jit(solution)/shard_map/all_to_all | solution.py:494
  53.0 6.8 %collective-permute-start.7 = (bf16[240,128]{1,0:T(8,128)(2,1)S(1)}, bf16[240,128]{1,0:T(8,128)(2,1)S(1)}, u32[]{:S(2)}, u32[]{:S(2)}) collective-permute-start(bf16[240,128]{1,0:T(8,128)(2,1)S(1)} %get-tuple-element.53), channel_id=1, source_target_pairs={{1,2},{2,1},{3,4},{4,3},{5,6},{6,5},{7,8},{8,7},{9,10},{10,9},{11,... | collective-permute-start | bytes 184328 | tf_op jit(solution)/shard_map/ppermute | solution.py:36
  60.0 3.2 %collective-permute-done.7 = bf16[240,128]{1,0:T(8,128)(2,1)S(1)} collective-permute-done((bf16[240,128]{1,0:T(8,128)(2,1)S(1)}, bf16[240,128]{1,0:T(8,128)(2,1)S(1)}, u32[]{:S(2)}, u32[]{:S(2)}) %collective-permute-start.7) | collective-permute-done | bytes 61472 | tf_op jit(solution)/shard_map/ppermute | solution.py:36
  63.2 3.8 %collective-permute-done.8 = bf16[240,128]{1,0:T(8,128)(2,1)S(1)} collective-permute-done((bf16[240,128]{1,0:T(8,128)(2,1)S(1)}, bf16[240,128]{1,0:T(8,128)(2,1)S(1)}, u32[]{:S(2)}, u32[]{:S(2)}) %collective-permute-start.8) | collective-permute-done | bytes 61472 | tf_op jit(solution)/shard_map/ppermute | solution.py:37
  67.7 1.1 %all-to-all-done = bf16[16,8,3456]{2,1,0:T(8,128)(2,1)S(1)} async-done(((bf16[16,8,3456]{2,1,0:T(8,128)(2,1)}), bf16[16,8,3456]{2,1,0:T(8,128)(2,1)S(1)}, u32[]{:S(2)}, u32[]{:S(2)}) %all-to-all-start) | async-done | bytes 884768 | tf_op jit(solution)/shard_map/all_to_all | solution.py:494
  68.9 0.7 copy.54
  69.6 5.3 %all-to-all-start.1 = ((f32[8,27,128]{2,1,0:T(8,128)}), f32[8,27,128]{2,1,0:T(8,128)S(1)}, u32[]{:S(2)}, u32[]{:S(2)}) async-start(f32[8,27,128]{2,1,0:T(8,128)} %copy.54), calls=%async_computation.1 | async-start | bytes 262144 | tf_op jit(solution)/shard_map/all_to_all | solution.py:499
  75.7 0.8 copy-done
  76.5 9.9 %shard_map.97 = (bf16[4,256,128]{2,1,0:T(8,128)(2,1)}, bf16[4,256,128]{2,1,0:T(8,128)(2,1)}) custom-call(f32[3008,256]{1,0:T(8,128)} %get-tuple-element.15.kept_in, bf16[4,432,128]{2,1,0:T(8,128)(2,1)S(1)} %bitcast.42, bf16[2,192,256]{2,1,0:T(8,128)(2,1)S(1)} %bitcast.44, bf16[4,432,128]{2,1,0:T(8,128)(2,1)S(1)} %bitcast.43, ...), custom_call_target="tpu_custom_call" | custom-call | tf_op jit(solution)/shard_map/pallas_call | solution.py:369
  (128 shorter events, 5.4 us)
Async XLA Ops:
  0.6 11.4 %copy-start.4 = (bf16[4,16,16,128]{3,2,1,0:T(8,128)(2,1)S(1)}, bf16[4,16,16,128]{3,2,1,0:T(8,128)(2,1)}, u32[]{:S(2)}) copy-start(bf16[4,16,16,128]{3,2,1,0:T(8,128)(2,1)} %param.7) | copy-start | bytes 786436
  2.9 9.4 %copy-start.5 = (bf16[4,16,16,128]{3,2,1,0:T(8,128)(2,1)S(1)}, bf16[4,16,16,128]{3,2,1,0:T(8,128)(2,1)}, u32[]{:S(2)}) copy-start(bf16[4,16,16,128]{3,2,1,0:T(8,128)(2,1)} %param.13) | copy-start | bytes 786436
  2.9 8.4 %collective-permute-start = (bf16[256,128]{1,0:T(8,128)(2,1)S(1)}, bf16[256,128]{1,0:T(8,128)(2,1)S(1)}, u32[]{:S(2)}, u32[]{:S(2)}) collective-permute-start(bf16[256,128]{1,0:T(8,128)(2,1)S(1)} %get-tuple-element.49), channel_id=1, source_target_pairs={{1,2},{2,1},{3,4},{4,3},{5,6},{6,5},{7,8},{8,7},{9,10},{10,9},{11,... | collective-permute-start | bytes 196616 | tf_op jit(solution)/shard_map/ppermute | solution.py:36
  7.5 4.4 %collective-permute-start.1 = (bf16[256,128]{1,0:T(8,128)(2,1)S(1)}, bf16[256,128]{1,0:T(8,128)(2,1)S(1)}, u32[]{:S(2)}, u32[]{:S(2)}) collective-permute-start(bf16[256,128]{1,0:T(8,128)(2,1)S(1)} %get-tuple-element.50), channel_id=1, source_target_pairs={{0,1},{1,0},{2,3},{3,2},{4,5},{5,4},{6,7},{7,6},{8,9},{9,8},{10,11... | collective-permute-start | bytes 196616 | tf_op jit(solution)/shard_map/ppermute | solution.py:37
  12.4 9.4 %collective-permute-start.2 = (bf16[336,128]{1,0:T(8,128)(2,1)S(1)}, bf16[336,128]{1,0:T(8,128)(2,1)S(1)}, u32[]{:S(2)}, u32[]{:S(2)}) collective-permute-start(bf16[336,128]{1,0:T(8,128)(2,1)S(1)} %get-tuple-element.45), channel_id=1, source_target_pairs={{16,32},{32,16},{48,64},{64,48},{80,96},{96,80},{112,128},{128,112... | collective-permute-start | bytes 258056 | tf_op jit(solution)/shard_map/ppermute | solution.py:36
  13.1 9.6 %collective-permute-start.3 = (bf16[336,128]{1,0:T(8,128)(2,1)S(1)}, bf16[336,128]{1,0:T(8,128)(2,1)S(1)}, u32[]{:S(2)}, u32[]{:S(2)}) collective-permute-start(bf16[336,128]{1,0:T(8,128)(2,1)S(1)} %get-tuple-element.46), channel_id=1, source_target_pairs={{0,16},{16,0},{32,48},{48,32},{64,80},{80,64},{96,112},{112,96},{1... | collective-permute-start | bytes 258056 | tf_op jit(solution)/shard_map/ppermute | solution.py:37
  22.8 1.0 %copy-start.1 = (bf16[1024,256]{1,0:T(8,128)(2,1)S(1)}, bf16[1024,256]{1,0:T(8,128)(2,1)}, u32[]{:S(2)}) copy-start(bf16[1024,256]{1,0:T(8,128)(2,1)} %w_down_in.3) | copy-start | bytes 1572868
  22.8 1.2 %copy-start.2 = (bf16[256,1024]{1,0:T(8,128)(2,1)S(1)}, bf16[256,1024]{1,0:T(8,128)(2,1)}, u32[]{:S(2)}) copy-start(bf16[256,1024]{1,0:T(8,128)(2,1)} %w_up_in.3) | copy-start | bytes 1572868
  32.3 5.3 %collective-permute-start.4 = (bf16[128,3456]{1,0:T(8,128)(2,1)}, bf16[128,3456]{1,0:T(8,128)(2,1)S(1)}, u32[]{:S(2)}, u32[]{:S(2)}) collective-permute-start(bf16[128,3456]{1,0:T(8,128)(2,1)} %get-tuple-element.17), channel_id=1, source_target_pairs={{0,16},{16,0},{32,48},{48,32},{64,80},{80,64},{96,112},{112,96},{1... | collective-permute-start | bytes 2654216 | tf_op jit(solution)/shard_map/ppermute | solution.py:464
  33.5 4.1 %copy-start.3 = (bf16[128,3456]{1,0:T(8,128)(2,1)S(1)}, bf16[128,3456]{1,0:T(8,128)(2,1)}, u32[]{:S(2)}) copy-start(bf16[128,3456]{1,0:T(8,128)(2,1)} %get-tuple-element.16.one) | copy-start | bytes 2654212
  38.9 13.5 %collective-permute-start.5 = (bf16[192,128]{1,0:T(8,128)(2,1)S(1)}, bf16[192,128]{1,0:T(8,128)(2,1)S(1)}, u32[]{:S(2)}, u32[]{:S(2)}) collective-permute-start(bf16[192,128]{1,0:T(8,128)(2,1)S(1)} %get-tuple-element.59), channel_id=1, source_target_pairs={{16,32},{32,16},{48,64},{64,48},{80,96},{96,80},{112,128},{128,112... | collective-permute-start | bytes 147464 | tf_op jit(solution)/shard_map/ppermute | solution.py:36
  39.5 12.8 %collective-permute-start.6 = (bf16[192,128]{1,0:T(8,128)(2,1)S(1)}, bf16[192,128]{1,0:T(8,128)(2,1)S(1)}, u32[]{:S(2)}, u32[]{:S(2)}) collective-permute-start(bf16[192,128]{1,0:T(8,128)(2,1)S(1)} %get-tuple-element.60), channel_id=1, source_target_pairs={{0,16},{16,0},{32,48},{48,32},{64,80},{80,64},{96,112},{112,96},{1... | collective-permute-start | bytes 147464 | tf_op jit(solution)/shard_map/ppermute | solution.py:37
  46.9 21.9 %all-to-all-start = ((bf16[16,8,3456]{2,1,0:T(8,128)(2,1)}), bf16[16,8,3456]{2,1,0:T(8,128)(2,1)S(1)}, u32[]{:S(2)}, u32[]{:S(2)}) async-start(bf16[16,8,3456]{2,1,0:T(8,128)(2,1)} %bitcast.24), calls=%async_computation | async-start | bytes 1769472 | tf_op jit(solution)/shard_map/all_to_all | solution.py:494
  53.0 10.2 %collective-permute-start.7 = (bf16[240,128]{1,0:T(8,128)(2,1)S(1)}, bf16[240,128]{1,0:T(8,128)(2,1)S(1)}, u32[]{:S(2)}, u32[]{:S(2)}) collective-permute-start(bf16[240,128]{1,0:T(8,128)(2,1)S(1)} %get-tuple-element.53), channel_id=1, source_target_pairs={{1,2},{2,1},{3,4},{4,3},{5,6},{6,5},{7,8},{8,7},{9,10},{10,9},{11,... | collective-permute-start | bytes 184328 | tf_op jit(solution)/shard_map/ppermute | solution.py:36
  59.8 7.3 %collective-permute-start.8 = (bf16[240,128]{1,0:T(8,128)(2,1)S(1)}, bf16[240,128]{1,0:T(8,128)(2,1)S(1)}, u32[]{:S(2)}, u32[]{:S(2)}) collective-permute-start(bf16[240,128]{1,0:T(8,128)(2,1)S(1)} %get-tuple-element.54), channel_id=1, source_target_pairs={{0,1},{1,0},{2,3},{3,2},{4,5},{5,4},{6,7},{7,6},{8,9},{9,8},{10,11... | collective-permute-start | bytes 184328 | tf_op jit(solution)/shard_map/ppermute | solution.py:37
  69.6 16.8 %all-to-all-start.1 = ((f32[8,27,128]{2,1,0:T(8,128)}), f32[8,27,128]{2,1,0:T(8,128)S(1)}, u32[]{:S(2)}, u32[]{:S(2)}) async-start(f32[8,27,128]{2,1,0:T(8,128)} %copy.54), calls=%async_computation.1 | async-start | bytes 262144 | tf_op jit(solution)/shard_map/all_to_all | solution.py:499
  75.3 1.2 %copy-start = (bf16[27,128,128]{2,1,0:T(8,128)(2,1)S(1)}, bf16[27,128,128]{2,1,0:T(8,128)(2,1)}, u32[]{:S(2)}) copy-start(bf16[27,128,128]{2,1,0:T(8,128)(2,1)} %w_first_in.1) | copy-start | bytes 2654212
